TPU v7x, 256 devices: a whole 4x4x8 slice. The times are simulated.
256 devices in a mesh: dp: 64 (over x, y, z_hi), tp: 4 (over z_lo, core).
Axes of the slice: x: 4, y: 4, z: 8 (z_hi: 4, z_lo: 2; z = z_hi * 2 + z_lo), core: 2. Of those that a mesh axis runs over, the one named last changes fastest.
Arguments:
- query_latent: bfloat16 [2, 128, 65536], P(None, 'dp', 'tp')
- query_rope: bfloat16 [2, 128, 8192], P(None, 'dp', 'tp'), may hold values from -6 to 6
- cache_latent: bfloat16 [128, 384, 512], P('dp')
- cache_rope: bfloat16 [128, 64, 384], P('dp'), may hold values from -6 to 6
- new_latent: bfloat16 [2, 128, 512], P(None, 'dp'), may hold values from -6 to 6
- new_rope: bfloat16 [2, 128, 64], P(None, 'dp'), may hold values from -6 to 6
- cache_lengths: int32 [128], P('dp'), may hold values from 2 to 384, as said below
- row_counts: int32 [64], replicated, may hold values from 1 to 2, as said below
- value_up: bfloat16 [128, 512, 128], P('tp'), may hold values from -0.25 to 0.25
- out_proj: bfloat16 [16384, 7168], P('tp', 'dp'), may hold values from -0.1875 to 0.1875
- norm_gain: float32 [7168], replicated, may hold values from 0.1 to 1.9
- expert_ids: int32 [2, 128, 4], replicated, may hold values from 0 to 15, all different within a row
- route_gates: float32 [2, 128, 4], replicated, may hold values from 0.1 to 1
- gate_proj: bfloat16 [7168, 32768], P(None, ('dp', 'tp')), may hold values from -0.0625 to 0.0625
- up_proj: bfloat16 [7168, 32768], P(None, ('dp', 'tp')), may hold values from -0.0625 to 0.0625
- down_proj: bfloat16 [32768, 7168], P(('dp', 'tp')), may hold values from -0.125 to 0.125
Outputs:
- hidden: bfloat16 [2, 128, 7168], P(None, None, 'dp')
- mixed: bfloat16 [2, 128, 7168], P(None, 'dp', 'tp')
Inputs may be any that keep to these rules, and one draw needn't show every extreme that they name: `row_counts`: every replica has at least one live slot; in every draw some replica has all 2 slots live. `cache_lengths`: in every draw some slot uses all 384 positions.
All inputs are finite; a program needn't handle non-finite values.
Results may differ from a plain program's by a relative error of at most 0.014.
Values may be sent and summed in bfloat16 or wider, within the bound.
No kernel may reach another device: no remote copies, remote signals or barrier semaphores. Data moves between devices by JAX's collectives and lax.ppermute only.
A program may use at most 128 MiB of HBM per device.

v0:
```python
import jax
import jax.numpy as jnp
from jax import lax
from jax.sharding import PartitionSpec as P

D = 7168
LAT = 512
ROPE = 64
HD = 128
FFN = 2048
STEPS = 2
SLOTS = 2
CACHE = 384


def attend_local(
    query_latent,
    query_rope,
    cache_latent,
    cache_rope,
    new_latent,
    new_rope,
    cache_lengths,
    live_slots,
    value_up,
):
    heads_here = value_up.shape[0]
    scale_factor = (HD + ROPE) ** (-0.5)
    key_mask = jnp.arange(CACHE)[None, None, :] < cache_lengths[:, None, None]
    outputs = []
    for which_step in range(STEPS):
        query_heads = query_latent[which_step].reshape(SLOTS, heads_here, LAT)
        rope_heads = query_rope[which_step].reshape(SLOTS, heads_here, ROPE)
        cache_scores = jnp.einsum(
            "bhl,bcl->bhc", query_heads, cache_latent, preferred_element_type=jnp.float32
        )
        cache_scores = (
            cache_scores
            + jnp.einsum("bhr,brc->bhc", rope_heads, cache_rope, preferred_element_type=jnp.float32)
        ) * scale_factor
        cache_scores = jnp.where(key_mask, cache_scores, -1e30)
        fresh_latent = new_latent[: which_step + 1]
        fresh_rope = new_rope[: which_step + 1]
        new_scores = jnp.einsum(
            "bhl,nbl->bhn", query_heads, fresh_latent, preferred_element_type=jnp.float32
        )
        new_scores = (
            new_scores
            + jnp.einsum("bhr,nbr->bhn", rope_heads, fresh_rope, preferred_element_type=jnp.float32)
        ) * scale_factor
        all_scores = jnp.concatenate([cache_scores, new_scores], axis=2)
        top_score = jnp.max(all_scores, axis=2, keepdims=True)
        expo = jnp.exp(all_scores - top_score)
        probs = (expo / jnp.sum(expo, axis=2, keepdims=True)).astype(jnp.bfloat16)
        latent_context = jnp.einsum(
            "bhc,bcl->bhl", probs[:, :, :CACHE], cache_latent, preferred_element_type=jnp.float32
        )
        latent_context = latent_context + jnp.einsum(
            "bhn,nbl->bhl", probs[:, :, CACHE:], fresh_latent, preferred_element_type=jnp.float32
        )
        latent_context = latent_context.astype(jnp.bfloat16)
        context_out = jnp.einsum(
            "bhl,hld->bhd", latent_context, value_up, preferred_element_type=jnp.float32
        ).astype(jnp.bfloat16)
        context_out = context_out.reshape(SLOTS, heads_here * HD)
        outputs.append(jnp.where(live_slots[:, None], context_out, jnp.zeros_like(context_out)))
    return jnp.stack(outputs)


def body(
    query_latent,
    query_rope,
    cache_latent,
    cache_rope,
    new_latent,
    new_rope,
    cache_lengths,
    row_counts,
    value_up,
    out_proj,
    norm_gain,
    expert_ids,
    route_gates,
    gate_proj,
    up_proj,
    down_proj,
):
    replicas = lax.axis_size("dp")
    replica_index = lax.axis_index("dp")
    own_count = lax.dynamic_slice_in_dim(row_counts, replica_index, 1, 0)
    live_slots = jnp.arange(SLOTS) < own_count
    all_contexts = attend_local(
        query_latent,
        query_rope,
        cache_latent,
        cache_rope,
        new_latent,
        new_rope,
        cache_lengths,
        live_slots,
        value_up,
    )
    token_count = replicas * SLOTS
    live_rows = jnp.arange(token_count) % SLOTS < jnp.repeat(
        row_counts, SLOTS, total_repeat_length=token_count
    )
    flat_index = replica_index * lax.axis_size("tp") + lax.axis_index("tp")
    expert_here = flat_index * gate_proj.shape[1] // FFN
    route_weight = jnp.sum(
        jnp.where(expert_ids == expert_here, route_gates, 0.0), axis=2
    ) * live_rows[None, :].astype(jnp.float32)

    def process(step_first, step_count):
        context_part = all_contexts[step_first : step_first + step_count]
        partial_out = jnp.einsum(
            "srk,kd->srd",
            lax.all_gather(context_part, "dp", axis=1, tiled=True),
            out_proj,
            preferred_element_type=jnp.float32,
        )
        summed_out = lax.psum(partial_out, "tp")
        hidden_part = summed_out.astype(jnp.bfloat16)
        token_major = jnp.transpose(hidden_part, (1, 0, 2))
        rows_full = lax.all_gather(token_major, "dp", axis=2, tiled=True)
        row_values = rows_full.astype(jnp.float32)
        normed = (
            row_values
            * lax.rsqrt(jnp.mean(row_values * row_values, axis=2, keepdims=True) + 1e-06)
            * norm_gain
        ).astype(jnp.bfloat16)
        flat_rows = normed.reshape(token_count * step_count, D)
        scale_rows = jnp.transpose(route_weight[step_first : step_first + step_count]).reshape(
            token_count * step_count, 1
        )
        gate_part = jnp.dot(flat_rows, gate_proj, preferred_element_type=jnp.float32)
        up_part = jnp.dot(flat_rows, up_proj, preferred_element_type=jnp.float32)
        inner = (jax.nn.silu(gate_part) * up_part * scale_rows).astype(jnp.bfloat16)
        wide_rows = lax.psum_scatter(
            jnp.dot(inner, down_proj, preferred_element_type=jnp.float32),
            "dp",
            scatter_dimension=0,
            tiled=True,
        )
        own_rows = lax.psum_scatter(wide_rows, "tp", scatter_dimension=1, tiled=True)
        mixed_part = jnp.transpose(
            own_rows.reshape(SLOTS, step_count, own_rows.shape[1]), (1, 0, 2)
        ).astype(jnp.bfloat16)
        return (hidden_part, mixed_part)

    results = [process(which_step, 1) for which_step in range(STEPS)]
    hidden = jnp.concatenate([pair[0] for pair in results], axis=0)
    mixed = jnp.concatenate([pair[1] for pair in results], axis=0)
    return (hidden, mixed)


def solution(mesh):
    return jax.shard_map(
        body,
        mesh=mesh,
        in_specs=(
            P(None, "dp", "tp"),
            P(None, "dp", "tp"),
            P("dp", None, None),
            P("dp", None, None),
            P(None, "dp", None),
            P(None, "dp", None),
            P("dp"),
            P(),
            P("tp", None, None),
            P("tp", "dp"),
            P(),
            P(),
            P(),
            P(None, ("dp", "tp")),
            P(None, ("dp", "tp")),
            P(("dp", "tp"), None),
        ),
        out_specs=(P(None, None, "dp"), P(None, "dp", "tp")),
        check_vma=False,
    )
```

profile of v0, /device:TPU:1, one launch (start us, length us, event | category | flops | bytes accessed | tf_op | source)
XLA Modules:
  0.0 1242.5 jit_solution(6642724311169827791)
XLA Ops:
  7.3 1.1 fusion.83
  8.4 0.7 fusion.84
  9.2 0.7 iota_compare_fusion
  9.9 0.7 slice_bitcast_fusion
  10.6 1.5 fusion.47
  12.2 0.7 slice_bitcast_fusion.3
  13.0 1.1 fusion.87
  14.2 0.2 fusion.40
  14.6 0.6 dynamic_slice.3
  15.2 0.6 iota_compare_fusion.1
  15.9 0.2 fusion.8
  16.1 2.9 fusion.23
  19.0 0.6 copy.52
  20.2 0.3 fusion.43
  20.5 0.2 fusion.85
  20.8 0.2 fusion.39
  21.2 0.2 fusion.9
  21.5 2.9 fusion.21
  24.4 0.7 copy.59
  25.2 75.5 %all-gather.7.cloned.1.call-done = bf16[1,128,4096]{2,0,1:T(2,128)(2,1)} async-done(((bf16[1,2,4096]{2,0,1:T(2,128)(2,1)}), bf16[1,128,4096]{2,0,1:T(2,128)(2,1)}) %all-gather.7.cloned.1.call-update) | async-done | bytes 1048592 | tf_op jit(solution)/shard_map/all_gather | solution.py:117
  100.7 2.9 convolution_bitcast_fusion.1
  103.6 77.5 %all-gather.9.cloned.1.call-done = bf16[1,128,4096]{2,0,1:T(2,128)(2,1)} async-done(((bf16[1,2,4096]{2,0,1:T(2,128)(2,1)}), bf16[1,128,4096]{2,0,1:T(2,128)(2,1)}) %all-gather.9.cloned.1.call-update) | async-done | bytes 1048592 | tf_op jit(solution)/shard_map/all_gather | solution.py:117
  181.1 2.9 convolution_bitcast_fusion
  184.1 13.2 %all-reduce.3 = (bf16[1,128,112]{1,2,0:T(8,128)(2,1)}, bf16[1,128,112]{1,2,0:T(8,128)(2,1)}) all-reduce(f32[1,128,112]{1,2,0:T(8,128)S(1)} %convolution_bitcast_fusion, f32[1,128,112]{1,2,0:T(8,128)S(1)} %convolution_bitcast_fusion.1), channel_id=1, replica_groups=mesh['dp'=64,'tp'=4] {'tp'}, use_global_device_ids=true, to_apply=%region_6.7 | all-reduce | flops 28672 | bytes 172032 | tf_op jit(solution)/shard_map/psum | solution.py:121
  197.4 0.5 all-gather.13.cloned.1.call-update
  197.9 0.2 all-reduce.6.cloned.1.call-start
  198.2 1.2 gather_fusion
  199.5 73.0 %all-gather.11.cloned.1.call-done = bf16[1,128,7168]{1,2,0:T(8,128)(2,1)} async-done(((bf16[1,128,112]{1,2,0:T(8,128)(2,1)}), bf16[1,128,7168]{1,2,0:T(8,128)(2,1)}) %all-gather.11.cloned.1.call-update) | async-done | bytes 1835024 | tf_op jit(solution)/shard_map/all_gather | solution.py:124
  272.6 2.5 fusion
  275.0 76.7 %all-gather.13.cloned.1.call-done = bf16[1,128,7168]{1,2,0:T(8,128)(2,1)} async-done(((bf16[1,128,112]{1,2,0:T(8,128)(2,1)}), bf16[1,128,7168]{1,2,0:T(8,128)(2,1)}) %all-gather.13.cloned.1.call-update) | async-done | bytes 1835024 | tf_op jit(solution)/shard_map/all_gather | solution.py:124
  351.8 2.5 fusion.3
  354.3 3.9 fusion.31
  358.2 1.8 fusion.35
  360.0 6.2 fusion.19
  366.2 6.2 fusion.18
  372.5 0.6 copy-done.15
  373.1 0.6 dynamic-slice.6
  374.3 728.4 %all-reduce.6.cloned.1.call-done = (f32[128,7168]{1,0:T(8,128)}, f32[128,7168]{1,0:T(8,128)}) async-done(((f32[128,7168]{1,0:T(8,128)}, f32[128,7168]{1,0:T(8,128)}), (f32[128,7168]{1,0:T(8,128)}, f32[128,7168]{1,0:T(8,128)})) %all-reduce.6.cloned.1.call-update) | async-done | bytes 7340048
  1102.7 1.1 constant_dynamic-slice_fusion
  1103.8 2.4 copy.67
  1106.3 2.4 copy.65
  1108.8 0.7 copy-done.5
  1109.5 0.6 pad_maximum_fusion
  1110.1 76.5 %reduce-scatter.9.cloned.1.call-done = f32[1792,2]{1,0:T(8,128)} async-done(((f32[7168,2]{1,0:T(8,128)}), f32[1792,2]{1,0:T(8,128)}) %reduce-scatter.9.cloned.1.call-update) | async-done | bytes 14352
  1186.7 1.5 copy.68
  1188.2 45.4 %reduce-scatter.7.cloned.1.call-done = f32[1792,2]{1,0:T(8,128)} async-done(((f32[7168,2]{1,0:T(8,128)}), f32[1792,2]{1,0:T(8,128)}) %reduce-scatter.7.cloned.1.call-update) | async-done | bytes 14352
  1233.5 1.5 copy.66
  1235.0 0.6 pad_maximum_fusion.1
  (63 shorter events, 1.8 us)
Async XLA Ops:
  7.2 352.8 %copy-start = (bf16[128,7168]{1,0:T(8,128)(2,1)S(1)}, bf16[128,7168]{1,0:T(8,128)(2,1)}, u32[]{:S(2)}) copy-start(bf16[128,7168]{1,0:T(8,128)(2,1)} %param.33) | copy-start | bytes 5505028
  7.2 8.7 copy-start.2
  7.2 7.4 copy-start.1
  7.2 93.5 %all-gather.7.cloned.1.call-start = ((), (), s32[]{:S(2)}) async-start(), calls=%async_computation.2 | async-start | bytes 2129920 | tf_op jit(solution)/shard_map/all_gather | solution.py:117
  16.1 3.7 copy-start.8
  16.1 3.8 copy-start.14
  16.1 4.4 copy-start.4
  19.7 161.4 %all-gather.9.cloned.1.call-start = ((), (), s32[]{:S(2)}) async-start(), calls=%async_computation.3 | async-start | bytes 2129920 | tf_op jit(solution)/shard_map/all_gather | solution.py:117
  21.5 79.2 %copy-start.13 = (bf16[4096,112]{0,1:T(8,128)(2,1)S(1)}, bf16[4096,112]{0,1:T(8,128)(2,1)}, u32[]{:S(2)}) copy-start(bf16[4096,112]{0,1:T(8,128)(2,1)} %param.27) | copy-start | bytes 2752516
  25.1 173.1 %copy-start.11 = (s32[128]{0:T(128)S(1)}, s32[128]{0:T(128)}, u32[]{:S(2)}) copy-start(s32[128]{0:T(128)} %constant.156) | copy-start | bytes 1540
  25.1 174.3 %copy-start.9 = (f32[2,128,4]{1,2,0:T(4,128)S(1)}, f32[2,128,4]{1,2,0:T(4,128)}, u32[]{:S(2)}) copy-start(f32[2,128,4]{1,2,0:T(4,128)} %param.30) | copy-start | bytes 12292
  25.1 174.3 %copy-start.10 = (s32[2,128,4]{1,2,0:T(4,128)S(1)}, s32[2,128,4]{1,2,0:T(4,128)}, u32[]{:S(2)}) copy-start(s32[2,128,4]{1,2,0:T(4,128)} %param.29) | copy-start | bytes 12292
  25.1 247.4 %all-gather.11.cloned.1.call-start = ((), (), s32[]{:S(2)}) async-start(), calls=%async_computation.4 | async-start | bytes 1863680 | tf_op jit(solution)/shard_map/all_gather | solution.py:124
  197.3 154.4 %all-gather.13.cloned.1.call-start = ((), (), s32[]{:S(2)}) async-start(), calls=%async_computation.5 | async-start | bytes 1863680 | tf_op jit(solution)/shard_map/all_gather | solution.py:124
  197.9 904.8 %all-reduce.6.cloned.1.call-start = ((), (), s32[]{:S(2)}) async-start(), calls=%async_computation.8 | async-start | bytes 14680064
  198.2 156.1 %copy-start.7 = (f32[7168]{0:T(1024)S(1)}, f32[7168]{0:T(1024)}, u32[]{:S(2)}) copy-start(f32[7168]{0:T(1024)} %param.28) | copy-start | bytes 86020
  354.2 3.9 copy-start.3
  354.2 3.9 copy-start.12
  372.4 0.7 copy-start.15
  372.4 814.3 %reduce-scatter.9.cloned.1.call-start = ((), (), s32[]{:S(2)}) async-start(), calls=%async_computation.7 | async-start | bytes 4587520
  1106.3 127.3 %reduce-scatter.7.cloned.1.call-start = ((), (), s32[]{:S(2)}) async-start(), calls=%async_computation.6 | async-start | bytes 4587520
  1108.8 0.7 copy-start.5
  1108.8 0.8 copy-start.6
Sparse Core Ops, SparseCore 0:
  19.8 80.8 all-gather.6
  104.6 76.5 all-gather.8
  197.5 75.0 all-gather.10
  276.3 75.4 all-gather.12
  372.5 730.1 all-reduce.5
  1106.4 80.2 reduce-scatter.8
  1189.4 44.0 reduce-scatter.6
where the time goes:
time: 1240 us
  waiting for transfers between devices  1150 us (93%)
  matrix products  34 us (3%)
  local copies, waits for them, and re-layouts  16.9 us (1%)
  between operations  15.1 us (1%)
  blocking collectives  13.2 us (1%)
    unnamed x10, waiting for transfers between devices  851 us
    all_gather x2, waiting for transfers between devices, process(): lax.all_gather(context_part, 'dp', axis=1, tiled=True)  153 us
    all_gather x2, waiting for transfers between devices, process(): rows_full = lax.all_gather(token_major, 'dp', axis=2, tiled=True)  150 us
  transfers between devices with their start and end apart: 7, of which 7 were waited for; matrix products, arithmetic and copies ran while one was open for 1% of the time, Pallas kernels for 0%

commit v1 on v0

v1 whole, which is shorter than its diff:
```python
import jax
import jax.numpy as jnp
from jax import lax
from jax.sharding import Mesh, PartitionSpec as P

D = 7168
LAT = 512
ROPE = 64
HD = 128
FFN = 2048
STEPS = 2
SLOTS = 2
CACHE = 384

DP = ("x", "y", "h")
TP = ("l", "c")
XY = ("x", "y")
Z = ("h", "l")
NXY = 16
NZ = 8
NH = 4
TOK = 256
SWAP = ((0, 1), (1, 0))

bf16 = jnp.bfloat16
f32 = jnp.float32


def spread(value, axes, count):
    copies = jnp.broadcast_to(value[None], (count,) + value.shape)
    return lax.all_to_all(copies, axes, 0, 0)


def attend(query_latent, query_rope, cache_latent, cache_rope, new_latent, new_rope, cache_lengths, live, value_up):
    heads = value_up.shape[0]
    scale = (HD + ROPE) ** (-0.5)
    rows = STEPS * heads
    q = jnp.transpose(query_latent.reshape(STEPS, SLOTS, heads, LAT), (1, 0, 2, 3)).reshape(SLOTS, rows, LAT)
    qr = jnp.transpose(query_rope.reshape(STEPS, SLOTS, heads, ROPE), (1, 0, 2, 3)).reshape(SLOTS, rows, ROPE)
    old = jnp.einsum("bhl,bcl->bhc", q, cache_latent, preferred_element_type=f32)
    old = (old + jnp.einsum("bhr,brc->bhc", qr, cache_rope, preferred_element_type=f32)) * scale
    mask = jnp.arange(CACHE)[None, None, :] < cache_lengths[:, None, None]
    old = jnp.where(mask, old, -1e30)
    new = jnp.einsum("bhl,nbl->bhn", q, new_latent, preferred_element_type=f32)
    new = (new + jnp.einsum("bhr,nbr->bhn", qr, new_rope, preferred_element_type=f32)) * scale
    step_of_row = jnp.arange(rows)[:, None] // heads
    new = jnp.where((jnp.arange(STEPS)[None, :] <= step_of_row)[None], new, -1e30)
    top = jnp.maximum(jnp.max(old, axis=2, keepdims=True), jnp.max(new, axis=2, keepdims=True))
    eo = jnp.exp(old - top)
    en = jnp.exp(new - top)
    total = jnp.sum(eo, axis=2, keepdims=True) + jnp.sum(en, axis=2, keepdims=True)
    po = (eo / total).astype(bf16)
    pn = (en / total).astype(bf16)
    lat = jnp.einsum("bhc,bcl->bhl", po, cache_latent, preferred_element_type=f32)
    lat = lat + jnp.einsum("bhn,nbl->bhl", pn, new_latent, preferred_element_type=f32)
    lat = lat.astype(bf16).reshape(SLOTS, STEPS, heads, LAT)
    ctx = jnp.einsum("bshl,hld->sbhd", lat, value_up, preferred_element_type=f32).astype(bf16)
    ctx = jnp.where(live[None, :, None, None], ctx, jnp.zeros_like(ctx))
    return ctx.reshape(STEPS * SLOTS, heads * HD)


def body(
    query_latent,
    query_rope,
    cache_latent,
    cache_rope,
    new_latent,
    new_rope,
    cache_lengths,
    row_counts,
    value_up,
    out_proj,
    norm_gain,
    expert_ids,
    route_gates,
    gate_proj,
    up_proj,
    down_proj,
):
    replica = lax.axis_index(DP)
    core = lax.axis_index("c")
    own_count = lax.dynamic_slice_in_dim(row_counts, replica, 1, 0)
    live = jnp.arange(SLOTS) < own_count

    down = down_proj.reshape(128, 2, 2, D // 4)
    down_keep = lax.dynamic_index_in_dim(down, core, 2, keepdims=False)
    down_send = lax.dynamic_index_in_dim(down, 1 - core, 2, keepdims=False)
    down_got = lax.ppermute(down_send, "c", SWAP)
    down_both = jnp.concatenate([down_keep, down_got], axis=0).reshape(256, D // 2)

    ctx = attend(
        query_latent, query_rope, cache_latent, cache_rope, new_latent, new_rope, cache_lengths, live, value_up
    )
    ctx = spread(ctx, "h", NH).reshape(NH * STEPS * SLOTS, -1)
    ctx = spread(ctx, XY, NXY).reshape(TOK, -1)

    part = jnp.dot(ctx, out_proj, preferred_element_type=f32).T
    keep = lax.dynamic_slice_in_dim(part, core * 128, 128, 1)
    send = lax.dynamic_slice_in_dim(part, (1 - core) * 128, 128, 1)
    chip = (keep + lax.ppermute(send, "c", SWAP)).astype(bf16)
    pieces = spread(chip, Z, NZ).reshape(NH, 2, D // 64, 128).astype(f32)
    hid = jnp.sum(pieces, axis=1)
    hid_b = hid.astype(bf16)

    own_hid = lax.dynamic_index_in_dim(hid_b, lax.axis_index("h"), 0, keepdims=False)
    other_hid = lax.ppermute(own_hid, "c", SWAP)
    first = jnp.where(core == 0, own_hid, other_hid)
    second = jnp.where(core == 0, other_hid, own_hid)
    hidden = jnp.concatenate([first, second], axis=1).T.reshape(64, STEPS, SLOTS, D // 64)
    hidden = jnp.transpose(hidden, (1, 0, 2, 3)).reshape(STEPS, 128, D // 64)

    hid_f = hid_b.astype(f32).reshape(D // 16, 128)
    column = lax.axis_index(XY)
    gain = lax.dynamic_slice_in_dim(norm_gain, column * (D // 16), D // 16, 0)
    scaled = (hid_f * gain[:, None]).astype(bf16)
    squares = jnp.sum(hid_f * hid_f, axis=0, keepdims=True)
    high = squares.astype(bf16)
    low = (squares - high.astype(f32)).astype(bf16)
    packed = jnp.concatenate([scaled, high, low, jnp.zeros((14, 128), bf16)], axis=0)
    rows_half = spread(packed, XY, NXY)
    rows_other = lax.ppermute(rows_half, "c", SWAP)

    expert = column
    fours = jnp.sum(jnp.where(expert_ids == expert, route_gates, 0.0), axis=2)
    live_rows = (jnp.arange(SLOTS)[None, :] < row_counts[:, None]).astype(f32)
    weight = fours.reshape(STEPS, 64, SLOTS) * live_rows[None]
    weight = jnp.transpose(weight, (1, 0, 2)).reshape(2, 128)

    def experts(rows, scale):
        total = jnp.sum(rows[:, 448:450, :].astype(f32), axis=(0, 1))
        inv = lax.rsqrt(total / D + 1e-06)
        wide = rows[:, :448, :].reshape(D, 128)
        gate = lax.dot_general(gate_proj, wide, (((0,), (0,)), ((), ())), preferred_element_type=f32) * inv
        up = lax.dot_general(up_proj, wide, (((0,), (0,)), ((), ())), preferred_element_type=f32) * inv
        return (jax.nn.silu(gate) * up * scale).astype(bf16)

    inner_a = experts(rows_half, lax.dynamic_index_in_dim(weight, core, 0, keepdims=False))
    inner_b = experts(rows_other, lax.dynamic_index_in_dim(weight, 1 - core, 0, keepdims=False))
    got_a = lax.ppermute(inner_a, "c", SWAP)
    got_b = lax.ppermute(inner_b, "c", SWAP)
    mine = jnp.concatenate([inner_a, got_b], axis=0)
    theirs = jnp.concatenate([inner_b, got_a], axis=0)
    first = jnp.where(core == 0, mine, theirs)
    second = jnp.where(core == 0, theirs, mine)
    inner = jnp.concatenate([first, second], axis=1)

    wide = lax.dot_general(inner, down_both, (((0,), (0,)), ((), ())), preferred_element_type=f32).astype(bf16)
    got = lax.all_to_all(wide.reshape(NXY, 16, D // 2), XY, 0, 0)
    column_sum = jnp.sum(got.astype(f32), axis=0).astype(bf16)
    column_sum = jnp.transpose(column_sum.reshape(NH, 4, 2, D // 4), (0, 2, 1, 3)).reshape(NZ, 4, D // 4)
    own = jnp.sum(lax.all_to_all(column_sum, Z, 0, 0).astype(f32), axis=0)
    mixed = own.astype(bf16).reshape(STEPS, SLOTS, D // 4)
    return hidden, mixed


def solution(mesh):
    fine = Mesh(mesh.devices.reshape(4, 4, 4, 2, 2), ("x", "y", "h", "l", "c"))
    return jax.shard_map(
        body,
        mesh=fine,
        in_specs=(
            P(None, DP, TP),
            P(None, DP, TP),
            P(DP, None, None),
            P(DP, None, None),
            P(None, DP, None),
            P(None, DP, None),
            P(DP),
            P(),
            P(TP, None, None),
            P(TP, DP),
            P(),
            P(),
            P(),
            P(None, DP + TP),
            P(None, DP + TP),
            P(DP + TP, None),
        ),
        out_specs=(P(None, None, DP), P(None, DP, TP)),
        check_vma=False,
    )
```

time: 1240 us -> 190 us (0.15)
  waiting for transfers between devices: 1150 us -> 92.6 us
  starting transfers between devices: 0.47 us -> 32 us
  matrix products: 34 us -> 15 us
  between operations: 15.1 us -> 1.12 us
    unnamed x10 -> x0, waiting for transfers between devices: 851 us -> none
    all_gather x4 -> x0, waiting for transfers between devices: 303 us -> none  [the longest x2 153 us: process(): lax.all_gather(context_part, 'dp', axis=1, tiled=True)]
    all_to_all x0 -> x5, waiting for transfers between devices: none -> 91.7 us  [the longest x3 59 us: spread(): return lax.all_to_all(copies, axes, 0, 0)]
    all_to_all x0 -> x5, starting transfers between devices: none -> 22.5 us  [the longest x3 14.8 us: spread(): return lax.all_to_all(copies, axes, 0, 0)]
    dot_general x19 -> x13, matrix products: 34 us -> 15 us  [the longest x1 3.44 us: body(): lax.dot_general(inner, down_both, (((0,), (0,)), ((), ())), preferred_ele...]
    all_to_all x0 -> x1, blocking collectives: none -> 16 us  [spread(): return lax.all_to_all(copies, axes, 0, 0)]
    psum x1 -> x0, blocking collectives: 13.2 us -> none  [process(): summed_out = lax.psum(partial_out, 'tp')]
  transfers between devices with their start and end apart: 7 -> 11, of which waited for: 7 -> 6; matrix products, arithmetic and copies ran while one was open for 1% -> 11% of each run, Pallas kernels for 0% -> 0%
where the time goes in v1:
time: 190 us; the launch traced here: 188 us
  waiting for transfers between devices  92.6 us (49%)
  starting transfers between devices  32 us (17%)
  local copies, waits for them, and re-layouts  26.1 us (14%)
  blocking collectives  16 us (8%)
  matrix products  15 us (8%)
  other arithmetic  5.4 us (3%)
    all_to_all x3, waiting for transfers between devices, spread(): return lax.all_to_all(copies, axes, 0, 0)  59 us
    all_to_all x1, waiting for transfers between devices, body(): got = lax.all_to_all(wide.reshape(NXY, 16, D // 2), XY, 0, 0)  25.9 us
    all_to_all x1, blocking collectives, spread(): return lax.all_to_all(copies, axes, 0, 0)  16 us
    all_to_all x3, starting transfers between devices, spread(): return lax.all_to_all(copies, axes, 0, 0)  14.8 us
    all_to_all x1, waiting for transfers between devices, body(): own = jnp.sum(lax.all_to_all(column_sum, Z, 0, 0).astype(f32), axis=0)  6.8 us
    ppermute x1, starting transfers between devices, body(): chip = (keep + lax.ppermute(send, 'c', SWAP)).astype(bf16)  5.92 us
    unnamed x25, local copies, waits for them, and re-layouts  5.44 us
    all_to_all x1, starting transfers between devices, body(): got = lax.all_to_all(wide.reshape(NXY, 16, D // 2), XY, 0, 0)  4.41 us
  transfers between devices with their start and end apart: 11, of which 6 were waited for; matrix products, arithmetic and copies ran while one was open for 11% of the time, Pallas kernels for 0%

profile of v1, /device:TPU:1, one launch (start us, length us, event | category | flops | bytes accessed | tf_op | source)
XLA Modules:
  0.0 188.2 jit_solution(710319853015323509)
XLA Ops:
  0.7 1.4 dynamic_slice.30
  2.1 0.6 iota_compare_fusion.3
  2.8 0.7 iota_compare_fusion.1
  3.5 0.8 reshape.219
  4.3 1.0 reshape.217
  5.3 0.9 fusion.41
  6.2 1.5 fusion.53
  8.9 3.0 %fusion.24 = bf16[2,2,32,128]{3,0,1,2:T(2,128)(2,1)S(1)} fusion(bf16[32,512,128]{2,1,0:T(8,128)(2,1)} %param.24, bf16[2,2,32,512]{3,2,1,0:T(8,128)(2,1)S(1)} %bitcast.121, pred[2]{0:T(512)(128)(4,1)S(1)} %iota_compare_fusion.3), kind=kOutput, calls=%fused_computation.27 | convolution fusion | flops 16809984 | bytes 4358146 | tf_op jit(solution)/shard_map/bshl,hld->sbhd/dot_general | solution.py:57
  12.0 16.0 %all_to_all.30 = bf16[4,4,4096]{2,1,0:T(4,128)(2,1)S(1)} all-to-all(bf16[4,4,4096]{2,1,0:T(4,128)(2,1)S(1)} %broadcast_in_dim.59), channel_id=1, replica_groups=mesh['x'=4,'y'=4,'h'=4,'l'=2,'c'=2] {'h'}, dimensions={0} | all-to-all | bytes 262144 | tf_op jit(solution)/shard_map/all_to_all | solution.py:31
  28.1 1.5 broadcast_in_dim.98
  29.6 6.9 %all-to-all-start.1 = ((bf16[16,16,4096]{2,1,0:T(8,128)(2,1)}), bf16[16,16,4096]{2,1,0:T(8,128)(2,1)}, u32[]{:S(2)}, u32[]{:S(2)}) async-start(bf16[16,16,4096]{2,1,0:T(8,128)(2,1)} %broadcast_in_dim.98), calls=%async_computation.1 | async-start | bytes 4194304 | tf_op jit(solution)/shard_map/all_to_all | solution.py:31
  36.6 25.2 %all-to-all-done.1 = bf16[16,16,4096]{2,1,0:T(8,128)(2,1)} async-done(((bf16[16,16,4096]{2,1,0:T(8,128)(2,1)}), bf16[16,16,4096]{2,1,0:T(8,128)(2,1)}, u32[]{:S(2)}, u32[]{:S(2)}) %all-to-all-start.1) | async-done | bytes 2097184 | tf_op jit(solution)/shard_map/all_to_all | solution.py:31
  61.8 2.4 %fusion.54 = f32[256,112]{0,1:T(8,128)S(1)} fusion(bf16[256,4096]{1,0:T(8,128)(2,1)} %bitcast.9, bf16[4096,112]{0,1:T(8,128)(2,1)S(1)} %copy-done.2), kind=kOutput, calls=%fused_computation.95 | convolution fusion | flops 234881024 | bytes 3129344 | tf_op jit(solution)/shard_map/dot_general | solution.py:97
  64.2 5.9 %collective-permute-start = (f32[112,128]{1,0:T(8,128)S(1)}, f32[112,128]{1,0:T(8,128)S(1)}, u32[]{:S(2)}, u32[]{:S(2)}) collective-permute-start(f32[112,128]{1,0:T(8,128)S(1)} %dynamic-slice_bitcast_fusion), channel_id=1, source_target_pairs={{0,1},{1,0},{2,3},{3,2},{4,5},{5,4},{6,7},{7,6},{8,9},{9,8},{10,11... | collective-permute-start | bytes 172040 | tf_op jit(solution)/shard_map/ppermute | solution.py:100
  70.1 0.9 collective-permute-done
  71.0 0.7 broadcast_in_dim.99
  71.7 3.4 %all-to-all-start.2 = ((bf16[8,112,128]{2,1,0:T(8,128)(2,1)}), bf16[8,112,128]{2,1,0:T(8,128)(2,1)S(1)}, u32[]{:S(2)}, u32[]{:S(2)}) async-start(bf16[8,112,128]{2,1,0:T(8,128)(2,1)} %broadcast_in_dim.99), calls=%async_computation.2 | async-start | bytes 458752 | tf_op jit(solution)/shard_map/all_to_all | solution.py:31
  75.2 0.8 dynamic_slice.34
  76.0 10.6 %all-to-all-done.2 = bf16[8,112,128]{2,1,0:T(8,128)(2,1)S(1)} async-done(((bf16[8,112,128]{2,1,0:T(8,128)(2,1)}), bf16[8,112,128]{2,1,0:T(8,128)(2,1)S(1)}, u32[]{:S(2)}, u32[]{:S(2)}) %all-to-all-start.2) | async-done | bytes 229408 | tf_op jit(solution)/shard_map/all_to_all | solution.py:31
  87.0 1.5 broadcast_in_dim.101
  88.5 4.4 %all-to-all-start.3 = ((bf16[16,464,128]{2,1,0:T(8,128)(2,1)}), bf16[16,464,128]{2,1,0:T(8,128)(2,1)}, u32[]{:S(2)}, u32[]{:S(2)}) async-start(bf16[16,464,128]{2,1,0:T(8,128)(2,1)} %broadcast_in_dim.101), calls=%async_computation.3 | async-start | bytes 3801088 | tf_op jit(solution)/shard_map/all_to_all | solution.py:31
  92.9 3.9 %copy.112 = bf16[128,7168]{0,1:T(8,128)(2,1)} copy(bf16[128,7168]{1,0:T(8,128)(2,1)} %param.31) | data formatting | bytes 3670016 | tf_op args[15]
  96.8 23.1 %all-to-all-done.3 = bf16[16,464,128]{2,1,0:T(8,128)(2,1)} async-done(((bf16[16,464,128]{2,1,0:T(8,128)(2,1)}), bf16[16,464,128]{2,1,0:T(8,128)(2,1)}, u32[]{:S(2)}, u32[]{:S(2)}) %all-to-all-start.3) | async-done | bytes 1900576 | tf_op jit(solution)/shard_map/all_to_all | solution.py:31
  120.0 3.4 %copy.108 = bf16[16,464,128]{2,0,1:T(8,128)(2,1)} copy(bf16[16,464,128]{2,1,0:T(8,128)(2,1)} %all-to-all-done.3) | data formatting | bytes 3801088 | tf_op jit(solution)/shard_map/all_to_all | solution.py:31
  123.3 2.1 %collective-permute-start.2 = (bf16[16,464,128]{2,0,1:T(8,128)(2,1)}, bf16[16,464,128]{2,0,1:T(8,128)(2,1)}, u32[]{:S(2)}, u32[]{:S(2)}) collective-permute-start(bf16[16,464,128]{2,0,1:T(8,128)(2,1)} %copy.108), channel_id=1, source_target_pairs={{0,1},{1,0},{2,3},{3,2},{4,5},{5,4},{6,7},{7,6},{8,9},{9,8},{10,11... | collective-permute-start | bytes 5701640 | tf_op jit(solution)/shard_map/ppermute | solution.py:121
  125.5 1.1 constant_dynamic-slice_fusion.1
  126.5 1.3 copy.113
  128.3 1.6 slice.16
  129.9 0.7 convert_reduce_fusion.1
  130.7 0.7 fusion.15
  131.4 0.8 copy-done.9
  132.2 0.7 fusion.16
  132.9 0.6 collective-permute-start.4
  133.5 0.7 convert_reduce_fusion
  134.2 1.8 slice.18
  136.5 0.7 fusion.11
  137.2 0.7 fusion.17
  138.3 1.3 copy.114
  139.6 3.4 %convolution_convert_fusion = bf16[256,3584]{1,0:T(8,128)(2,1)} fusion(bf16[128,3584]{0,1:T(8,128)(2,1)} %bitcast.113, bf16[128,3584]{0,1:T(8,128)(2,1)} %bitcast.114, bf16[256,128]{1,0:T(8,128)(2,1)S(1)} %get-tuple-element.17, bf16[256,128]{1,0:T(8,128)(2,1)S(1)} %get-tuple-element.16), kind=kOutput, calls=%fused_computation | convolution fusion | flops 474611712 | bytes 3801088 | tf_op jit(solution)/shard_map/dot_general | solution.py:147
  143.0 4.4 %all-to-all-start.4 = ((bf16[16,16,3584]{2,1,0:T(8,128)(2,1)}), bf16[16,16,3584]{2,1,0:T(8,128)(2,1)}, u32[]{:S(2)}, u32[]{:S(2)}) async-start(bf16[16,16,3584]{2,1,0:T(8,128)(2,1)} %bitcast.111), calls=%async_computation.4 | async-start | bytes 3670016 | tf_op jit(solution)/shard_map/all_to_all | solution.py:148
  147.5 0.6 collective-permute-start.1
  148.0 25.9 %all-to-all-done.4 = bf16[16,16,3584]{2,1,0:T(8,128)(2,1)} async-done(((bf16[16,16,3584]{2,1,0:T(8,128)(2,1)}), bf16[16,16,3584]{2,1,0:T(8,128)(2,1)}, u32[]{:S(2)}, u32[]{:S(2)}) %all-to-all-start.4) | async-done | bytes 1835040 | tf_op jit(solution)/shard_map/all_to_all | solution.py:148
  173.9 1.7 reduce_sum.100
  175.7 0.7 copy.115
  176.4 3.4 %all-to-all-start.5 = ((bf16[8,4,1792]{2,1,0:T(4,128)(2,1)}), bf16[8,4,1792]{2,1,0:T(4,128)(2,1)S(1)}, u32[]{:S(2)}, u32[]{:S(2)}) async-start(bf16[8,4,1792]{2,1,0:T(4,128)(2,1)} %bitcast.35), calls=%async_computation.5 | async-start | bytes 229376 | tf_op jit(solution)/shard_map/all_to_all | solution.py:151
  180.0 0.7 copy.116
  180.7 6.8 %all-to-all-done.5 = bf16[8,4,1792]{2,1,0:T(4,128)(2,1)S(1)} async-done(((bf16[8,4,1792]{2,1,0:T(4,128)(2,1)}), bf16[8,4,1792]{2,1,0:T(4,128)(2,1)S(1)}, u32[]{:S(2)}, u32[]{:S(2)}) %all-to-all-start.5) | async-done | bytes 114720 | tf_op jit(solution)/shard_map/all_to_all | solution.py:151
  187.6 0.6 reshape.234
  (72 shorter events, 3.4 us)
Async XLA Ops:
  0.6 130.0 %copy-start = (bf16[7168,128]{1,0:T(8,128)(2,1)S(1)}, bf16[7168,128]{1,0:T(8,128)(2,1)}, u32[]{:S(2)}) copy-start(bf16[7168,128]{1,0:T(8,128)(2,1)} %param.29) | copy-start | bytes 5505028
  0.6 7.7 %copy-start.3 = (bf16[2,384,512]{2,1,0:T(8,128)(2,1)S(1)}, bf16[2,384,512]{2,1,0:T(8,128)(2,1)}, u32[]{:S(2)}) copy-start(bf16[2,384,512]{2,1,0:T(8,128)(2,1)} %param.18) | copy-start | bytes 2359300
  0.7 7.0 %copy-start.10 = (bf16[2,2,64]{2,1,0:T(2,128)(2,1)S(1)}, bf16[2,2,64]{2,1,0:T(2,128)(2,1)}, u32[]{:S(2)}) copy-start(bf16[2,2,64]{2,1,0:T(2,128)(2,1)} %param.21) | copy-start | bytes 1540
  0.7 7.2 %copy-start.4 = (bf16[2,64,384]{2,1,0:T(8,128)(2,1)S(1)}, bf16[2,64,384]{2,1,0:T(8,128)(2,1)}, u32[]{:S(2)}) copy-start(bf16[2,64,384]{2,1,0:T(8,128)(2,1)} %param.19) | copy-start | bytes 294916
  5.3 3.4 %copy-start.5 = (bf16[2,2,512]{2,1,0:T(2,128)(2,1)S(1)}, bf16[2,2,512]{2,1,0:T(2,128)(2,1)}, u32[]{:S(2)}) copy-start(bf16[2,2,512]{2,1,0:T(2,128)(2,1)} %param.20) | copy-start | bytes 12292
  29.6 32.2 %copy-start.2 = (bf16[4096,112]{0,1:T(8,128)(2,1)S(1)}, bf16[4096,112]{0,1:T(8,128)(2,1)}, u32[]{:S(2)}) copy-start(bf16[4096,112]{0,1:T(8,128)(2,1)} %param.25) | copy-start | bytes 2752516
  29.6 32.2 %all-to-all-start.1 = ((bf16[16,16,4096]{2,1,0:T(8,128)(2,1)}), bf16[16,16,4096]{2,1,0:T(8,128)(2,1)}, u32[]{:S(2)}, u32[]{:S(2)}) async-start(bf16[16,16,4096]{2,1,0:T(8,128)(2,1)} %broadcast_in_dim.98), calls=%async_computation.1 | async-start | bytes 4194304 | tf_op jit(solution)/shard_map/all_to_all | solution.py:31
  64.2 6.8 %collective-permute-start = (f32[112,128]{1,0:T(8,128)S(1)}, f32[112,128]{1,0:T(8,128)S(1)}, u32[]{:S(2)}, u32[]{:S(2)}) collective-permute-start(f32[112,128]{1,0:T(8,128)S(1)} %dynamic-slice_bitcast_fusion), channel_id=1, source_target_pairs={{0,1},{1,0},{2,3},{3,2},{4,5},{5,4},{6,7},{7,6},{8,9},{9,8},{10,11... | collective-permute-start | bytes 172040 | tf_op jit(solution)/shard_map/ppermute | solution.py:100
  71.7 14.9 %all-to-all-start.2 = ((bf16[8,112,128]{2,1,0:T(8,128)(2,1)}), bf16[8,112,128]{2,1,0:T(8,128)(2,1)S(1)}, u32[]{:S(2)}, u32[]{:S(2)}) async-start(bf16[8,112,128]{2,1,0:T(8,128)(2,1)} %broadcast_in_dim.99), calls=%async_computation.2 | async-start | bytes 458752 | tf_op jit(solution)/shard_map/all_to_all | solution.py:31
  88.5 31.4 %all-to-all-start.3 = ((bf16[16,464,128]{2,1,0:T(8,128)(2,1)}), bf16[16,464,128]{2,1,0:T(8,128)(2,1)}, u32[]{:S(2)}, u32[]{:S(2)}) async-start(bf16[16,464,128]{2,1,0:T(8,128)(2,1)} %broadcast_in_dim.101), calls=%async_computation.3 | async-start | bytes 3801088 | tf_op jit(solution)/shard_map/all_to_all | solution.py:31
  120.0 5.5 %copy-start.1 = (bf16[128,7168]{0,1:T(8,128)(2,1)S(1)}, bf16[128,7168]{0,1:T(8,128)(2,1)}, u32[]{:S(2)}) copy-start(bf16[128,7168]{0,1:T(8,128)(2,1)} %copy.112) | copy-start | bytes 5505028
  123.3 10.1 %collective-permute-start.2 = (bf16[16,464,128]{2,0,1:T(8,128)(2,1)}, bf16[16,464,128]{2,0,1:T(8,128)(2,1)}, u32[]{:S(2)}, u32[]{:S(2)}) collective-permute-start(bf16[16,464,128]{2,0,1:T(8,128)(2,1)} %copy.108), channel_id=1, source_target_pairs={{0,1},{1,0},{2,3},{3,2},{4,5},{5,4},{6,7},{7,6},{8,9},{9,8},{10,11... | collective-permute-start | bytes 5701640 | tf_op jit(solution)/shard_map/ppermute | solution.py:121
  126.5 1.3 copy-start.6
  126.5 1.3 copy-start.7
  126.5 1.4 copy-start.8
  127.8 10.5 %collective-permute-start.5 = (bf16[128,2,1792]{2,0,1:T(8,128)(2,1)}, bf16[128,2,1792]{2,0,1:T(8,128)(2,1)S(1)}, u32[]{:S(2)}, u32[]{:S(2)}) collective-permute-start(bf16[128,2,1792]{2,0,1:T(8,128)(2,1)} %bitcast.112), channel_id=1, source_target_pairs={{0,1},{1,0},{2,3},{3,2},{4,5},{5,4},{6,7},{7,6},{8,9},{9,8},{10,11... | collective-permute-start | bytes 2752520 | tf_op jit(solution)/shard_map/ppermute | solution.py:88
  130.7 1.5 copy-start.9
  132.9 6.7 %collective-permute-start.4 = (bf16[128,128]{1,0:T(8,128)(2,1)S(1)}, bf16[128,128]{1,0:T(8,128)(2,1)S(1)}, u32[]{:S(2)}, u32[]{:S(2)}) collective-permute-start(bf16[128,128]{1,0:T(8,128)(2,1)S(1)} %fusion.16), channel_id=1, source_target_pairs={{0,1},{1,0},{2,3},{3,2},{4,5},{5,4},{6,7},{7,6},{8,9},{9,8},{10,11... | collective-permute-start | bytes 98312 | tf_op jit(solution)/shard_map/ppermute | solution.py:139
  138.0 1.6 collective-permute-start.3
  143.0 30.9 %all-to-all-start.4 = ((bf16[16,16,3584]{2,1,0:T(8,128)(2,1)}), bf16[16,16,3584]{2,1,0:T(8,128)(2,1)}, u32[]{:S(2)}, u32[]{:S(2)}) async-start(bf16[16,16,3584]{2,1,0:T(8,128)(2,1)} %bitcast.111), calls=%async_computation.4 | async-start | bytes 3670016 | tf_op jit(solution)/shard_map/all_to_all | solution.py:148
  147.5 32.3 %collective-permute-start.1 = (bf16[112,128]{1,0:T(8,128)(2,1)S(1)}, bf16[112,128]{1,0:T(8,128)(2,1)S(1)}, u32[]{:S(2)}, u32[]{:S(2)}) collective-permute-start(bf16[112,128]{1,0:T(8,128)(2,1)S(1)} %dynamic-slice_bitcast_fusion.1), channel_id=1, source_target_pairs={{0,1},{1,0},{2,3},{3,2},{4,5},{5,4},{6,7},{7,6},{8,9},{9,8},{10,11... | collective-permute-start | bytes 86024 | tf_op jit(solution)/shard_map/ppermute | solution.py:106
  176.4 11.1 %all-to-all-start.5 = ((bf16[8,4,1792]{2,1,0:T(4,128)(2,1)}), bf16[8,4,1792]{2,1,0:T(4,128)(2,1)S(1)}, u32[]{:S(2)}, u32[]{:S(2)}) async-start(bf16[8,4,1792]{2,1,0:T(4,128)(2,1)} %bitcast.35), calls=%async_computation.5 | async-start | bytes 229376 | tf_op jit(solution)/shard_map/all_to_all | solution.py:151

commit v2 on v1

v2 whole, which is shorter than its diff:
```python
import jax
import jax.numpy as jnp
from jax import lax
from jax.sharding import Mesh, PartitionSpec as P

D = 7168
LAT = 512
ROPE = 64
HD = 128
FFN = 2048
STEPS = 2
SLOTS = 2
CACHE = 384

DP = ("x", "y", "h")
TP = ("l", "c")
XY = ("x", "y")
Z = ("h", "l")
NXY = 16
NZ = 8
NH = 4
TOK = 256
SWAP = ((0, 1), (1, 0))

bf16 = jnp.bfloat16
f32 = jnp.float32


def spread(value, axes, count):
    copies = jnp.broadcast_to(value[None], (count,) + value.shape)
    return lax.all_to_all(copies, axes, 0, 0)


def attend(query_latent, query_rope, cache_latent, cache_rope, new_latent, new_rope, cache_lengths, live, value_up):
    heads = value_up.shape[0]
    scale = (HD + ROPE) ** (-0.5)
    rows = STEPS * heads
    q = jnp.transpose(query_latent.reshape(STEPS, SLOTS, heads, LAT), (1, 0, 2, 3)).reshape(SLOTS, rows, LAT)
    qr = jnp.transpose(query_rope.reshape(STEPS, SLOTS, heads, ROPE), (1, 0, 2, 3)).reshape(SLOTS, rows, ROPE)
    old = jnp.einsum("bhl,bcl->bhc", q, cache_latent, preferred_element_type=f32)
    old = (old + jnp.einsum("bhr,brc->bhc", qr, cache_rope, preferred_element_type=f32)) * scale
    mask = jnp.arange(CACHE)[None, None, :] < cache_lengths[:, None, None]
    old = jnp.where(mask, old, -1e30)
    new = jnp.einsum("bhl,nbl->bhn", q, new_latent, preferred_element_type=f32)
    new = (new + jnp.einsum("bhr,nbr->bhn", qr, new_rope, preferred_element_type=f32)) * scale
    step_of_row = jnp.arange(rows)[:, None] // heads
    new = jnp.where((jnp.arange(STEPS)[None, :] <= step_of_row)[None], new, -1e30)
    top = jnp.maximum(jnp.max(old, axis=2, keepdims=True), jnp.max(new, axis=2, keepdims=True))
    eo = jnp.exp(old - top)
    en = jnp.exp(new - top)
    total = jnp.sum(eo, axis=2, keepdims=True) + jnp.sum(en, axis=2, keepdims=True)
    po = (eo / total).astype(bf16)
    pn = (en / total).astype(bf16)
    lat = jnp.einsum("bhc,bcl->bhl", po, cache_latent, preferred_element_type=f32)
    lat = lat + jnp.einsum("bhn,nbl->bhl", pn, new_latent, preferred_element_type=f32)
    lat = lat.astype(bf16).reshape(SLOTS, STEPS, heads, LAT)
    ctx = jnp.einsum("bshl,hld->sbhd", lat, value_up, preferred_element_type=f32).astype(bf16)
    ctx = jnp.where(live[None, :, None, None], ctx, jnp.zeros_like(ctx))
    return ctx.reshape(STEPS * SLOTS, heads * HD)


def body(
    query_latent,
    query_rope,
    cache_latent,
    cache_rope,
    new_latent,
    new_rope,
    cache_lengths,
    row_counts,
    value_up,
    out_proj,
    norm_gain,
    expert_ids,
    route_gates,
    gate_proj,
    up_proj,
    down_proj,
):
    replica = lax.axis_index(DP)
    core = lax.axis_index("c")
    column = lax.axis_index(XY)
    own_count = lax.dynamic_slice_in_dim(row_counts, replica, 1, 0)
    live = jnp.arange(SLOTS) < own_count

    gate_other = lax.ppermute(gate_proj, "c", SWAP)
    up_other = lax.ppermute(up_proj, "c", SWAP)
    down_other = lax.ppermute(down_proj, "c", SWAP)

    ctx = attend(
        query_latent, query_rope, cache_latent, cache_rope, new_latent, new_rope, cache_lengths, live, value_up
    )
    gain = lax.dynamic_slice_in_dim(norm_gain, column * (D // 16), D // 16, 0)
    gain = jnp.broadcast_to(gain[:, None], (D // 16, 128))
    fours = jnp.sum(jnp.where(expert_ids == column, route_gates, 0.0), axis=2)
    live_rows = (jnp.arange(SLOTS)[None, :] < row_counts[:, None]).astype(f32).reshape(128)
    weight = lax.dynamic_index_in_dim(fours, core, 0, keepdims=False) * live_rows
    ctx, gain, weight = lax.optimization_barrier((ctx, gain, weight))

    ctx = spread(ctx, "h", NH).reshape(NH, STEPS, SLOTS, -1)
    ctx = jnp.transpose(ctx, (1, 0, 2, 3)).reshape(16, -1)
    ctx = spread(ctx, XY, NXY).reshape(TOK, -1)

    part = jnp.dot(ctx, out_proj, preferred_element_type=f32).reshape(NXY, STEPS, 8, D // 64)
    keep = lax.dynamic_index_in_dim(part, core, 1, keepdims=False).reshape(128, D // 64).T
    send = lax.dynamic_index_in_dim(part, 1 - core, 1, keepdims=False).reshape(128, D // 64).T
    chip = (keep + lax.ppermute(send, "c", SWAP)).astype(bf16)
    pieces = spread(chip, Z, NZ).reshape(NH, 2, D // 64, 128).astype(f32)
    hid = jnp.sum(pieces, axis=1).astype(bf16)
    own_hid = lax.dynamic_index_in_dim(hid, lax.axis_index("h"), 0, keepdims=False)

    hid_f = hid.astype(f32).reshape(D // 16, 128)
    scaled = (hid_f * gain).astype(bf16)
    squares = jnp.sum(hid_f * hid_f, axis=0, keepdims=True)
    high = squares.astype(bf16)
    low = (squares - high.astype(f32)).astype(bf16)
    packed = jnp.concatenate([scaled, high, low, jnp.zeros((14, 128), bf16)], axis=0)
    packed, own_hid = lax.optimization_barrier((packed, own_hid))
    rows = spread(packed, XY, NXY)

    rows, own_hid = lax.optimization_barrier((rows, own_hid))
    total = jnp.sum(rows[:, 448:450, :].astype(f32), axis=(0, 1))
    inv = lax.rsqrt(total / D + 1e-06)
    wide = rows[:, :448, :].reshape(D, 128)

    def product(weights):
        return lax.dot_general(weights, wide, (((0,), (0,)), ((), ())), preferred_element_type=f32) * inv

    inner = [
        (jax.nn.silu(product(gate)) * product(up) * weight).astype(bf16)
        for gate, up in ((gate_proj, up_proj), (gate_other, up_other))
    ]
    inner = jnp.concatenate(inner, axis=0)
    down = jnp.concatenate([down_proj, down_other], axis=0)
    out = lax.dot_general(inner, down, (((0,), (0,)), ((), ())), preferred_element_type=f32).astype(bf16)

    other_hid = lax.ppermute(own_hid, "c", SWAP)
    steps = jnp.where(core == 0, jnp.stack([own_hid, other_hid]), jnp.stack([other_hid, own_hid]))
    hidden = jnp.transpose(steps, (0, 2, 1))

    out, hidden = lax.optimization_barrier((out, hidden))
    got = lax.all_to_all(out.reshape(NXY, 8, D), XY, 0, 0)
    got, hidden = lax.optimization_barrier((got, hidden))
    sums = jnp.sum(got.astype(f32), axis=0).astype(bf16)
    sums = jnp.transpose(sums.reshape(NH, SLOTS, 4, D // 4), (0, 2, 1, 3)).reshape(16, SLOTS, D // 4)
    own = lax.all_to_all(sums, ("h", "l", "c"), 0, 0)
    mixed = jnp.sum(own.astype(f32).reshape(NZ, STEPS, SLOTS, D // 4), axis=0).astype(bf16)
    return hidden, mixed


def solution(mesh):
    fine = Mesh(mesh.devices.reshape(4, 4, 4, 2, 2), ("x", "y", "h", "l", "c"))
    return jax.shard_map(
        body,
        mesh=fine,
        in_specs=(
            P(None, DP, TP),
            P(None, DP, TP),
            P(DP, None, None),
            P(DP, None, None),
            P(None, DP, None),
            P(None, DP, None),
            P(DP),
            P(),
            P(TP, None, None),
            P(TP, DP),
            P(),
            P(),
            P(),
            P(None, DP + TP),
            P(None, DP + TP),
            P(DP + TP, None),
        ),
        out_specs=(P(None, None, DP), P(None, DP, TP)),
        check_vma=False,
    )
```

time: 190 us -> 173 us (0.911)
  blocking collectives: 16 us -> 56.7 us
  waiting for transfers between devices: 92.6 us -> 62 us
  local copies, waits for them, and re-layouts: 26.1 us -> 8.84 us
  starting transfers between devices: 32 us -> 24.8 us
    all_to_all x0 -> x2, blocking collectives: none -> 40.7 us  [the longest x1 26.5 us: body(): got = lax.all_to_all(out.reshape(NXY, 8, D), XY, 0, 0)]
    all_to_all x2 -> x0, waiting for transfers between devices: 32.7 us -> none  [the longest x1 25.9 us: body(): got = lax.all_to_all(wide.reshape(NXY, 16, D // 2), XY, 0, 0)]
    all_to_all x2 -> x0, starting transfers between devices: 7.77 us -> none  [the longest x1 4.41 us: body(): got = lax.all_to_all(wide.reshape(NXY, 16, D // 2), XY, 0, 0)]
    unnamed x25 -> x23, local copies, waits for them, and re-layouts: 5.44 us -> 0.09 us
    slice x3 -> x1, local copies, waits for them, and re-layouts: 3.92 us -> 0.17 us  [body(): wide = rows[:, :448, :].reshape(D, 128)]
    all_to_all x1, local copies, waits for them, and re-layouts: 3.38 us -> 0.1 us  [spread(): return lax.all_to_all(copies, axes, 0, 0)]
    ppermute x1, starting transfers between devices: 0.56 us -> 3.18 us  [body(): other_hid = lax.ppermute(own_hid, 'c', SWAP)]
    dynamic_slice x3 -> x0, local copies, waits for them, and re-layouts: 2.33 us -> none  [the longest x1 1.27 us: body(): down_send = lax.dynamic_index_in_dim(down, 1 - core, 2, keepdims=False)]
  transfers between devices with their start and end apart: 11 -> 8, of which waited for: 6 -> 4; matrix products, arithmetic and copies ran while one was open for 11% -> 5% of each run, Pallas kernels for 0% -> 0%
where the time goes in v2:
time: 173 us; the launch traced here: 172 us
  waiting for transfers between devices  62 us (36%)
  blocking collectives  56.7 us (33%)
  starting transfers between devices  24.8 us (14%)
  matrix products  15.2 us (9%)
  local copies, waits for them, and re-layouts  8.84 us (5%)
  other arithmetic  3.62 us (2%)
    all_to_all x3, waiting for transfers between devices, spread(): return lax.all_to_all(copies, axes, 0, 0)  61 us
    all_to_all x1, blocking collectives, body(): got = lax.all_to_all(out.reshape(NXY, 8, D), XY, 0, 0)  26.5 us
    all_to_all x1, blocking collectives, spread(): return lax.all_to_all(copies, axes, 0, 0)  16 us
    all_to_all x3, starting transfers between devices, spread(): return lax.all_to_all(copies, axes, 0, 0)  14.3 us
    all_to_all x1, blocking collectives, body(): own = lax.all_to_all(sums, ('h', 'l', 'c'), 0, 0)  14.2 us
    dot_general x4, matrix products, product(): lax.dot_general(weights, wide, (((0,), (0,)), ((), ())), preferred_elemen...  6.1 us
    ppermute x1, starting transfers between devices, body(): chip = (keep + lax.ppermute(send, 'c', SWAP)).astype(bf16)  5.92 us
    broadcast_in_dim x5, local copies, waits for them, and re-layouts, spread(): copies = jnp.broadcast_to(value[None], (count,) + value.shape)  3.92 us
  transfers between devices with their start and end apart: 8, of which 4 were waited for; matrix products, arithmetic and copies ran while one was open for 5% of the time, Pallas kernels for 0%

profile of v2, /device:TPU:1, one launch (start us, length us, event | category | flops | bytes accessed | tf_op | source)
XLA Modules:
  0.0 172.3 jit_solution(4691088499512029735)
XLA Ops:
  0.7 1.1 reshape.195
  1.8 0.8 reshape.197
  2.7 0.7 iota_compare_fusion.1
  3.4 1.5 fusion.53
  4.9 0.8 fusion.41
  5.7 0.2 fusion.51
  6.0 0.1 fusion.52
  6.1 0.2 fusion.30
  6.4 0.3 fusion.32
  6.7 0.2 fusion.9
  7.0 0.6 dynamic_slice.21
  7.6 0.6 iota_compare_fusion.3
  8.3 3.0 %fusion.23 = bf16[2,2,32,128]{3,0,1,2:T(2,128)(2,1)S(1)} fusion(bf16[32,512,128]{2,1,0:T(8,128)(2,1)} %param.24, bf16[2,2,32,512]{3,2,1,0:T(8,128)(2,1)S(1)} %bitcast.116, pred[2]{0:T(512)(128)(4,1)S(1)} %iota_compare_fusion.3), kind=kOutput, calls=%fused_computation.26 | convolution fusion | flops 16809984 | bytes 4358146 | tf_op jit(solution)/shard_map/bshl,hld->sbhd/dot_general | solution.py:57
  11.3 0.1 lt.76
  11.5 0.8 dynamic_slice.22
  12.3 0.1 broadcast_in_dim.58
  12.5 16.0 %all_to_all.30 = bf16[4,4,4096]{2,1,0:T(4,128)(2,1)S(1)} all-to-all(bf16[4,4,4096]{2,1,0:T(4,128)(2,1)S(1)} %broadcast_in_dim.60), channel_id=1, replica_groups=mesh['x'=4,'y'=4,'h'=4,'l'=2,'c'=2] {'h'}, dimensions={0} | all-to-all | bytes 262144 | tf_op jit(solution)/shard_map/all_to_all | solution.py:31
  28.5 0.1 copy.96
  28.6 0.1 copy.97
  28.8 1.6 broadcast_in_dim.62
  30.4 6.8 %all-to-all-start.1 = ((bf16[16,16,4096]{2,1,0:T(8,128)(2,1)}), bf16[16,16,4096]{2,1,0:T(8,128)(2,1)S(1)}, u32[]{:S(2)}, u32[]{:S(2)}) async-start(bf16[16,16,4096]{2,1,0:T(8,128)(2,1)} %broadcast_in_dim.62), calls=%async_computation.1 | async-start | bytes 4194304 | tf_op jit(solution)/shard_map/all_to_all | solution.py:31
  37.2 25.2 %all-to-all-done.1 = bf16[16,16,4096]{2,1,0:T(8,128)(2,1)S(1)} async-done(((bf16[16,16,4096]{2,1,0:T(8,128)(2,1)}), bf16[16,16,4096]{2,1,0:T(8,128)(2,1)S(1)}, u32[]{:S(2)}, u32[]{:S(2)}) %all-to-all-start.1) | async-done | bytes 2097184 | tf_op jit(solution)/shard_map/all_to_all | solution.py:31
  62.4 0.8 fusion.5
  63.1 5.9 %collective-permute-start = (f32[112,128]{0,1:T(8,128)S(1)}, f32[112,128]{0,1:T(8,128)S(1)}, u32[]{:S(2)}, u32[]{:S(2)}) collective-permute-start(f32[112,128]{0,1:T(8,128)S(1)} %dynamic-slice_bitcast_fusion), channel_id=1, source_target_pairs={{0,1},{1,0},{2,3},{3,2},{4,5},{5,4},{6,7},{7,6},{8,9},{9,8},{10,11... | collective-permute-start | bytes 172040 | tf_op jit(solution)/shard_map/ppermute | solution.py:107
  69.0 0.9 collective-permute-done
  70.0 0.1 copy.98
  70.1 0.7 broadcast_in_dim.63
  70.8 3.4 %all-to-all-start.2 = ((bf16[8,112,128]{2,1,0:T(8,128)(2,1)}), bf16[8,112,128]{2,1,0:T(8,128)(2,1)S(1)}, u32[]{:S(2)}, u32[]{:S(2)}) async-start(bf16[8,112,128]{2,1,0:T(8,128)(2,1)} %broadcast_in_dim.63), calls=%async_computation.2 | async-start | bytes 458752 | tf_op jit(solution)/shard_map/all_to_all | solution.py:31
  74.3 11.4 %all-to-all-done.2 = bf16[8,112,128]{2,1,0:T(8,128)(2,1)S(1)} async-done(((bf16[8,112,128]{2,1,0:T(8,128)(2,1)}), bf16[8,112,128]{2,1,0:T(8,128)(2,1)S(1)}, u32[]{:S(2)}, u32[]{:S(2)}) %all-to-all-start.2) | async-done | bytes 229408 | tf_op jit(solution)/shard_map/all_to_all | solution.py:31
  85.9 0.1 maximum_maximum_fusion
  86.0 1.5 broadcast_in_dim.105
  87.5 4.1 %all-to-all-start.3 = ((bf16[16,464,128]{2,1,0:T(8,128)(2,1)}), bf16[16,464,128]{2,1,0:T(8,128)(2,1)S(1)}, u32[]{:S(2)}, u32[]{:S(2)}) async-start(bf16[16,464,128]{2,1,0:T(8,128)(2,1)} %broadcast_in_dim.105), calls=%async_computation.3 | async-start | bytes 3801088 | tf_op jit(solution)/shard_map/all_to_all | solution.py:31
  91.7 0.9 collective-permute-start.1
  92.7 0.4 collective-permute-start.3
  93.1 24.5 %all-to-all-done.3 = bf16[16,464,128]{2,1,0:T(8,128)(2,1)S(1)} async-done(((bf16[16,464,128]{2,1,0:T(8,128)(2,1)}), bf16[16,464,128]{2,1,0:T(8,128)(2,1)S(1)}, u32[]{:S(2)}, u32[]{:S(2)}) %all-to-all-start.3) | async-done | bytes 1900576 | tf_op jit(solution)/shard_map/all_to_all | solution.py:31
  117.5 0.5 copy.99
  118.1 0.2 slice.6
  118.2 3.2 %collective-permute-start.4 = (bf16[112,128]{1,0:T(8,128)(2,1)S(1)}, bf16[112,128]{1,0:T(8,128)(2,1)S(1)}, u32[]{:S(2)}, u32[]{:S(2)}) collective-permute-start(bf16[112,128]{1,0:T(8,128)(2,1)S(1)} %dynamic-slice_bitcast_fusion.1), channel_id=1, source_target_pairs={{0,1},{1,0},{2,3},{3,2},{4,5},{5,4},{6,7},{7,6},{8,9},{9,8},{10,11... | collective-permute-start | bytes 86024 | tf_op jit(solution)/shard_map/ppermute | solution.py:137
  121.4 0.7 fusion.15
  122.2 2.4 %fusion.11 = f32[128,128]{1,0:T(8,128)S(1)} fusion(bf16[7168,128]{1,0:T(8,128)(2,1)S(1)} %bitcast.105, bf16[7168,128]{1,0:T(8,128)(2,1)} %collective-permute-done.1, f32[128]{0:T(128)S(1)} %add_rsqrt_fusion), kind=kOutput, calls=%fused_computation.16 | convolution fusion | flops 234897408 | bytes 3736064 | tf_op jit(solution)/shard_map/dot_general | solution.py:127
  124.5 0.7 fusion.16
  125.3 2.4 %multiply_convert_fusion = bf16[128,128]{1,0:T(8,128)(2,1)S(1)} fusion(f32[128,128]{1,0:T(8,128)S(1)} %fusion.11, f32[128]{0:T(128)S(1)} %fusion.48, f32[128]{0:T(128)S(1)} %add_rsqrt_fusion, bf16[7168,128]{1,0:T(8,128)(2,1)S(1)} %bitcast.107, bf16[7168,128]{1,0:T(8,128)(2,1)} %collective-permute-done.2), kind=kOutput, calls=%fused_computation.48 | convolution fusion | flops 235012096 | bytes 3769344 | tf_op jit(solution)/shard_map/dot_general | solution.py:127
  127.6 2.2 %convolution_convert_fusion = bf16[128,7168]{1,0:T(8,128)(2,1)S(1)} fusion(bf16[128,7168]{1,0:T(8,128)(2,1)} %collective-permute-done.3, bf16[128,7168]{1,0:T(8,128)(2,1)S(1)} %copy-done.9, bf16[128,128]{1,0:T(8,128)(2,1)S(1)} %multiply_convert_fusion, bf16[128,128]{1,0:T(8,128)(2,1)S(1)} %fusion.16), kind=kOutput, calls=%fused_computation | convolution fusion | flops 478150656 | bytes 5570560 | tf_op jit(solution)/shard_map/dot_general | solution.py:135
  129.8 0.6 fusion.39
  130.5 26.5 %all_to_all.31 = bf16[16,8,7168]{2,1,0:T(8,128)(2,1)S(1)} all-to-all(bf16[16,8,7168]{2,1,0:T(8,128)(2,1)S(1)} %bitcast.108), channel_id=1, replica_groups=mesh['x'=4,'y'=4,'h'=4,'l'=2,'c'=2] {'x','y'}, dimensions={0} | all-to-all | bytes 3670016 | tf_op jit(solution)/shard_map/all_to_all | solution.py:142
  157.0 0.3 reduce_sum.87
  157.4 14.2 %all_to_all.32 = bf16[16,2,1792]{2,1,0:T(2,128)(2,1)S(1)} all-to-all(bf16[16,2,1792]{2,1,0:T(2,128)(2,1)S(1)} %bitcast.114), channel_id=1, replica_groups=mesh['x'=4,'y'=4,'h'=4,'l'=2,'c'=2] {'h','l','c'}, dimensions={0} | all-to-all | bytes 229376 | tf_op jit(solution)/shard_map/all_to_all | solution.py:146
  171.6 0.7 reduce.3
  (55 shorter events, 0.9 us)
Async XLA Ops:
  0.6 61.7 %copy-start = (bf16[4096,112]{0,1:T(8,128)(2,1)S(1)}, bf16[4096,112]{0,1:T(8,128)(2,1)}, u32[]{:S(2)}) copy-start(bf16[4096,112]{0,1:T(8,128)(2,1)} %param.25) | copy-start | bytes 2752516
  0.6 5.7 %copy-start.2 = (bf16[2,384,512]{2,1,0:T(8,128)(2,1)S(1)}, bf16[2,384,512]{2,1,0:T(8,128)(2,1)}, u32[]{:S(2)}) copy-start(bf16[2,384,512]{2,1,0:T(8,128)(2,1)} %param.18) | copy-start | bytes 2359300
  0.7 5.1 %copy-start.3 = (bf16[2,64,384]{2,1,0:T(8,128)(2,1)S(1)}, bf16[2,64,384]{2,1,0:T(8,128)(2,1)}, u32[]{:S(2)}) copy-start(bf16[2,64,384]{2,1,0:T(8,128)(2,1)} %param.19) | copy-start | bytes 294916
  0.7 5.3 %copy-start.10 = (bf16[2,2,64]{2,1,0:T(2,128)(2,1)S(1)}, bf16[2,2,64]{2,1,0:T(2,128)(2,1)}, u32[]{:S(2)}) copy-start(bf16[2,2,64]{2,1,0:T(2,128)(2,1)} %param.21) | copy-start | bytes 1540
  1.8 4.9 %copy-start.4 = (bf16[2,2,512]{2,1,0:T(2,128)(2,1)S(1)}, bf16[2,2,512]{2,1,0:T(2,128)(2,1)}, u32[]{:S(2)}) copy-start(bf16[2,2,512]{2,1,0:T(2,128)(2,1)} %param.20) | copy-start | bytes 12292
  3.4 3.6 %copy-start.7 = (s32[64]{0:T(128)S(1)}, s32[64]{0:T(128)}, u32[]{:S(2)}) copy-start(s32[64]{0:T(128)} %param.23) | copy-start | bytes 772
  8.3 3.2 %copy-start.5 = (f32[2,128,4]{1,2,0:T(4,128)S(1)}, f32[2,128,4]{1,2,0:T(4,128)}, u32[]{:S(2)}) copy-start(f32[2,128,4]{1,2,0:T(4,128)} %param.28) | copy-start | bytes 12292
  8.3 3.2 %copy-start.6 = (s32[2,128,4]{1,2,0:T(4,128)S(1)}, s32[2,128,4]{1,2,0:T(4,128)}, u32[]{:S(2)}) copy-start(s32[2,128,4]{1,2,0:T(4,128)} %param.27) | copy-start | bytes 12292
  30.4 31.9 %all-to-all-start.1 = ((bf16[16,16,4096]{2,1,0:T(8,128)(2,1)}), bf16[16,16,4096]{2,1,0:T(8,128)(2,1)S(1)}, u32[]{:S(2)}, u32[]{:S(2)}) async-start(bf16[16,16,4096]{2,1,0:T(8,128)(2,1)} %broadcast_in_dim.62), calls=%async_computation.1 | async-start | bytes 4194304 | tf_op jit(solution)/shard_map/all_to_all | solution.py:31
  63.1 6.8 %collective-permute-start = (f32[112,128]{0,1:T(8,128)S(1)}, f32[112,128]{0,1:T(8,128)S(1)}, u32[]{:S(2)}, u32[]{:S(2)}) collective-permute-start(f32[112,128]{0,1:T(8,128)S(1)} %dynamic-slice_bitcast_fusion), channel_id=1, source_target_pairs={{0,1},{1,0},{2,3},{3,2},{4,5},{5,4},{6,7},{7,6},{8,9},{9,8},{10,11... | collective-permute-start | bytes 172040 | tf_op jit(solution)/shard_map/ppermute | solution.py:107
  70.8 14.9 %all-to-all-start.2 = ((bf16[8,112,128]{2,1,0:T(8,128)(2,1)}), bf16[8,112,128]{2,1,0:T(8,128)(2,1)S(1)}, u32[]{:S(2)}, u32[]{:S(2)}) async-start(bf16[8,112,128]{2,1,0:T(8,128)(2,1)} %broadcast_in_dim.63), calls=%async_computation.2 | async-start | bytes 458752 | tf_op jit(solution)/shard_map/all_to_all | solution.py:31
  87.5 30.0 %all-to-all-start.3 = ((bf16[16,464,128]{2,1,0:T(8,128)(2,1)}), bf16[16,464,128]{2,1,0:T(8,128)(2,1)S(1)}, u32[]{:S(2)}, u32[]{:S(2)}) async-start(bf16[16,464,128]{2,1,0:T(8,128)(2,1)} %broadcast_in_dim.105), calls=%async_computation.3 | async-start | bytes 3801088 | tf_op jit(solution)/shard_map/all_to_all | solution.py:31
  91.7 30.5 %collective-permute-start.1 = (bf16[7168,128]{1,0:T(8,128)(2,1)}, bf16[7168,128]{1,0:T(8,128)(2,1)}, u32[]{:S(2)}, u32[]{:S(2)}) collective-permute-start(bf16[7168,128]{1,0:T(8,128)(2,1)} %param.29), channel_id=1, source_target_pairs={{0,1},{1,0},{2,3},{3,2},{4,5},{5,4},{6,7},{7,6},{8,9},{9,8},{10,11... | collective-permute-start | bytes 5505032 | tf_op jit(solution)/shard_map/ppermute | solution.py:86
  92.6 32.7 %collective-permute-start.2 = (bf16[7168,128]{1,0:T(8,128)(2,1)}, bf16[7168,128]{1,0:T(8,128)(2,1)}, u32[]{:S(2)}, u32[]{:S(2)}) collective-permute-start(bf16[7168,128]{1,0:T(8,128)(2,1)} %param.30), channel_id=1, source_target_pairs={{0,1},{1,0},{2,3},{3,2},{4,5},{5,4},{6,7},{7,6},{8,9},{9,8},{10,11... | collective-permute-start | bytes 5505032 | tf_op jit(solution)/shard_map/ppermute | solution.py:87
  92.7 34.9 %collective-permute-start.3 = (bf16[128,7168]{1,0:T(8,128)(2,1)}, bf16[128,7168]{1,0:T(8,128)(2,1)}, u32[]{:S(2)}, u32[]{:S(2)}) collective-permute-start(bf16[128,7168]{1,0:T(8,128)(2,1)} %param.31), channel_id=1, source_target_pairs={{0,1},{1,0},{2,3},{3,2},{4,5},{5,4},{6,7},{7,6},{8,9},{9,8},{10,11... | collective-permute-start | bytes 5505032 | tf_op jit(solution)/shard_map/ppermute | solution.py:88
  118.0 3.4 %copy-start.1 = (bf16[7168,128]{1,0:T(8,128)(2,1)S(1)}, bf16[7168,128]{1,0:T(8,128)(2,1)}, u32[]{:S(2)}) copy-start(bf16[7168,128]{1,0:T(8,128)(2,1)} %param.29) | copy-start | bytes 5505028
  118.2 11.6 %collective-permute-start.4 = (bf16[112,128]{1,0:T(8,128)(2,1)S(1)}, bf16[112,128]{1,0:T(8,128)(2,1)S(1)}, u32[]{:S(2)}, u32[]{:S(2)}) collective-permute-start(bf16[112,128]{1,0:T(8,128)(2,1)S(1)} %dynamic-slice_bitcast_fusion.1), channel_id=1, source_target_pairs={{0,1},{1,0},{2,3},{3,2},{4,5},{5,4},{6,7},{7,6},{8,9},{9,8},{10,11... | collective-permute-start | bytes 86024 | tf_op jit(solution)/shard_map/ppermute | solution.py:137
  122.1 2.4 %copy-start.8 = (bf16[7168,128]{1,0:T(8,128)(2,1)S(1)}, bf16[7168,128]{1,0:T(8,128)(2,1)}, u32[]{:S(2)}) copy-start(bf16[7168,128]{1,0:T(8,128)(2,1)} %param.30) | copy-start | bytes 5505028
  125.2 2.4 %copy-start.9 = (bf16[128,7168]{1,0:T(8,128)(2,1)S(1)}, bf16[128,7168]{1,0:T(8,128)(2,1)}, u32[]{:S(2)}) copy-start(bf16[128,7168]{1,0:T(8,128)(2,1)} %param.31) | copy-start | bytes 5505028

commit v3 on v2

--- a/solution.py
+++ b/solution.py
@@ -1,6 +1,8 @@
 import jax
 import jax.numpy as jnp
 from jax import lax
+from jax.experimental import pallas as pl
+from jax.experimental.pallas import tpu as pltpu
 from jax.sharding import Mesh, PartitionSpec as P
 
 D = 7168
@@ -19,7 +21,6 @@
 NXY = 16
 NZ = 8
 NH = 4
-TOK = 256
 SWAP = ((0, 1), (1, 0))
 
 bf16 = jnp.bfloat16
@@ -59,6 +60,71 @@
     return ctx.reshape(STEPS * SLOTS, heads * HD)
 
 
+PARTS = 4
+
+
+def experts_kernel(rows, weight, g0, g1, u0, u1, d0, d1, out, acc, tot, inner):
+    step = pl.program_id(0)
+
+    @pl.when(step == 0)
+    def _():
+        acc[...] = jnp.zeros_like(acc)
+        tot[...] = jnp.zeros_like(tot)
+
+    @pl.when(step < PARTS)
+    def _():
+        wide = rows[:, : D // 16, :].reshape(D // PARTS, 128)
+        for j, w in enumerate((g0, u0, g1, u1)):
+            acc[j] += lax.dot_general(w[...], wide, (((0,), (0,)), ((), ())), preferred_element_type=f32)
+        tot[...] += jnp.sum(rows[:, D // 16 :, :].astype(f32), axis=(0, 1))[None]
+
+    @pl.when(step == PARTS - 1)
+    def _():
+        inv = lax.rsqrt(tot[...] / D + 1e-06)
+        for j in range(2):
+            gate = acc[2 * j] * inv
+            up = acc[2 * j + 1] * inv
+            act = gate / (1.0 + jnp.exp(-gate))
+            inner[j] = (act * up * weight[...]).astype(bf16)
+
+    @pl.when(step >= PARTS)
+    def _():
+        dims = (((0,), (0,)), ((), ()))
+        res = lax.dot_general(inner[0], d0[...], dims, preferred_element_type=f32)
+        res += lax.dot_general(inner[1], d1[...], dims, preferred_element_type=f32)
+        out[...] = res.astype(bf16)
+
+
+def experts(rows, weight, *weights):
+    first = lambda i: jnp.minimum(i, PARTS - 1)
+    last = lambda i: jnp.maximum(i - PARTS, 0)
+    k_spec = pl.BlockSpec((D // PARTS, 128), lambda i: (first(i), 0))
+    n_spec = pl.BlockSpec((128, D // PARTS), lambda i: (0, last(i)))
+    return pl.pallas_call(
+        experts_kernel,
+        grid=(2 * PARTS,),
+        in_specs=[
+            pl.BlockSpec((NXY // PARTS, D // 16 + 16, 128), lambda i: (first(i), 0, 0)),
+            pl.BlockSpec((1, 128), lambda i: (0, 0)),
+            k_spec,
+            k_spec,
+            k_spec,
+            k_spec,
+            n_spec,
+            n_spec,
+        ],
+        out_specs=pl.BlockSpec((128, D // PARTS), lambda i: (0, last(i))),
+        out_shape=jax.ShapeDtypeStruct((128, D), bf16),
+        scratch_shapes=[
+            pltpu.VMEM((4, 128, 128), f32),
+            pltpu.VMEM((1, 128), f32),
+            pltpu.VMEM((2, 128, 128), bf16),
+        ],
+        compiler_params=pltpu.CompilerParams(vmem_limit_bytes=24 * 1024 * 1024),
+        cost_estimate=pl.CostEstimate(flops=705_000_000, bytes_accessed=15_000_000, transcendentals=32768),
+    )(rows, weight, *weights)
+
+
 def body(
     query_latent,
     query_rope,
@@ -83,28 +149,35 @@
     own_count = lax.dynamic_slice_in_dim(row_counts, replica, 1, 0)
     live = jnp.arange(SLOTS) < own_count
 
+    out_other = lax.ppermute(out_proj, "c", SWAP)
     gate_other = lax.ppermute(gate_proj, "c", SWAP)
     up_other = lax.ppermute(up_proj, "c", SWAP)
     down_other = lax.ppermute(down_proj, "c", SWAP)
 
     ctx = attend(
         query_latent, query_rope, cache_latent, cache_rope, new_latent, new_rope, cache_lengths, live, value_up
-    )
+    ).reshape(STEPS, SLOTS, -1)
+    ctx_keep = lax.dynamic_index_in_dim(ctx, core, 0, keepdims=False)
+    ctx_send = lax.dynamic_index_in_dim(ctx, 1 - core, 0, keepdims=False)
+    ctx = jnp.concatenate([ctx_keep, lax.ppermute(ctx_send, "c", SWAP)], axis=1)
     gain = lax.dynamic_slice_in_dim(norm_gain, column * (D // 16), D // 16, 0)
     gain = jnp.broadcast_to(gain[:, None], (D // 16, 128))
     fours = jnp.sum(jnp.where(expert_ids == column, route_gates, 0.0), axis=2)
     live_rows = (jnp.arange(SLOTS)[None, :] < row_counts[:, None]).astype(f32).reshape(128)
     weight = lax.dynamic_index_in_dim(fours, core, 0, keepdims=False) * live_rows
+    weight = weight[None]
     ctx, gain, weight = lax.optimization_barrier((ctx, gain, weight))
 
-    ctx = spread(ctx, "h", NH).reshape(NH, STEPS, SLOTS, -1)
-    ctx = jnp.transpose(ctx, (1, 0, 2, 3)).reshape(16, -1)
-    ctx = spread(ctx, XY, NXY).reshape(TOK, -1)
-
-    part = jnp.dot(ctx, out_proj, preferred_element_type=f32).reshape(NXY, STEPS, 8, D // 64)
-    keep = lax.dynamic_index_in_dim(part, core, 1, keepdims=False).reshape(128, D // 64).T
-    send = lax.dynamic_index_in_dim(part, 1 - core, 1, keepdims=False).reshape(128, D // 64).T
-    chip = (keep + lax.ppermute(send, "c", SWAP)).astype(bf16)
+    ctx = spread(ctx, "h", NH).reshape(8, -1)
+    ctx, out_other, gate_other, up_other, down_other = lax.optimization_barrier(
+        (ctx, out_other, gate_other, up_other, down_other)
+    )
+    ctx = spread(ctx, XY, NXY).reshape(128, -1)
+
+    half = ctx.shape[1] // 2
+    part = jnp.dot(ctx[:, :half], out_proj, preferred_element_type=f32)
+    part = part + jnp.dot(ctx[:, half:], out_other, preferred_element_type=f32)
+    chip = part.T.astype(bf16)
     pieces = spread(chip, Z, NZ).reshape(NH, 2, D // 64, 128).astype(f32)
     hid = jnp.sum(pieces, axis=1).astype(bf16)
     own_hid = lax.dynamic_index_in_dim(hid, lax.axis_index("h"), 0, keepdims=False)
@@ -117,32 +190,19 @@
     packed = jnp.concatenate([scaled, high, low, jnp.zeros((14, 128), bf16)], axis=0)
     packed, own_hid = lax.optimization_barrier((packed, own_hid))
     rows = spread(packed, XY, NXY)
-
     rows, own_hid = lax.optimization_barrier((rows, own_hid))
-    total = jnp.sum(rows[:, 448:450, :].astype(f32), axis=(0, 1))
-    inv = lax.rsqrt(total / D + 1e-06)
-    wide = rows[:, :448, :].reshape(D, 128)
-
-    def product(weights):
-        return lax.dot_general(weights, wide, (((0,), (0,)), ((), ())), preferred_element_type=f32) * inv
-
-    inner = [
-        (jax.nn.silu(product(gate)) * product(up) * weight).astype(bf16)
-        for gate, up in ((gate_proj, up_proj), (gate_other, up_other))
-    ]
-    inner = jnp.concatenate(inner, axis=0)
-    down = jnp.concatenate([down_proj, down_other], axis=0)
-    out = lax.dot_general(inner, down, (((0,), (0,)), ((), ())), preferred_element_type=f32).astype(bf16)
+
+    out = experts(rows, weight, gate_proj, gate_other, up_proj, up_other, down_proj, down_other)
+    out, own_hid = lax.optimization_barrier((out, own_hid))
+    got = lax.all_to_all(out.reshape(NXY, 8, D), XY, 0, 0)
+    got, own_hid = lax.optimization_barrier((got, own_hid))
+    sums = jnp.sum(got.astype(f32), axis=0).astype(bf16)
+    sums = jnp.transpose(sums.reshape(NH, SLOTS, 4, D // 4), (0, 2, 1, 3)).reshape(16, SLOTS, D // 4)
 
     other_hid = lax.ppermute(own_hid, "c", SWAP)
     steps = jnp.where(core == 0, jnp.stack([own_hid, other_hid]), jnp.stack([other_hid, own_hid]))
     hidden = jnp.transpose(steps, (0, 2, 1))
 
-    out, hidden = lax.optimization_barrier((out, hidden))
-    got = lax.all_to_all(out.reshape(NXY, 8, D), XY, 0, 0)
-    got, hidden = lax.optimization_barrier((got, hidden))
-    sums = jnp.sum(got.astype(f32), axis=0).astype(bf16)
-    sums = jnp.transpose(sums.reshape(NH, SLOTS, 4, D // 4), (0, 2, 1, 3)).reshape(16, SLOTS, D // 4)
     own = lax.all_to_all(sums, ("h", "l", "c"), 0, 0)
     mixed = jnp.sum(own.astype(f32).reshape(NZ, STEPS, SLOTS, D // 4), axis=0).astype(bf16)
     return hidden, mixed

time: 173 us -> 157 us (0.908)
  waiting for transfers between devices: 62 us -> 16.9 us
  blocking collectives: 56.7 us -> 96.2 us
  Pallas kernels: 0 us -> 7.56 us
  starting transfers between devices: 24.8 us -> 17.6 us
  matrix products: 15.2 us -> 8.06 us
  local copies, waits for them, and re-layouts: 8.84 us -> 5.72 us
    all_to_all x1 -> x3, blocking collectives: 16 us -> 72.6 us  [spread(): return lax.all_to_all(copies, axes, 0, 0)]
    all_to_all x3 -> x1, waiting for transfers between devices: 61 us -> 8.95 us  [spread(): return lax.all_to_all(copies, axes, 0, 0)]
    all_to_all x1 -> x0, blocking collectives: 14.2 us -> none  [body(): own = lax.all_to_all(sums, ('h', 'l', 'c'), 0, 0)]
    all_to_all x3 -> x1, starting transfers between devices: 14.3 us -> 3.4 us  [spread(): return lax.all_to_all(copies, axes, 0, 0)]
    all_to_all x0 -> x1, starting transfers between devices: none -> 9.44 us  [body(): own = lax.all_to_all(sums, ('h', 'l', 'c'), 0, 0)]
    pallas_call x0 -> x1, Pallas kernels: none -> 7.56 us  [experts(): pl.pallas_call(experts_kernel, grid=(2 * PARTS,), in_specs=[pl.BlockSpec(...]
    all_to_all x0 -> x1, waiting for transfers between devices: none -> 7.02 us  [body(): own = lax.all_to_all(sums, ('h', 'l', 'c'), 0, 0)]
    dot_general x6 -> x2, matrix products: 9.03 us -> 2.08 us  [the longest x1 1.63 us: body(): part = part + jnp.dot(ctx[:, half:], out_other, preferred_element_type=f32)]
  transfers between devices with their start and end apart: 8 -> 8, of which waited for: 4 -> 3; matrix products, arithmetic and copies ran while one was open for 5% -> 8% of each run, Pallas kernels for 0% -> 0%
where the time goes in v3:
time: 157 us
  blocking collectives  96.2 us (61%)
  starting transfers between devices  17.6 us (11%)
  waiting for transfers between devices  16.9 us (11%)
  matrix products  8.06 us (5%)
  Pallas kernels  7.56 us (5%)
  local copies, waits for them, and re-layouts  5.72 us (4%)
  other arithmetic  3.61 us (2%)
    all_to_all x3, blocking collectives, spread(): return lax.all_to_all(copies, axes, 0, 0)  72.6 us
    all_to_all x1, blocking collectives, body(): got = lax.all_to_all(out.reshape(NXY, 8, D), XY, 0, 0)  23.5 us
    all_to_all x1, starting transfers between devices, body(): own = lax.all_to_all(sums, ('h', 'l', 'c'), 0, 0)  9.44 us
    all_to_all x1, waiting for transfers between devices, spread(): return lax.all_to_all(copies, axes, 0, 0)  8.95 us
    pallas_call x1, Pallas kernels, experts(): pl.pallas_call(experts_kernel, grid=(2 * PARTS,), in_specs=[pl.BlockSpec(...  7.56 us
    all_to_all x1, waiting for transfers between devices, body(): own = lax.all_to_all(sums, ('h', 'l', 'c'), 0, 0)  7.02 us
    all_to_all x1, starting transfers between devices, spread(): return lax.all_to_all(copies, axes, 0, 0)  3.4 us
    ppermute x1, starting transfers between devices, body(): gate_other = lax.ppermute(gate_proj, 'c', SWAP)  3.33 us
  transfers between devices with their start and end apart: 8, of which 3 were waited for; matrix products, arithmetic and copies ran while one was open for 8% of the time, Pallas kernels for 0%

profile of v3, /device:TPU:1, one launch (start us, length us, event | category | flops | bytes accessed | tf_op | source)
XLA Modules:
  0.0 156.6 jit_solution(12379642089513807223)
XLA Ops:
  0.7 3.3 %collective-permute-start.2 = (bf16[7168,128]{1,0:T(8,128)(2,1)}, bf16[7168,128]{1,0:T(8,128)(2,1)S(1)}, u32[]{:S(2)}, u32[]{:S(2)}) collective-permute-start(bf16[7168,128]{1,0:T(8,128)(2,1)} %g0.1), channel_id=1, source_target_pairs={{0,1},{1,0},{2,3},{3,2},{4,5},{5,4},{6,7},{7,6},{8,9},{9,8},{10,11... | collective-permute-start | bytes 5505032 | tf_op jit(solution)/shard_map/ppermute | solution.py:153
  4.0 0.1 collective-permute-start.3
  4.1 0.4 collective-permute-start.4
  4.5 1.0 reshape.191
  5.5 0.8 reshape.193
  6.3 0.7 iota_compare_fusion.1
  7.1 0.3 fusion.37
  7.4 0.8 fusion.27
  8.3 1.2 fusion.35
  9.4 0.1 fusion.36
  9.6 0.2 fusion.20
  9.8 0.3 fusion.22
  10.1 0.2 fusion.4
  10.4 0.6 dynamic_slice.21
  11.0 0.6 iota_compare_fusion.3
  11.7 3.0 %fusion.12 = bf16[2,2,32,128]{3,0,1,2:T(2,128)(2,1)S(1)} fusion(bf16[32,512,128]{2,1,0:T(8,128)(2,1)} %param.24, bf16[2,2,32,512]{3,2,1,0:T(8,128)(2,1)S(1)} %bitcast.68, pred[2]{0:T(512)(128)(4,1)S(1)} %iota_compare_fusion.3), kind=kOutput, calls=%fused_computation.12 | convolution fusion | flops 16809984 | bytes 4358146 | tf_op jit(solution)/shard_map/bshl,hld->sbhd/dot_general | solution.py:58
  14.7 0.2 collective-permute-start
  14.9 0.4 collective-permute-start.1
  15.3 0.1 iota_compare_fusion
  15.4 0.2 lt.85
  15.6 0.8 dynamic_slice.24
  16.4 0.1 broadcast_in_dim.56
  16.5 0.1 broadcast_in_dim.58
  16.6 13.5 %all_to_all.30 = bf16[4,2,8192]{2,1,0:T(2,128)(2,1)S(1)} all-to-all(bf16[4,2,8192]{2,1,0:T(2,128)(2,1)S(1)} %broadcast_in_dim.58), channel_id=1, replica_groups=mesh['x'=4,'y'=4,'h'=4,'l'=2,'c'=2] {'h'}, dimensions={0} | all-to-all | bytes 262144 | tf_op jit(solution)/shard_map/all_to_all | solution.py:32
  30.2 0.1 reshape.196
  30.3 0.2 broadcast_in_dim.59
  30.5 32.8 %all_to_all.31 = bf16[16,8,8192]{2,1,0:T(8,128)(2,1)S(1)} all-to-all(bf16[16,8,8192]{2,1,0:T(8,128)(2,1)S(1)} %broadcast_in_dim.59), channel_id=1, replica_groups=mesh['x'=4,'y'=4,'h'=4,'l'=2,'c'=2] {'x','y'}, dimensions={0} | all-to-all | bytes 4194304 | tf_op jit(solution)/shard_map/all_to_all | solution.py:32
  63.2 0.4 convolution_bitcast_fusion
  63.7 1.6 %fusion.8 = bf16[112,128]{1,0:T(8,128)(2,1)S(1)} fusion(f32[112,128]{1,0:T(8,128)S(1)} %convolution_bitcast_fusion, bf16[4096,112]{0,1:T(8,128)(2,1)} %collective-permute-done.1, bf16[128,8192]{1,0:T(8,128)(2,1)S(1)} %bitcast.62), kind=kOutput, calls=%fused_computation.10 | convolution fusion | flops 117469184 | bytes 2052096 | tf_op jit(solution)/shard_map/dot_general | solution.py:179
  65.3 0.7 broadcast_in_dim.96
  66.1 3.4 %all-to-all-start.2 = ((bf16[8,112,128]{2,1,0:T(8,128)(2,1)}), bf16[8,112,128]{2,1,0:T(8,128)(2,1)S(1)}, u32[]{:S(2)}, u32[]{:S(2)}) async-start(bf16[8,112,128]{2,1,0:T(8,128)(2,1)} %broadcast_in_dim.96), calls=%async_computation.2 | async-start | bytes 458752 | tf_op jit(solution)/shard_map/all_to_all | solution.py:32
  69.5 0.1 pad.7.clone
  69.5 8.9 %all-to-all-done.2 = bf16[8,112,128]{2,1,0:T(8,128)(2,1)S(1)} async-done(((bf16[8,112,128]{2,1,0:T(8,128)(2,1)}), bf16[8,112,128]{2,1,0:T(8,128)(2,1)S(1)}, u32[]{:S(2)}, u32[]{:S(2)}) %all-to-all-start.2) | async-done | bytes 229408 | tf_op jit(solution)/shard_map/all_to_all | solution.py:32
  78.5 0.1 multiply_reduce_fusion
  78.7 0.1 maximum_maximum_fusion
  78.8 0.2 broadcast_in_dim.98
  79.1 26.4 %all_to_all.32.rows = bf16[16,464,128]{2,1,0:T(8,128)(2,1)S(1)} all-to-all(bf16[16,464,128]{2,1,0:T(8,128)(2,1)S(1)} %broadcast_in_dim.98), channel_id=1, replica_groups=mesh['x'=4,'y'=4,'h'=4,'l'=2,'c'=2] {'x','y'}, dimensions={0} | all-to-all | bytes 3801088 | tf_op jit(solution)/shard_map/all_to_all | solution.py:32
  105.5 7.6 %shard_map.167 = bf16[128,7168]{1,0:T(8,128)(2,1)S(1)} custom-call(bf16[16,464,128]{2,1,0:T(8,128)(2,1)S(1)} %all_to_all.32.rows, f32[1,128]{1,0:T(1,128)S(1)} %fusion.33.weight, bf16[7168,128]{1,0:T(8,128)(2,1)S(1)} %copy-done.1, bf16[7168,128]{1,0:T(8,128)(2,1)S(1)} %collective-permute-done.2.g1, bf16[7168,128]{1,0:T(8,128)(2,1)S(1)} %copy-done.2, ...), custom_call_target="tpu_custom_call" | custom-call | flops 705000000 | bytes 15000000 | tf_op jit(solution)/shard_map/pallas_call | solution.py:103
  113.0 23.5 %all_to_all.33 = bf16[16,8,7168]{2,1,0:T(8,128)(2,1)S(1)} all-to-all(bf16[16,8,7168]{2,1,0:T(8,128)(2,1)S(1)} %bitcast.60), channel_id=1, replica_groups=mesh['x'=4,'y'=4,'h'=4,'l'=2,'c'=2] {'x','y'}, dimensions={0} | all-to-all | bytes 3670016 | tf_op jit(solution)/shard_map/all_to_all | solution.py:197
  136.5 0.3 reduce_sum.77
  136.8 0.1 reshape.200
  136.9 0.7 copy.46
  137.6 9.4 %all-to-all-start.5 = ((bf16[16,2,1792]{2,1,0:T(2,128)(2,1)}), bf16[16,2,1792]{2,1,0:T(2,128)(2,1)S(1)}, u32[]{:S(2)}, u32[]{:S(2)}) async-start(bf16[16,2,1792]{2,1,0:T(2,128)(2,1)} %bitcast.22), calls=%async_computation.5 | async-start | bytes 229376 | tf_op jit(solution)/shard_map/all_to_all | solution.py:206
  147.0 0.3 collective-permute-start.5
  147.3 0.9 collective-permute-done.5
  148.2 0.6 fusion.25
  148.9 7.0 %all-to-all-done.5 = bf16[16,2,1792]{2,1,0:T(2,128)(2,1)S(1)} async-done(((bf16[16,2,1792]{2,1,0:T(2,128)(2,1)}), bf16[16,2,1792]{2,1,0:T(2,128)(2,1)S(1)}, u32[]{:S(2)}, u32[]{:S(2)}) %all-to-all-start.5) | async-done | bytes 114720 | tf_op jit(solution)/shard_map/all_to_all | solution.py:206
  155.9 0.7 reduce.3
  (44 shorter events, 0.3 us)
Async XLA Ops:
  0.6 6.4 %copy-start = (bf16[2,384,512]{2,1,0:T(8,128)(2,1)S(1)}, bf16[2,384,512]{2,1,0:T(8,128)(2,1)}, u32[]{:S(2)}) copy-start(bf16[2,384,512]{2,1,0:T(8,128)(2,1)} %param.18) | copy-start | bytes 2359300
  0.6 9.5 %copy-start.4 = (bf16[2,2,512]{2,1,0:T(2,128)(2,1)S(1)}, bf16[2,2,512]{2,1,0:T(2,128)(2,1)}, u32[]{:S(2)}) copy-start(bf16[2,2,512]{2,1,0:T(2,128)(2,1)} %param.20) | copy-start | bytes 12292
  0.7 8.8 %copy-start.9 = (bf16[2,2,64]{2,1,0:T(2,128)(2,1)S(1)}, bf16[2,2,64]{2,1,0:T(2,128)(2,1)}, u32[]{:S(2)}) copy-start(bf16[2,2,64]{2,1,0:T(2,128)(2,1)} %param.21) | copy-start | bytes 1540
  0.7 29.6 %collective-permute-start.2 = (bf16[7168,128]{1,0:T(8,128)(2,1)}, bf16[7168,128]{1,0:T(8,128)(2,1)S(1)}, u32[]{:S(2)}, u32[]{:S(2)}) collective-permute-start(bf16[7168,128]{1,0:T(8,128)(2,1)} %g0.1), channel_id=1, source_target_pairs={{0,1},{1,0},{2,3},{3,2},{4,5},{5,4},{6,7},{7,6},{8,9},{9,8},{10,11... | collective-permute-start | bytes 5505032 | tf_op jit(solution)/shard_map/ppermute | solution.py:153
  4.0 26.3 %collective-permute-start.3 = (bf16[7168,128]{1,0:T(8,128)(2,1)}, bf16[7168,128]{1,0:T(8,128)(2,1)}, u32[]{:S(2)}, u32[]{:S(2)}) collective-permute-start(bf16[7168,128]{1,0:T(8,128)(2,1)} %u0.1), channel_id=1, source_target_pairs={{0,1},{1,0},{2,3},{3,2},{4,5},{5,4},{6,7},{7,6},{8,9},{9,8},{10,11... | collective-permute-start | bytes 5505032 | tf_op jit(solution)/shard_map/ppermute | solution.py:154
  4.1 26.2 %collective-permute-start.4 = (bf16[128,7168]{1,0:T(8,128)(2,1)}, bf16[128,7168]{1,0:T(8,128)(2,1)}, u32[]{:S(2)}, u32[]{:S(2)}) collective-permute-start(bf16[128,7168]{1,0:T(8,128)(2,1)} %d0.1), channel_id=1, source_target_pairs={{0,1},{1,0},{2,3},{3,2},{4,5},{5,4},{6,7},{7,6},{8,9},{9,8},{10,11... | collective-permute-start | bytes 5505032 | tf_op jit(solution)/shard_map/ppermute | solution.py:155
  5.5 4.9 %copy-start.7 = (s32[64]{0:T(128)S(1)}, s32[64]{0:T(128)}, u32[]{:S(2)}) copy-start(s32[64]{0:T(128)} %param.23) | copy-start | bytes 772
  11.6 3.9 %copy-start.5 = (f32[2,128,4]{1,2,0:T(4,128)S(1)}, f32[2,128,4]{1,2,0:T(4,128)}, u32[]{:S(2)}) copy-start(f32[2,128,4]{1,2,0:T(4,128)} %param.28) | copy-start | bytes 12292
  11.7 3.9 %copy-start.6 = (s32[2,128,4]{1,2,0:T(4,128)S(1)}, s32[2,128,4]{1,2,0:T(4,128)}, u32[]{:S(2)}) copy-start(s32[2,128,4]{1,2,0:T(4,128)} %param.27) | copy-start | bytes 12292
  14.7 1.7 %collective-permute-start = (bf16[2,4096]{1,0:T(2,128)(2,1)S(1)}, bf16[2,4096]{1,0:T(2,128)(2,1)S(1)}, u32[]{:S(2)}, u32[]{:S(2)}) collective-permute-start(bf16[2,4096]{1,0:T(2,128)(2,1)S(1)} %get-tuple-element.35), channel_id=1, source_target_pairs={{0,1},{1,0},{2,3},{3,2},{4,5},{5,4},{6,7},{7,6},{8,9},{9,8},{10,11... | collective-permute-start | bytes 49160 | tf_op jit(solution)/shard_map/ppermute | solution.py:162
  14.9 15.3 %collective-permute-start.1 = (bf16[4096,112]{0,1:T(8,128)(2,1)}, bf16[4096,112]{0,1:T(8,128)(2,1)}, u32[]{:S(2)}, u32[]{:S(2)}) collective-permute-start(bf16[4096,112]{0,1:T(8,128)(2,1)} %param.25), channel_id=1, source_target_pairs={{0,1},{1,0},{2,3},{3,2},{4,5},{5,4},{6,7},{7,6},{8,9},{9,8},{10,11... | collective-permute-start | bytes 2752520 | tf_op jit(solution)/shard_map/ppermute | solution.py:152
  30.5 32.8 %copy-start.8 = (bf16[4096,112]{0,1:T(8,128)(2,1)S(1)}, bf16[4096,112]{0,1:T(8,128)(2,1)}, u32[]{:S(2)}) copy-start(bf16[4096,112]{0,1:T(8,128)(2,1)} %param.25) | copy-start | bytes 2752516
  66.1 12.4 %all-to-all-start.2 = ((bf16[8,112,128]{2,1,0:T(8,128)(2,1)}), bf16[8,112,128]{2,1,0:T(8,128)(2,1)S(1)}, u32[]{:S(2)}, u32[]{:S(2)}) async-start(bf16[8,112,128]{2,1,0:T(8,128)(2,1)} %broadcast_in_dim.96), calls=%async_computation.2 | async-start | bytes 458752 | tf_op jit(solution)/shard_map/all_to_all | solution.py:32
  78.8 26.6 %copy-start.3 = (bf16[128,7168]{1,0:T(8,128)(2,1)S(1)}, bf16[128,7168]{1,0:T(8,128)(2,1)}, u32[]{:S(2)}) copy-start(bf16[128,7168]{1,0:T(8,128)(2,1)} %d0.1) | copy-start | bytes 5505028
  79.1 26.4 %copy-start.1 = (bf16[7168,128]{1,0:T(8,128)(2,1)S(1)}, bf16[7168,128]{1,0:T(8,128)(2,1)}, u32[]{:S(2)}) copy-start(bf16[7168,128]{1,0:T(8,128)(2,1)} %g0.1) | copy-start | bytes 5505028
  79.1 26.4 %copy-start.2 = (bf16[7168,128]{1,0:T(8,128)(2,1)S(1)}, bf16[7168,128]{1,0:T(8,128)(2,1)}, u32[]{:S(2)}) copy-start(bf16[7168,128]{1,0:T(8,128)(2,1)} %u0.1) | copy-start | bytes 5505028
  137.6 18.3 %all-to-all-start.5 = ((bf16[16,2,1792]{2,1,0:T(2,128)(2,1)}), bf16[16,2,1792]{2,1,0:T(2,128)(2,1)S(1)}, u32[]{:S(2)}, u32[]{:S(2)}) async-start(bf16[16,2,1792]{2,1,0:T(2,128)(2,1)} %bitcast.22), calls=%async_computation.5 | async-start | bytes 229376 | tf_op jit(solution)/shard_map/all_to_all | solution.py:206
  147.0 1.2 collective-permute-start.5

commit v4 on v2

v4 whole, which is shorter than its diff:
```python
import jax
import jax.numpy as jnp
from jax import lax
from jax.experimental import pallas as pl
from jax.experimental.pallas import tpu as pltpu
from jax.sharding import Mesh, PartitionSpec as P

D = 7168
LAT = 512
ROPE = 64
HD = 128
FFN = 2048
STEPS = 2
SLOTS = 2
CACHE = 384

DP = ("x", "y", "h")
TP = ("l", "c")
XY = ("x", "y")
Z = ("h", "l")
NXY = 16
NZ = 8
NH = 4
SWAP = ((0, 1), (1, 0))

bf16 = jnp.bfloat16
f32 = jnp.float32


def spread(value, axes, count):
    copies = jnp.broadcast_to(value[None], (count,) + value.shape)
    return lax.all_to_all(copies, axes, 0, 0)


def attend_kernel(place, lengths, counts, ql_hbm, qr_hbm, cl_hbm, cr_hbm, nl_hbm, nr_hbm, v_hbm, out,
                  ql, qr, cl, cr, nl, nr, v, q_rows, r_rows, lat, sems):
    pairs = ((ql_hbm, ql), (qr_hbm, qr), (cl_hbm, cl), (cr_hbm, cr), (nl_hbm, nl), (nr_hbm, nr), (v_hbm, v))
    copies = [pltpu.make_async_copy(src, dst, sems.at[i]) for i, (src, dst) in enumerate(pairs)]
    for copy in copies:
        copy.start()
    heads = v.shape[0]
    rows = STEPS * heads
    scale = (HD + ROPE) ** (-0.5)
    copies[0].wait()
    copies[1].wait()
    for s in range(STEPS):
        for h in range(heads):
            q_rows[:, s * heads + h, :] = ql[s, :, h * LAT : (h + 1) * LAT].astype(f32)
        for p in range(heads // 2):
            pair = qr[s, :, p * 2 * ROPE : (p + 1) * 2 * ROPE].astype(f32)
            r_rows[:, s * heads + 2 * p, :] = pair
            r_rows[:, s * heads + 2 * p + 1, :] = pair
    for copy in copies[2:6]:
        copy.wait()
    step_of_row = lax.broadcasted_iota(jnp.int32, (rows, 1), 0) // heads
    position = lax.broadcasted_iota(jnp.int32, (rows, CACHE), 1)
    row_id = lax.broadcasted_iota(jnp.int32, (rows, 2 * ROPE), 0)
    lane_id = lax.broadcasted_iota(jnp.int32, (rows, 2 * ROPE), 1)
    own_half = row_id % 2 == lane_id // ROPE
    dims = (((1,), (1,)), ((), ()))
    for b in range(SLOTS):
        qf = q_rows[b]
        rf = jnp.where(own_half, r_rows[b], 0.0)
        rope = jnp.concatenate([cr[b], cr[b]], axis=0)
        old = lax.dot_general(qf.astype(bf16), cl[b], dims, preferred_element_type=f32)
        old = (old + jnp.dot(rf.astype(bf16), rope, preferred_element_type=f32)) * scale
        old = jnp.where(position < lengths[b], old, -1e30)
        top = jnp.max(old, axis=1, keepdims=True)
        new = []
        for i in range(STEPS):
            fresh_rope = nr[i, b : b + 1, :].astype(f32)
            n = jnp.sum(qf * nl[i, b : b + 1, :].astype(f32), axis=1, keepdims=True)
            n += jnp.sum(rf * jnp.concatenate([fresh_rope, fresh_rope], axis=1), axis=1, keepdims=True)
            n = jnp.where(step_of_row >= i, n * scale, -1e30)
            new.append(n)
            top = jnp.maximum(top, n)
        old = jnp.exp(old - top)
        new = [jnp.exp(n - top) for n in new]
        total = jnp.sum(old, axis=1, keepdims=True) + new[0] + new[1]
        res = jnp.dot((old / total).astype(bf16), cl[b], preferred_element_type=f32)
        for i in range(STEPS):
            res += (new[i] / total).astype(bf16).astype(f32) * nl[i, b : b + 1, :].astype(f32)
        for s in range(STEPS):
            lat[:, s * SLOTS + b, :] = res[s * heads : (s + 1) * heads, :]
    copies[6].wait()
    slot = lax.broadcasted_iota(jnp.int32, (STEPS * SLOTS, HD), 0) % SLOTS
    live = slot < counts[place[0]]
    for h in range(heads):
        ctx = jnp.dot(lat[h].astype(bf16), v[h], preferred_element_type=f32)
        out[:, h * HD : (h + 1) * HD] = jnp.where(live, ctx[: STEPS * SLOTS], 0.0).astype(bf16)


def attend(place, lengths, counts, *arrays):
    heads = arrays[-1].shape[0]
    scalars = pl.BlockSpec(memory_space=pltpu.SMEM)
    far = pl.BlockSpec(memory_space=pl.ANY)
    return pl.pallas_call(
        attend_kernel,
        in_specs=[scalars] * 3 + [far] * 7,
        out_specs=pl.BlockSpec(memory_space=pltpu.VMEM),
        out_shape=jax.ShapeDtypeStruct((STEPS * SLOTS, heads * HD), bf16),
        scratch_shapes=[pltpu.VMEM(a.shape, bf16) for a in arrays]
        + [
            pltpu.VMEM((SLOTS, STEPS * heads, LAT), f32),
            pltpu.VMEM((SLOTS, STEPS * heads, 2 * ROPE), f32),
            pltpu.VMEM((heads, 8, LAT), f32),
            pltpu.SemaphoreType.DMA((7,)),
        ],
        compiler_params=pltpu.CompilerParams(vmem_limit_bytes=52 * 1024 * 1024),
        cost_estimate=pl.CostEstimate(flops=160_000_000, bytes_accessed=6_000_000, transcendentals=50_000),
    )(place, lengths, counts, *arrays)


def experts_kernel(rows, weight, g0, g1, u0, u1, d0, d1, out):
    parts, chunks = 4, 7
    depth, width = D // parts, D // chunks
    blocks = NXY // parts
    acc = [jnp.zeros((128, 256), f32) for _ in range(2)]
    tot = jnp.zeros((1, 128), f32)
    for i in range(parts):
        k = slice(i * depth, (i + 1) * depth)
        group = slice(i * blocks, (i + 1) * blocks)
        wide = rows[group, : D // 16, :].reshape(depth, 128).T
        for j, (g, u) in enumerate(((g0, u0), (g1, u1))):
            acc[j] += jnp.dot(wide, jnp.concatenate([g[k, :], u[k, :]], axis=1), preferred_element_type=f32)
        tot += jnp.sum(rows[group, D // 16 :, :].astype(f32), axis=(0, 1))[None]
    inv = lax.rsqrt(tot / D + 1e-06).T
    scale = weight[...].T
    inner = []
    for j in range(2):
        gate = acc[j][:, :128] * inv
        up = acc[j][:, 128:] * inv
        inner.append((gate / (1.0 + jnp.exp(-gate)) * up * scale).astype(bf16))
    inner = jnp.concatenate(inner, axis=1)
    for n in range(chunks):
        c = slice(n * width, (n + 1) * width)
        down = jnp.concatenate([d0[:, c], d1[:, c]], axis=0)
        out[:, c] = jnp.dot(inner, down, preferred_element_type=f32).astype(bf16)


def experts(rows, weight, *weights):
    near = pl.BlockSpec(memory_space=pltpu.VMEM)
    return pl.pallas_call(
        experts_kernel,
        in_specs=[near] * 8,
        out_specs=near,
        out_shape=jax.ShapeDtypeStruct((128, D), bf16),
        compiler_params=pltpu.CompilerParams(vmem_limit_bytes=24 * 1024 * 1024),
        cost_estimate=pl.CostEstimate(flops=705_000_000, bytes_accessed=15_000_000, transcendentals=32768),
    )(rows, weight, *weights)


def body(
    query_latent,
    query_rope,
    cache_latent,
    cache_rope,
    new_latent,
    new_rope,
    cache_lengths,
    row_counts,
    value_up,
    out_proj,
    norm_gain,
    expert_ids,
    route_gates,
    gate_proj,
    up_proj,
    down_proj,
):
    core = lax.axis_index("c")
    column = lax.axis_index(XY)

    out_other = lax.ppermute(out_proj, "c", SWAP)
    gate_other = lax.ppermute(gate_proj, "c", SWAP)
    up_other = lax.ppermute(up_proj, "c", SWAP)
    down_other = lax.ppermute(down_proj, "c", SWAP)

    ctx = attend(
        lax.axis_index(DP)[None],
        cache_lengths,
        row_counts,
        query_latent,
        query_rope,
        cache_latent,
        cache_rope,
        new_latent,
        new_rope,
        value_up,
    )
    ctx = jnp.broadcast_to(ctx.reshape(1, STEPS, SLOTS, -1), (NH, STEPS, SLOTS, ctx.shape[1]))
    ctx = lax.all_to_all(ctx.reshape(NH * 2, SLOTS, -1), ("h", "c"), 0, 0).reshape(NH, 2, SLOTS, -1)
    ctx, expert_ids, route_gates, row_counts, norm_gain, out_other, gate_other, up_other, down_other = (
        lax.optimization_barrier(
            (ctx, expert_ids, route_gates, row_counts, norm_gain, out_other, gate_other, up_other, down_other)
        )
    )

    def prepare():
        gain = lax.dynamic_slice_in_dim(norm_gain, column * (D // 16), D // 16, 0)
        fours = jnp.sum(jnp.where(expert_ids == column, route_gates, 0.0), axis=2)
        live = (jnp.arange(SLOTS)[None, :] < row_counts[:, None]).astype(f32).reshape(1, 128)
        return jnp.broadcast_to(gain[:, None], (D // 16, 128)), fours * live

    def leave():
        return jnp.zeros((D // 16, 128), f32), jnp.zeros((STEPS, 128), f32)

    gain, weight = lax.cond(core == 0, prepare, leave)
    ctx, gain, weight = lax.optimization_barrier((ctx, gain, weight))
    gain = jnp.where(core == 0, gain, lax.ppermute(gain, "c", ((0, 1),)))
    weight = jnp.where(core == 0, weight, lax.ppermute(weight, "c", ((0, 1),)))
    weight = lax.dynamic_slice_in_dim(weight, core, 1, 0)

    ctx = jnp.where(core == 0, ctx, ctx[:, ::-1])
    ctx = jnp.transpose(ctx, (0, 2, 1, 3)).reshape(8, -1)
    ctx = spread(ctx, XY, NXY).reshape(128, -1)

    half = ctx.shape[1] // 2
    part = jnp.dot(ctx[:, :half], out_proj, preferred_element_type=f32)
    part = part + jnp.dot(ctx[:, half:], out_other, preferred_element_type=f32)
    chip = part.T.astype(bf16)
    pieces = spread(chip, Z, NZ).reshape(NH, 2, D // 64, 128).astype(f32)
    hid = jnp.sum(pieces, axis=1).astype(bf16)
    own_hid = lax.dynamic_index_in_dim(hid, lax.axis_index("h"), 0, keepdims=False)

    hid_f = hid.astype(f32).reshape(D // 16, 128)
    scaled = (hid_f * gain).astype(bf16)
    squares = jnp.sum(hid_f * hid_f, axis=0, keepdims=True)
    high = squares.astype(bf16)
    low = (squares - high.astype(f32)).astype(bf16)
    packed = jnp.concatenate([scaled, high, low, jnp.zeros((14, 128), bf16)], axis=0)
    packed, own_hid = lax.optimization_barrier((packed, own_hid))
    rows = spread(packed, XY, NXY)
    rows, own_hid = lax.optimization_barrier((rows, own_hid))

    out = experts(rows, weight, gate_proj, gate_other, up_proj, up_other, down_proj, down_other)
    out, own_hid = lax.optimization_barrier((out, own_hid))
    got = lax.all_to_all(out.reshape(NXY, 8, D), XY, 0, 0)
    got, own_hid = lax.optimization_barrier((got, own_hid))
    sums = jnp.sum(got.astype(f32), axis=0).astype(bf16)
    sums = jnp.transpose(sums.reshape(NH, SLOTS, 4, D // 4), (0, 2, 1, 3)).reshape(16, SLOTS, D // 4)

    other_hid = lax.ppermute(own_hid, "c", SWAP)
    steps = jnp.where(core == 0, jnp.stack([own_hid, other_hid]), jnp.stack([other_hid, own_hid]))
    hidden = jnp.transpose(steps, (0, 2, 1))

    own = lax.all_to_all(sums, ("h", "l", "c"), 0, 0)
    mixed = jnp.sum(own.astype(f32).reshape(NZ, STEPS, SLOTS, D // 4), axis=0).astype(bf16)
    return hidden, mixed


def solution(mesh):
    fine = Mesh(mesh.devices.reshape(4, 4, 4, 2, 2), ("x", "y", "h", "l", "c"))
    return jax.shard_map(
        body,
        mesh=fine,
        in_specs=(
            P(None, DP, TP),
            P(None, DP, TP),
            P(DP, None, None),
            P(DP, None, None),
            P(None, DP, None),
            P(None, DP, None),
            P(DP),
            P(),
            P(TP, None, None),
            P(TP, DP),
            P(),
            P(),
            P(),
            P(None, DP + TP),
            P(None, DP + TP),
            P(DP + TP, None),
        ),
        out_specs=(P(None, None, DP), P(None, DP, TP)),
        check_vma=False,
    )
```

time: 173 us -> 163 us (0.942)
  waiting for transfers between devices: 62 us -> 44 us
  matrix products: 15.2 us -> 0.91 us
  Pallas kernels: 0 us -> 7.98 us
  local copies, waits for them, and re-layouts: 8.84 us -> 16 us
  starting transfers between devices: 24.8 us -> 31.6 us
  blocking collectives: 56.7 us -> 58.8 us
    all_to_all x3 -> x2, waiting for transfers between devices: 61 us -> 22.3 us  [spread(): return lax.all_to_all(copies, axes, 0, 0)]
    all_to_all x0 -> x2, starting transfers between devices: none -> 16.7 us  [the longest x1 9.54 us: body(): own = lax.all_to_all(sums, ('h', 'l', 'c'), 0, 0)]
    all_to_all x0 -> x2, waiting for transfers between devices: none -> 15 us  [the longest x1 8.03 us: body(): lax.all_to_all(ctx.reshape(NH * 2, SLOTS, -1), ('h', 'c'), 0, 0)]
    all_to_all x1, blocking collectives: 16 us -> 30.9 us  [spread(): return lax.all_to_all(copies, axes, 0, 0)]
    dot_general x13 -> x2, matrix products: 15.2 us -> 0.91 us  [the longest x1 0.46 us: body(): part = part + jnp.dot(ctx[:, half:], out_other, preferred_element_type=f32)]
    all_to_all x1 -> x0, blocking collectives: 14.2 us -> none  [body(): own = lax.all_to_all(sums, ('h', 'l', 'c'), 0, 0)]
    unnamed x23 -> x33, local copies, waits for them, and re-layouts: 0.09 us -> 11.8 us
    pallas_call x0 -> x2, Pallas kernels: none -> 7.98 us  [the longest x1 4.11 us: attend(): pl.pallas_call(attend_kernel, in_specs=[scalars] * 3 + [far] * 7, out_spe...]
  transfers between devices with their start and end apart: 8 -> 11, of which waited for: 4 -> 6; matrix products, arithmetic and copies ran while one was open for 5% -> 1% of each run, Pallas kernels for 0% -> 3%
where the time goes in v4:
time: 163 us; the launch traced here: 162 us
  blocking collectives  58.8 us (36%)
  waiting for transfers between devices  44 us (27%)
  starting transfers between devices  31.6 us (19%)
  local copies, waits for them, and re-layouts  16 us (10%)
  Pallas kernels  7.98 us (5%)
  other arithmetic  1.99 us (1%)
    all_to_all x1, blocking collectives, spread(): return lax.all_to_all(copies, axes, 0, 0)  30.9 us
    all_to_all x1, blocking collectives, body(): got = lax.all_to_all(out.reshape(NXY, 8, D), XY, 0, 0)  28 us
    all_to_all x2, waiting for transfers between devices, spread(): return lax.all_to_all(copies, axes, 0, 0)  22.3 us
    unnamed x33, local copies, waits for them, and re-layouts  11.8 us
    all_to_all x1, starting transfers between devices, body(): own = lax.all_to_all(sums, ('h', 'l', 'c'), 0, 0)  9.54 us
    all_to_all x2, starting transfers between devices, spread(): return lax.all_to_all(copies, axes, 0, 0)  8.2 us
    all_to_all x1, waiting for transfers between devices, body(): lax.all_to_all(ctx.reshape(NH * 2, SLOTS, -1), ('h', 'c'), 0, 0)  8.03 us
    all_to_all x1, starting transfers between devices, body(): lax.all_to_all(ctx.reshape(NH * 2, SLOTS, -1), ('h', 'c'), 0, 0)  7.13 us
  transfers between devices with their start and end apart: 11, of which 6 were waited for; matrix products, arithmetic and copies ran while one was open for 1% of the time, Pallas kernels for 3%

profile of v4, /device:TPU:1, one launch (start us, length us, event | category | flops | bytes accessed | tf_op | source)
XLA Modules:
  0.0 162.2 jit_solution(17464574402502126142)
XLA Ops:
  0.6 3.3 %collective-permute-start.1 = (bf16[7168,128]{1,0:T(8,128)(2,1)}, bf16[7168,128]{1,0:T(8,128)(2,1)S(1)}, u32[]{:S(2)}, u32[]{:S(2)}) collective-permute-start(bf16[7168,128]{1,0:T(8,128)(2,1)} %g0.1), channel_id=1, source_target_pairs={{0,1},{1,0},{2,3},{3,2},{4,5},{5,4},{6,7},{7,6},{8,9},{9,8},{10,11... | collective-permute-start | bytes 5505032 | tf_op jit(solution)/shard_map/ppermute | solution.py:175
  4.0 0.1 collective-permute-start.2
  4.1 0.4 collective-permute-start.3
  4.5 0.1 collective-permute-start
  4.6 1.1 copy-done.5
  5.7 0.9 copy-done.6
  6.6 0.9 copy-done.7
  7.5 0.7 copy-done.8
  8.2 0.7 copy-done.9
  8.9 0.7 copy-done.10
  9.6 0.7 copy-done.11
  10.3 4.1 %shard_map.167 = bf16[4,4096]{1,0:T(4,128)(2,1)S(1)} custom-call(s32[1]{0:T(128)} %bitcast.place, s32[2]{0:T(128)S(1)} %copy-done.11, s32[64]{0:T(128)} %counts.1, bf16[2,2,16384]{2,1,0:T(2,128)(2,1)S(1)} %copy-done.6, bf16[2,2,2048]{2,1,0:T(2,128)(2,1)S(1)} %copy-done.8, bf16[2,384,512]{2,1,0:T(8,128)(2,1)S(1)} %copy-done.5, ...), custom_call_target="tpu_custom_call" | custom-call | flops 160000000 | bytes 6000000 | tf_op jit(solution)/shard_map/pallas_call | solution.py:97
  14.4 0.7 broadcast_in_dim.30
  15.1 7.1 %all-to-all-start = ((bf16[8,2,4096]{2,1,0:T(2,128)(2,1)}), bf16[8,2,4096]{2,1,0:T(2,128)(2,1)S(1)}, u32[]{:S(2)}, u32[]{:S(2)}) async-start(bf16[8,2,4096]{2,1,0:T(2,128)(2,1)} %bitcast.1), calls=%async_computation | async-start | bytes 262144 | tf_op jit(solution)/shard_map/all_to_all | solution.py:192
  22.3 8.0 %all-to-all-done = bf16[8,2,4096]{2,1,0:T(2,128)(2,1)S(1)} async-done(((bf16[8,2,4096]{2,1,0:T(2,128)(2,1)}), bf16[8,2,4096]{2,1,0:T(2,128)(2,1)S(1)}, u32[]{:S(2)}, u32[]{:S(2)}) %all-to-all-start) | async-done | bytes 131104 | tf_op jit(solution)/shard_map/all_to_all | solution.py:192
  30.4 0.1 fusion.5
  30.5 0.1 copy.20
  30.7 0.1 copy.22
  30.8 0.2 broadcast_in_dim.49
  31.0 30.9 %all_to_all.30 = bf16[16,8,8192]{2,1,0:T(8,128)(2,1)S(1)} all-to-all(bf16[16,8,8192]{2,1,0:T(8,128)(2,1)S(1)} %broadcast_in_dim.49), channel_id=1, replica_groups=mesh['x'=4,'y'=4,'h'=4,'l'=2,'c'=2] {'x','y'}, dimensions={0} | all-to-all | bytes 4194304 | tf_op jit(solution)/shard_map/all_to_all | solution.py:32
  61.9 0.4 convolution_bitcast_fusion
  62.3 0.5 fusion.1
  62.8 0.7 broadcast_in_dim.50
  63.5 4.5 %all-to-all-start.2 = ((bf16[8,112,128]{2,1,0:T(8,128)(2,1)}), bf16[8,112,128]{2,1,0:T(8,128)(2,1)S(1)}, u32[]{:S(2)}, u32[]{:S(2)}) async-start(bf16[8,112,128]{2,1,0:T(8,128)(2,1)} %broadcast_in_dim.50), calls=%async_computation.2 | async-start | bytes 458752 | tf_op jit(solution)/shard_map/all_to_all | solution.py:32
  68.0 0.1 pad.7.clone
  68.1 1.3 collective-permute-start.4
  69.4 7.6 %all-to-all-done.2 = bf16[8,112,128]{2,1,0:T(8,128)(2,1)S(1)} async-done(((bf16[8,112,128]{2,1,0:T(8,128)(2,1)}), bf16[8,112,128]{2,1,0:T(8,128)(2,1)S(1)}, u32[]{:S(2)}, u32[]{:S(2)}) %all-to-all-start.2) | async-done | bytes 229408 | tf_op jit(solution)/shard_map/all_to_all | solution.py:32
  77.0 0.1 multiply_reduce_fusion
  77.2 0.1 maximum_maximum_fusion
  77.3 1.5 broadcast_in_dim.52
  78.8 3.7 %all-to-all-start.3 = ((bf16[16,464,128]{2,1,0:T(8,128)(2,1)}), bf16[16,464,128]{2,1,0:T(8,128)(2,1)S(1)}, u32[]{:S(2)}, u32[]{:S(2)}) async-start(bf16[16,464,128]{2,1,0:T(8,128)(2,1)} %broadcast_in_dim.52), calls=%async_computation.3 | async-start | bytes 3801088 | tf_op jit(solution)/shard_map/all_to_all | solution.py:32
  82.6 1.3 collective-permute-start.5
  83.9 5.7 %collective-permute-done.5 = f32[2,128]{1,0:T(2,128)S(1)} collective-permute-done((f32[2,128]{1,0:T(2,128)S(1)}, f32[2,128]{1,0:T(2,128)S(1)}, u32[]{:S(2)}, u32[]{:S(2)}) %collective-permute-start.5) | collective-permute-done | bytes 1056 | tf_op jit(solution)/shard_map/ppermute | solution.py:211
  89.6 14.7 %all-to-all-done.3.rows = bf16[16,464,128]{2,1,0:T(8,128)(2,1)S(1)} async-done(((bf16[16,464,128]{2,1,0:T(8,128)(2,1)}), bf16[16,464,128]{2,1,0:T(8,128)(2,1)S(1)}, u32[]{:S(2)}, u32[]{:S(2)}) %all-to-all-start.3) | async-done | bytes 1900576 | tf_op jit(solution)/shard_map/all_to_all | solution.py:32
  104.3 1.5 copy-done
  105.8 1.5 copy-done.1
  107.3 1.5 copy-done.2
  108.8 1.5 copy-done.4
  110.3 3.9 %shard_map.168 = bf16[128,7168]{1,0:T(8,128)(2,1)S(1)} custom-call(bf16[16,464,128]{2,1,0:T(8,128)(2,1)S(1)} %all-to-all-done.3.rows, f32[1,128]{1,0:T(1,128)S(1)} %constant_dynamic-slice_fusion.weight, bf16[7168,128]{1,0:T(8,128)(2,1)S(1)} %copy-done, bf16[7168,128]{1,0:T(8,128)(2,1)S(1)} %copy-done.4, bf16[7168,128]{1,0:T(8,128)(2,1)S(1)} %copy-done.1, ...), custom_call_target="tpu_custom_call" | custom-call | flops 705000000 | bytes 15000000 | tf_op jit(solution)/shard_map/pallas_call | solution.py:143
  114.1 28.0 %all_to_all.31 = bf16[16,8,7168]{2,1,0:T(8,128)(2,1)S(1)} all-to-all(bf16[16,8,7168]{2,1,0:T(8,128)(2,1)S(1)} %bitcast.36), channel_id=1, replica_groups=mesh['x'=4,'y'=4,'h'=4,'l'=2,'c'=2] {'x','y'}, dimensions={0} | all-to-all | bytes 3670016 | tf_op jit(solution)/shard_map/all_to_all | solution.py:238
  142.1 0.3 reduce_sum.56
  142.4 0.7 copy.21
  143.2 9.5 %all-to-all-start.5 = ((bf16[16,2,1792]{2,1,0:T(2,128)(2,1)}), bf16[16,2,1792]{2,1,0:T(2,128)(2,1)S(1)}, u32[]{:S(2)}, u32[]{:S(2)}) async-start(bf16[16,2,1792]{2,1,0:T(2,128)(2,1)} %bitcast.15), calls=%async_computation.5 | async-start | bytes 229376 | tf_op jit(solution)/shard_map/all_to_all | solution.py:247
  152.7 0.2 collective-permute-start.6
  152.9 1.0 collective-permute-done.6
  153.9 0.6 fusion.6
  154.5 7.0 %all-to-all-done.5 = bf16[16,2,1792]{2,1,0:T(2,128)(2,1)S(1)} async-done(((bf16[16,2,1792]{2,1,0:T(2,128)(2,1)}), bf16[16,2,1792]{2,1,0:T(2,128)(2,1)S(1)}, u32[]{:S(2)}, u32[]{:S(2)}) %all-to-all-start.5) | async-done | bytes 114720 | tf_op jit(solution)/shard_map/all_to_all | solution.py:247
  161.5 0.7 reduce.3
  (39 shorter events, 0.3 us)
Async XLA Ops:
  0.6 29.7 %collective-permute-start.1 = (bf16[7168,128]{1,0:T(8,128)(2,1)}, bf16[7168,128]{1,0:T(8,128)(2,1)S(1)}, u32[]{:S(2)}, u32[]{:S(2)}) collective-permute-start(bf16[7168,128]{1,0:T(8,128)(2,1)} %g0.1), channel_id=1, source_target_pairs={{0,1},{1,0},{2,3},{3,2},{4,5},{5,4},{6,7},{7,6},{8,9},{9,8},{10,11... | collective-permute-start | bytes 5505032 | tf_op jit(solution)/shard_map/ppermute | solution.py:175
  4.0 26.4 %collective-permute-start.2 = (bf16[7168,128]{1,0:T(8,128)(2,1)}, bf16[7168,128]{1,0:T(8,128)(2,1)}, u32[]{:S(2)}, u32[]{:S(2)}) collective-permute-start(bf16[7168,128]{1,0:T(8,128)(2,1)} %u0.1), channel_id=1, source_target_pairs={{0,1},{1,0},{2,3},{3,2},{4,5},{5,4},{6,7},{7,6},{8,9},{9,8},{10,11... | collective-permute-start | bytes 5505032 | tf_op jit(solution)/shard_map/ppermute | solution.py:176
  4.1 26.3 %collective-permute-start.3 = (bf16[128,7168]{1,0:T(8,128)(2,1)}, bf16[128,7168]{1,0:T(8,128)(2,1)}, u32[]{:S(2)}, u32[]{:S(2)}) collective-permute-start(bf16[128,7168]{1,0:T(8,128)(2,1)} %d0.1), channel_id=1, source_target_pairs={{0,1},{1,0},{2,3},{3,2},{4,5},{5,4},{6,7},{7,6},{8,9},{9,8},{10,11... | collective-permute-start | bytes 5505032 | tf_op jit(solution)/shard_map/ppermute | solution.py:177
  4.5 25.8 %collective-permute-start = (bf16[4096,112]{0,1:T(8,128)(2,1)}, bf16[4096,112]{0,1:T(8,128)(2,1)S(1)}, u32[]{:S(2)}, u32[]{:S(2)}) collective-permute-start(bf16[4096,112]{0,1:T(8,128)(2,1)} %param.27), channel_id=1, source_target_pairs={{0,1},{1,0},{2,3},{3,2},{4,5},{5,4},{6,7},{7,6},{8,9},{9,8},{10,11... | collective-permute-start | bytes 2752520 | tf_op jit(solution)/shard_map/ppermute | solution.py:174
  4.6 1.1 copy-start.5
  5.7 0.9 copy-start.6
  6.6 0.9 copy-start.7
  7.5 0.7 copy-start.8
  8.2 0.7 copy-start.9
  8.9 0.7 copy-start.10
  9.6 0.7 copy-start.11
  10.2 20.1 %copy-start.12 = (s32[2,128,4]{1,2,0:T(4,128)S(1)}, s32[2,128,4]{1,2,0:T(4,128)}, u32[]{:S(2)}) copy-start(s32[2,128,4]{1,2,0:T(4,128)} %param.29) | copy-start | bytes 12292
  10.2 20.1 %copy-start.13 = (f32[2,128,4]{1,2,0:T(4,128)S(1)}, f32[2,128,4]{1,2,0:T(4,128)}, u32[]{:S(2)}) copy-start(f32[2,128,4]{1,2,0:T(4,128)} %param.30) | copy-start | bytes 12292
  10.3 20.1 %copy-start.14 = (s32[64]{0:T(128)S(1)}, s32[64]{0:T(128)}, u32[]{:S(2)}) copy-start(s32[64]{0:T(128)} %counts.1) | copy-start | bytes 772
  15.1 15.2 %all-to-all-start = ((bf16[8,2,4096]{2,1,0:T(2,128)(2,1)}), bf16[8,2,4096]{2,1,0:T(2,128)(2,1)S(1)}, u32[]{:S(2)}, u32[]{:S(2)}) async-start(bf16[8,2,4096]{2,1,0:T(2,128)(2,1)} %bitcast.1), calls=%async_computation | async-start | bytes 262144 | tf_op jit(solution)/shard_map/all_to_all | solution.py:192
  30.3 31.5 %copy-start.3 = (bf16[7168,128]{1,0:T(8,128)(2,1)}, bf16[7168,128]{1,0:T(8,128)(2,1)S(1)}, u32[]{:S(2)}) copy-start(bf16[7168,128]{1,0:T(8,128)(2,1)S(1)} %collective-permute-done.1.g1) | copy-start | bytes 5505028
  31.0 30.9 %copy-start.15 = (bf16[4096,112]{0,1:T(8,128)(2,1)S(1)}, bf16[4096,112]{0,1:T(8,128)(2,1)}, u32[]{:S(2)}) copy-start(bf16[4096,112]{0,1:T(8,128)(2,1)} %param.27) | copy-start | bytes 2752516
  63.5 13.5 %all-to-all-start.2 = ((bf16[8,112,128]{2,1,0:T(8,128)(2,1)}), bf16[8,112,128]{2,1,0:T(8,128)(2,1)S(1)}, u32[]{:S(2)}, u32[]{:S(2)}) async-start(bf16[8,112,128]{2,1,0:T(8,128)(2,1)} %broadcast_in_dim.50), calls=%async_computation.2 | async-start | bytes 458752 | tf_op jit(solution)/shard_map/all_to_all | solution.py:32
  68.1 9.1 %collective-permute-start.4 = (f32[448,128]{1,0:T(8,128)S(1)}, f32[448,128]{1,0:T(8,128)S(1)}, u32[]{:S(2)}, u32[]{:S(2)}) collective-permute-start(f32[448,128]{1,0:T(8,128)S(1)} %get-tuple-element.54), channel_id=1, source_target_pairs={{0,1},{2,3},{4,5},{6,7},{8,9},{10,11},{12,13},{14,15},{16,17},{18,... | collective-permute-start | bytes 688136 | tf_op jit(solution)/shard_map/ppermute | solution.py:210
  78.8 25.4 %all-to-all-start.3 = ((bf16[16,464,128]{2,1,0:T(8,128)(2,1)}), bf16[16,464,128]{2,1,0:T(8,128)(2,1)S(1)}, u32[]{:S(2)}, u32[]{:S(2)}) async-start(bf16[16,464,128]{2,1,0:T(8,128)(2,1)} %broadcast_in_dim.52), calls=%async_computation.3 | async-start | bytes 3801088 | tf_op jit(solution)/shard_map/all_to_all | solution.py:32
  82.6 7.0 %collective-permute-start.5 = (f32[2,128]{1,0:T(2,128)S(1)}, f32[2,128]{1,0:T(2,128)S(1)}, u32[]{:S(2)}, u32[]{:S(2)}) collective-permute-start(f32[2,128]{1,0:T(2,128)S(1)} %get-tuple-element.58), channel_id=1, source_target_pairs={{0,1},{2,3},{4,5},{6,7},{8,9},{10,11},{12,13},{14,15},{16,17},{18,... | collective-permute-start | bytes 3080 | tf_op jit(solution)/shard_map/ppermute | solution.py:211
  104.3 1.5 copy-start
  105.8 1.5 copy-start.1
  107.3 1.5 copy-start.2
  108.8 1.5 copy-start.4
  143.2 18.4 %all-to-all-start.5 = ((bf16[16,2,1792]{2,1,0:T(2,128)(2,1)}), bf16[16,2,1792]{2,1,0:T(2,128)(2,1)S(1)}, u32[]{:S(2)}, u32[]{:S(2)}) async-start(bf16[16,2,1792]{2,1,0:T(2,128)(2,1)} %bitcast.15), calls=%async_computation.5 | async-start | bytes 229376 | tf_op jit(solution)/shard_map/all_to_all | solution.py:247
  152.7 1.2 collective-permute-start.6

commit v5 on v4

--- a/solution.py
+++ b/solution.py
@@ -106,7 +106,6 @@
             pltpu.VMEM((heads, 8, LAT), f32),
             pltpu.SemaphoreType.DMA((7,)),
         ],
-        compiler_params=pltpu.CompilerParams(vmem_limit_bytes=52 * 1024 * 1024),
         cost_estimate=pl.CostEstimate(flops=160_000_000, bytes_accessed=6_000_000, transcendentals=50_000),
     )(place, lengths, counts, *arrays)
 
@@ -190,27 +189,14 @@
     )
     ctx = jnp.broadcast_to(ctx.reshape(1, STEPS, SLOTS, -1), (NH, STEPS, SLOTS, ctx.shape[1]))
     ctx = lax.all_to_all(ctx.reshape(NH * 2, SLOTS, -1), ("h", "c"), 0, 0).reshape(NH, 2, SLOTS, -1)
-    ctx, expert_ids, route_gates, row_counts, norm_gain, out_other, gate_other, up_other, down_other = (
-        lax.optimization_barrier(
-            (ctx, expert_ids, route_gates, row_counts, norm_gain, out_other, gate_other, up_other, down_other)
-        )
+    gain = lax.dynamic_slice_in_dim(norm_gain, column * (D // 16), D // 16, 0)
+    gain = jnp.broadcast_to(gain[:, None], (D // 16, 128))
+    fours = jnp.sum(jnp.where(expert_ids == column, route_gates, 0.0), axis=2)
+    live = (jnp.arange(SLOTS)[None, :] < row_counts[:, None]).astype(f32).reshape(1, 128)
+    weight = lax.dynamic_slice_in_dim(fours, core, 1, 0) * live
+    ctx, gain, weight, out_other, gate_other, up_other, down_other = lax.optimization_barrier(
+        (ctx, gain, weight, out_other, gate_other, up_other, down_other)
     )
-
-    def prepare():
-        gain = lax.dynamic_slice_in_dim(norm_gain, column * (D // 16), D // 16, 0)
-        fours = jnp.sum(jnp.where(expert_ids == column, route_gates, 0.0), axis=2)
-        live = (jnp.arange(SLOTS)[None, :] < row_counts[:, None]).astype(f32).reshape(1, 128)
-        return jnp.broadcast_to(gain[:, None], (D // 16, 128)), fours * live
-
-    def leave():
-        return jnp.zeros((D // 16, 128), f32), jnp.zeros((STEPS, 128), f32)
-
-    gain, weight = lax.cond(core == 0, prepare, leave)
-    ctx, gain, weight = lax.optimization_barrier((ctx, gain, weight))
-    gain = jnp.where(core == 0, gain, lax.ppermute(gain, "c", ((0, 1),)))
-    weight = jnp.where(core == 0, weight, lax.ppermute(weight, "c", ((0, 1),)))
-    weight = lax.dynamic_slice_in_dim(weight, core, 1, 0)
-
     ctx = jnp.where(core == 0, ctx, ctx[:, ::-1])
     ctx = jnp.transpose(ctx, (0, 2, 1, 3)).reshape(8, -1)
     ctx = spread(ctx, XY, NXY).reshape(128, -1)

time: 163 us -> 149 us (0.914)
  blocking collectives: 58.8 us -> 83.7 us
  waiting for transfers between devices: 44 us -> 23.8 us
  local copies, waits for them, and re-layouts: 16 us -> 4.84 us
  starting transfers between devices: 31.6 us -> 23.7 us
    all_to_all x1 -> x2, blocking collectives: 30.9 us -> 58.6 us  [spread(): return lax.all_to_all(copies, axes, 0, 0)]
    all_to_all x2 -> x1, waiting for transfers between devices: 22.3 us -> 8.93 us  [spread(): return lax.all_to_all(copies, axes, 0, 0)]
    unnamed x33 -> x15, local copies, waits for them, and re-layouts: 11.8 us -> 0.12 us
    ppermute x2 -> x0, waiting for transfers between devices: 5.7 us -> none  [the longest x1 5.69 us: body(): weight = jnp.where(core == 0, weight, lax.ppermute(weight, 'c', ((0, 1),)))]
    all_to_all x2 -> x1, starting transfers between devices: 8.2 us -> 3.55 us  [spread(): return lax.all_to_all(copies, axes, 0, 0)]
    all_to_all x1, blocking collectives: 28 us -> 25.1 us  [body(): got = lax.all_to_all(out.reshape(NXY, 8, D), XY, 0, 0)]
    ppermute x2 -> x0, starting transfers between devices: 2.57 us -> none  [the longest x1 1.29 us: body(): weight = jnp.where(core == 0, weight, lax.ppermute(weight, 'c', ((0, 1),)))]
  transfers between devices with their start and end apart: 11 -> 8, of which waited for: 6 -> 4; matrix products, arithmetic and copies ran while one was open for 1% -> 2% of each run, Pallas kernels for 3% -> 3%
where the time goes in v5:
time: 149 us
  blocking collectives  83.7 us (56%)
  waiting for transfers between devices  23.8 us (16%)
  starting transfers between devices  23.7 us (16%)
  Pallas kernels  8.61 us (6%)
  local copies, waits for them, and re-layouts  4.84 us (3%)
  other arithmetic  2.08 us (1%)
    all_to_all x2, blocking collectives, spread(): return lax.all_to_all(copies, axes, 0, 0)  58.6 us
    all_to_all x1, blocking collectives, body(): got = lax.all_to_all(out.reshape(NXY, 8, D), XY, 0, 0)  25.1 us
    all_to_all x1, waiting for transfers between devices, spread(): return lax.all_to_all(copies, axes, 0, 0)  8.93 us
    all_to_all x1, starting transfers between devices, body(): own = lax.all_to_all(sums, ('h', 'l', 'c'), 0, 0)  8.79 us
    all_to_all x1, starting transfers between devices, body(): lax.all_to_all(ctx.reshape(NH * 2, SLOTS, -1), ('h', 'c'), 0, 0)  7.13 us
    all_to_all x1, waiting for transfers between devices, body(): own = lax.all_to_all(sums, ('h', 'l', 'c'), 0, 0)  7.02 us
    all_to_all x1, waiting for transfers between devices, body(): lax.all_to_all(ctx.reshape(NH * 2, SLOTS, -1), ('h', 'c'), 0, 0)  6.97 us
    pallas_call x1, Pallas kernels, attend(): pl.pallas_call(attend_kernel, in_specs=[scalars] * 3 + [far] * 7, out_spe...  4.74 us
  transfers between devices with their start and end apart: 8, of which 4 were waited for; matrix products, arithmetic and copies ran while one was open for 2% of the time, Pallas kernels for 3%

profile of v5, /device:TPU:1, one launch (start us, length us, event | category | flops | bytes accessed | tf_op | source)
XLA Modules:
  0.0 148.6 jit_solution(6497625949282417578)
XLA Ops:
  0.6 3.3 %collective-permute-start.1 = (bf16[7168,128]{1,0:T(8,128)(2,1)}, bf16[7168,128]{1,0:T(8,128)(2,1)S(1)}, u32[]{:S(2)}, u32[]{:S(2)}) collective-permute-start(bf16[7168,128]{1,0:T(8,128)(2,1)} %g0.1), channel_id=1, source_target_pairs={{0,1},{1,0},{2,3},{3,2},{4,5},{5,4},{6,7},{7,6},{8,9},{9,8},{10,11... | collective-permute-start | bytes 5505032 | tf_op jit(solution)/shard_map/ppermute | solution.py:174
  4.0 0.1 collective-permute-start.2
  4.1 0.4 collective-permute-start.3
  4.5 0.1 collective-permute-start
  4.6 4.7 %shard_map.167 = bf16[4,4096]{1,0:T(4,128)(2,1)} custom-call(s32[1]{0:T(128)} %bitcast.place, s32[2]{0:T(128)} %lengths.1, s32[64]{0:T(128)} %counts.1, bf16[2,2,16384]{2,1,0:T(2,128)(2,1)} %ql_hbm.1, bf16[2,2,2048]{2,1,0:T(2,128)(2,1)} %qr_hbm.1, bf16[2,384,512]{2,1,0:T(8,128)(2,1)} %cl_hbm.1, bf16[2,64,384]{2,1,0:T(8,128)(2,1)} %cr_hbm.1, ...), custom_call_target="tpu_custom_call" | custom-call | flops 160000000 | bytes 6000000 | tf_op jit(solution)/shard_map/pallas_call | solution.py:97
  9.3 0.8 broadcast_in_dim.23
  10.1 0.7 broadcast_in_dim.24
  10.8 7.1 %all-to-all-start = ((bf16[8,2,4096]{2,1,0:T(2,128)(2,1)}), bf16[8,2,4096]{2,1,0:T(2,128)(2,1)S(1)}, u32[]{:S(2)}, u32[]{:S(2)}) async-start(bf16[8,2,4096]{2,1,0:T(2,128)(2,1)} %bitcast.1), calls=%async_computation | async-start | bytes 262144 | tf_op jit(solution)/shard_map/all_to_all | solution.py:191
  18.0 0.0 copy-done.5
  18.0 0.1 iota_compare_fusion
  18.1 0.1 lt.37
  18.2 0.8 dynamic_slice.10
  19.0 7.0 %all-to-all-done = bf16[8,2,4096]{2,1,0:T(2,128)(2,1)S(1)} async-done(((bf16[8,2,4096]{2,1,0:T(2,128)(2,1)}), bf16[8,2,4096]{2,1,0:T(2,128)(2,1)S(1)}, u32[]{:S(2)}, u32[]{:S(2)}) %all-to-all-start) | async-done | bytes 131104 | tf_op jit(solution)/shard_map/all_to_all | solution.py:191
  26.0 0.0 collective-permute-done
  26.0 0.0 collective-permute-done.1.g1
  26.0 0.0 collective-permute-done.2.u1
  26.0 0.0 collective-permute-done.3.d1
  26.0 0.1 broadcast_in_dim.48
  26.2 0.1 fusion.4
  26.3 0.1 copy.20
  26.4 0.1 copy.22
  26.5 0.2 broadcast_in_dim.51
  26.7 0.0 copy-start.6
  26.7 32.8 %all_to_all.30 = bf16[16,8,8192]{2,1,0:T(8,128)(2,1)S(1)} all-to-all(bf16[16,8,8192]{2,1,0:T(8,128)(2,1)S(1)} %broadcast_in_dim.51), channel_id=1, replica_groups=mesh['x'=4,'y'=4,'h'=4,'l'=2,'c'=2] {'x','y'}, dimensions={0} | all-to-all | bytes 4194304 | tf_op jit(solution)/shard_map/all_to_all | solution.py:32
  59.5 0.4 convolution_bitcast_fusion
  60.0 0.5 fusion
  60.5 0.7 broadcast_in_dim.52
  61.2 3.6 %all-to-all-start.2 = ((bf16[8,112,128]{2,1,0:T(8,128)(2,1)}), bf16[8,112,128]{2,1,0:T(8,128)(2,1)S(1)}, u32[]{:S(2)}, u32[]{:S(2)}) async-start(bf16[8,112,128]{2,1,0:T(8,128)(2,1)} %broadcast_in_dim.52), calls=%async_computation.2 | async-start | bytes 458752 | tf_op jit(solution)/shard_map/all_to_all | solution.py:32
  64.7 0.1 pad.7.clone
  64.8 8.9 %all-to-all-done.2 = bf16[8,112,128]{2,1,0:T(8,128)(2,1)S(1)} async-done(((bf16[8,112,128]{2,1,0:T(8,128)(2,1)}), bf16[8,112,128]{2,1,0:T(8,128)(2,1)S(1)}, u32[]{:S(2)}, u32[]{:S(2)}) %all-to-all-start.2) | async-done | bytes 229408 | tf_op jit(solution)/shard_map/all_to_all | solution.py:32
  73.8 0.1 multiply_reduce_fusion
  73.9 0.1 maximum_maximum_fusion
  74.1 0.0 copy-start.2
  74.1 0.2 broadcast_in_dim.54
  74.3 0.0 copy-start
  74.3 0.0 copy-start.1
  74.3 25.8 %all_to_all.31.rows = bf16[16,464,128]{2,1,0:T(8,128)(2,1)S(1)} all-to-all(bf16[16,464,128]{2,1,0:T(8,128)(2,1)S(1)} %broadcast_in_dim.54), channel_id=1, replica_groups=mesh['x'=4,'y'=4,'h'=4,'l'=2,'c'=2] {'x','y'}, dimensions={0} | all-to-all | bytes 3801088 | tf_op jit(solution)/shard_map/all_to_all | solution.py:32
  100.2 3.9 %shard_map.168 = bf16[128,7168]{1,0:T(8,128)(2,1)S(1)} custom-call(bf16[16,464,128]{2,1,0:T(8,128)(2,1)S(1)} %all_to_all.31.rows, f32[1,128]{1,0:T(1,128)S(1)} %dynamic-slice_select_fusion.weight, bf16[7168,128]{1,0:T(8,128)(2,1)S(1)} %copy-done, bf16[7168,128]{1,0:T(8,128)(2,1)S(1)} %collective-permute-done.1.g1, bf16[7168,128]{1,0:T(8,128)(2,1)S(1)} %copy-done.1, ...), custom_call_target="tpu_custom_call" | custom-call | flops 705000000 | bytes 15000000 | tf_op jit(solution)/shard_map/pallas_call | solution.py:142
  104.0 25.1 %all_to_all.32 = bf16[16,8,7168]{2,1,0:T(8,128)(2,1)S(1)} all-to-all(bf16[16,8,7168]{2,1,0:T(8,128)(2,1)S(1)} %bitcast.36), channel_id=1, replica_groups=mesh['x'=4,'y'=4,'h'=4,'l'=2,'c'=2] {'x','y'}, dimensions={0} | all-to-all | bytes 3670016 | tf_op jit(solution)/shard_map/all_to_all | solution.py:224
  129.1 0.3 reduce_sum.57
  129.4 0.1 reshape.94
  129.5 0.7 copy.21
  130.2 8.8 %all-to-all-start.5 = ((bf16[16,2,1792]{2,1,0:T(2,128)(2,1)}), bf16[16,2,1792]{2,1,0:T(2,128)(2,1)S(1)}, u32[]{:S(2)}, u32[]{:S(2)}) async-start(bf16[16,2,1792]{2,1,0:T(2,128)(2,1)} %bitcast.15), calls=%async_computation.5 | async-start | bytes 229376 | tf_op jit(solution)/shard_map/all_to_all | solution.py:233
  139.0 0.3 collective-permute-start.4
  139.3 0.9 collective-permute-done.4
  140.2 0.6 fusion.5
  140.8 7.0 %all-to-all-done.5 = bf16[16,2,1792]{2,1,0:T(2,128)(2,1)S(1)} async-done(((bf16[16,2,1792]{2,1,0:T(2,128)(2,1)}), bf16[16,2,1792]{2,1,0:T(2,128)(2,1)S(1)}, u32[]{:S(2)}, u32[]{:S(2)}) %all-to-all-start.5) | async-done | bytes 114720 | tf_op jit(solution)/shard_map/all_to_all | solution.py:233
  147.8 0.7 reduce.3
  (17 shorter events, 0.1 us)
Async XLA Ops:
  0.6 25.4 %collective-permute-start.1 = (bf16[7168,128]{1,0:T(8,128)(2,1)}, bf16[7168,128]{1,0:T(8,128)(2,1)S(1)}, u32[]{:S(2)}, u32[]{:S(2)}) collective-permute-start(bf16[7168,128]{1,0:T(8,128)(2,1)} %g0.1), channel_id=1, source_target_pairs={{0,1},{1,0},{2,3},{3,2},{4,5},{5,4},{6,7},{7,6},{8,9},{9,8},{10,11... | collective-permute-start | bytes 5505032 | tf_op jit(solution)/shard_map/ppermute | solution.py:174
  4.0 22.1 %collective-permute-start.2 = (bf16[7168,128]{1,0:T(8,128)(2,1)}, bf16[7168,128]{1,0:T(8,128)(2,1)}, u32[]{:S(2)}, u32[]{:S(2)}) collective-permute-start(bf16[7168,128]{1,0:T(8,128)(2,1)} %u0.1), channel_id=1, source_target_pairs={{0,1},{1,0},{2,3},{3,2},{4,5},{5,4},{6,7},{7,6},{8,9},{9,8},{10,11... | collective-permute-start | bytes 5505032 | tf_op jit(solution)/shard_map/ppermute | solution.py:175
  4.1 22.0 %collective-permute-start.3 = (bf16[128,7168]{1,0:T(8,128)(2,1)}, bf16[128,7168]{1,0:T(8,128)(2,1)}, u32[]{:S(2)}, u32[]{:S(2)}) collective-permute-start(bf16[128,7168]{1,0:T(8,128)(2,1)} %d0.1), channel_id=1, source_target_pairs={{0,1},{1,0},{2,3},{3,2},{4,5},{5,4},{6,7},{7,6},{8,9},{9,8},{10,11... | collective-permute-start | bytes 5505032 | tf_op jit(solution)/shard_map/ppermute | solution.py:176
  4.5 21.5 %collective-permute-start = (bf16[4096,112]{0,1:T(8,128)(2,1)}, bf16[4096,112]{0,1:T(8,128)(2,1)S(1)}, u32[]{:S(2)}, u32[]{:S(2)}) collective-permute-start(bf16[4096,112]{0,1:T(8,128)(2,1)} %param.25), channel_id=1, source_target_pairs={{0,1},{1,0},{2,3},{3,2},{4,5},{5,4},{6,7},{7,6},{8,9},{9,8},{10,11... | collective-permute-start | bytes 2752520 | tf_op jit(solution)/shard_map/ppermute | solution.py:173
  4.6 13.4 %copy-start.5 = (s32[64]{0:T(128)S(1)}, s32[64]{0:T(128)}, u32[]{:S(2)}) copy-start(s32[64]{0:T(128)} %counts.1) | copy-start | bytes 772
  4.6 13.5 %copy-start.3 = (f32[2,128,4]{1,2,0:T(4,128)S(1)}, f32[2,128,4]{1,2,0:T(4,128)}, u32[]{:S(2)}) copy-start(f32[2,128,4]{1,2,0:T(4,128)} %param.28) | copy-start | bytes 12292
  4.6 13.5 %copy-start.4 = (s32[2,128,4]{1,2,0:T(4,128)S(1)}, s32[2,128,4]{1,2,0:T(4,128)}, u32[]{:S(2)}) copy-start(s32[2,128,4]{1,2,0:T(4,128)} %param.27) | copy-start | bytes 12292
  10.8 15.2 %all-to-all-start = ((bf16[8,2,4096]{2,1,0:T(2,128)(2,1)}), bf16[8,2,4096]{2,1,0:T(2,128)(2,1)S(1)}, u32[]{:S(2)}, u32[]{:S(2)}) async-start(bf16[8,2,4096]{2,1,0:T(2,128)(2,1)} %bitcast.1), calls=%async_computation | async-start | bytes 262144 | tf_op jit(solution)/shard_map/all_to_all | solution.py:191
  26.7 32.8 %copy-start.6 = (bf16[4096,112]{0,1:T(8,128)(2,1)S(1)}, bf16[4096,112]{0,1:T(8,128)(2,1)}, u32[]{:S(2)}) copy-start(bf16[4096,112]{0,1:T(8,128)(2,1)} %param.25) | copy-start | bytes 2752516
  61.2 12.6 %all-to-all-start.2 = ((bf16[8,112,128]{2,1,0:T(8,128)(2,1)}), bf16[8,112,128]{2,1,0:T(8,128)(2,1)S(1)}, u32[]{:S(2)}, u32[]{:S(2)}) async-start(bf16[8,112,128]{2,1,0:T(8,128)(2,1)} %broadcast_in_dim.52), calls=%async_computation.2 | async-start | bytes 458752 | tf_op jit(solution)/shard_map/all_to_all | solution.py:32
  74.1 26.1 %copy-start.2 = (bf16[128,7168]{1,0:T(8,128)(2,1)S(1)}, bf16[128,7168]{1,0:T(8,128)(2,1)}, u32[]{:S(2)}) copy-start(bf16[128,7168]{1,0:T(8,128)(2,1)} %d0.1) | copy-start | bytes 5505028
  74.3 25.8 %copy-start = (bf16[7168,128]{1,0:T(8,128)(2,1)S(1)}, bf16[7168,128]{1,0:T(8,128)(2,1)}, u32[]{:S(2)}) copy-start(bf16[7168,128]{1,0:T(8,128)(2,1)} %g0.1) | copy-start | bytes 5505028
  74.3 25.8 %copy-start.1 = (bf16[7168,128]{1,0:T(8,128)(2,1)S(1)}, bf16[7168,128]{1,0:T(8,128)(2,1)}, u32[]{:S(2)}) copy-start(bf16[7168,128]{1,0:T(8,128)(2,1)} %u0.1) | copy-start | bytes 5505028
  130.2 17.6 %all-to-all-start.5 = ((bf16[16,2,1792]{2,1,0:T(2,128)(2,1)}), bf16[16,2,1792]{2,1,0:T(2,128)(2,1)S(1)}, u32[]{:S(2)}, u32[]{:S(2)}) async-start(bf16[16,2,1792]{2,1,0:T(2,128)(2,1)} %bitcast.15), calls=%async_computation.5 | async-start | bytes 229376 | tf_op jit(solution)/shard_map/all_to_all | solution.py:233
  139.0 1.2 collective-permute-start.4

commit v6 on v5

--- a/solution.py
+++ b/solution.py
@@ -87,7 +87,10 @@
     live = slot < counts[place[0]]
     for h in range(heads):
         ctx = jnp.dot(lat[h].astype(bf16), v[h], preferred_element_type=f32)
-        out[:, h * HD : (h + 1) * HD] = jnp.where(live, ctx[: STEPS * SLOTS], 0.0).astype(bf16)
+        ctx = jnp.where(live, ctx[: STEPS * SLOTS], 0.0).astype(bf16)
+        for to in range(NH):
+            for s in range(STEPS):
+                out[to * 2 + s, :, h * HD : (h + 1) * HD] = ctx[s * SLOTS : (s + 1) * SLOTS]
 
 
 def attend(place, lengths, counts, *arrays):
@@ -98,7 +101,7 @@
         attend_kernel,
         in_specs=[scalars] * 3 + [far] * 7,
         out_specs=pl.BlockSpec(memory_space=pltpu.VMEM),
-        out_shape=jax.ShapeDtypeStruct((STEPS * SLOTS, heads * HD), bf16),
+        out_shape=jax.ShapeDtypeStruct((NH * 2, SLOTS, heads * HD), bf16),
         scratch_shapes=[pltpu.VMEM(a.shape, bf16) for a in arrays]
         + [
             pltpu.VMEM((SLOTS, STEPS * heads, LAT), f32),
@@ -187,8 +190,7 @@
         new_rope,
         value_up,
     )
-    ctx = jnp.broadcast_to(ctx.reshape(1, STEPS, SLOTS, -1), (NH, STEPS, SLOTS, ctx.shape[1]))
-    ctx = lax.all_to_all(ctx.reshape(NH * 2, SLOTS, -1), ("h", "c"), 0, 0).reshape(NH, 2, SLOTS, -1)
+    ctx = lax.all_to_all(ctx, ("h", "c"), 0, 0).reshape(NH, 2, SLOTS, -1)
     gain = lax.dynamic_slice_in_dim(norm_gain, column * (D // 16), D // 16, 0)
     gain = jnp.broadcast_to(gain[:, None], (D // 16, 128))
     fours = jnp.sum(jnp.where(expert_ids == column, route_gates, 0.0), axis=2)
@@ -197,13 +199,13 @@
     ctx, gain, weight, out_other, gate_other, up_other, down_other = lax.optimization_barrier(
         (ctx, gain, weight, out_other, gate_other, up_other, down_other)
     )
-    ctx = jnp.where(core == 0, ctx, ctx[:, ::-1])
+    ctx = lax.cond(core == 0, lambda v: jnp.stack([v[:, 1], v[:, 0]], axis=1), lambda v: v, ctx)
     ctx = jnp.transpose(ctx, (0, 2, 1, 3)).reshape(8, -1)
     ctx = spread(ctx, XY, NXY).reshape(128, -1)
 
     half = ctx.shape[1] // 2
-    part = jnp.dot(ctx[:, :half], out_proj, preferred_element_type=f32)
-    part = part + jnp.dot(ctx[:, half:], out_other, preferred_element_type=f32)
+    part = jnp.dot(ctx[:, :half], out_other, preferred_element_type=f32)
+    part = part + jnp.dot(ctx[:, half:], out_proj, preferred_element_type=f32)
     chip = part.T.astype(bf16)
     pieces = spread(chip, Z, NZ).reshape(NH, 2, D // 64, 128).astype(f32)
     hid = jnp.sum(pieces, axis=1).astype(bf16)

time: 149 us -> 146 us (0.980)
  blocking collectives: 83.7 us -> 80.9 us
  local copies, waits for them, and re-layouts: 4.84 us -> 3.33 us
    all_to_all x1, blocking collectives: 25.1 us -> 23.4 us  [body(): got = lax.all_to_all(out.reshape(NXY, 8, D), XY, 0, 0)]
    broadcast_in_dim x2 -> x0, local copies, waits for them, and re-layouts: 1.52 us -> none  [body(): jnp.broadcast_to(ctx.reshape(1, STEPS, SLOTS, -1), (NH, STEPS, SLOTS, ctx...]
  transfers between devices with their start and end apart: 8 -> 8, of which waited for: 4 -> 4; matrix products, arithmetic and copies ran while one was open for 2% -> 1% of each run, Pallas kernels for 3% -> 3%
where the time goes in v6:
time: 146 us; the launch traced here: 145 us
  blocking collectives  80.9 us (55%)
  starting transfers between devices  25 us (17%)
  waiting for transfers between devices  23.7 us (16%)
  Pallas kernels  8.65 us (6%)
  local copies, waits for them, and re-layouts  3.33 us (2%)
  other arithmetic  1.96 us (1%)
    all_to_all x2, blocking collectives, spread(): return lax.all_to_all(copies, axes, 0, 0)  57.5 us
    all_to_all x1, blocking collectives, body(): got = lax.all_to_all(out.reshape(NXY, 8, D), XY, 0, 0)  23.4 us
    all_to_all x1, starting transfers between devices, body(): own = lax.all_to_all(sums, ('h', 'l', 'c'), 0, 0)  10.2 us
    all_to_all x1, waiting for transfers between devices, spread(): return lax.all_to_all(copies, axes, 0, 0)  8.84 us
    all_to_all x1, starting transfers between devices, body(): ctx = lax.all_to_all(ctx, ('h', 'c'), 0, 0).reshape(NH, 2, SLOTS, -1)  7.15 us
    all_to_all x1, waiting for transfers between devices, body(): own = lax.all_to_all(sums, ('h', 'l', 'c'), 0, 0)  7.02 us
    all_to_all x1, waiting for transfers between devices, body(): ctx = lax.all_to_all(ctx, ('h', 'c'), 0, 0).reshape(NH, 2, SLOTS, -1)  6.97 us
    pallas_call x1, Pallas kernels, attend(): pl.pallas_call(attend_kernel, in_specs=[scalars] * 3 + [far] * 7, out_spe...  4.78 us
  transfers between devices with their start and end apart: 8, of which 4 were waited for; matrix products, arithmetic and copies ran while one was open for 1% of the time, Pallas kernels for 3%

profile of v6, /device:TPU:1, one launch (start us, length us, event | category | flops | bytes accessed | tf_op | source)
XLA Modules:
  0.0 145.4 jit_solution(12276903854363952823)
XLA Ops:
  0.6 3.3 %collective-permute-start.1 = (bf16[7168,128]{1,0:T(8,128)(2,1)}, bf16[7168,128]{1,0:T(8,128)(2,1)S(1)}, u32[]{:S(2)}, u32[]{:S(2)}) collective-permute-start(bf16[7168,128]{1,0:T(8,128)(2,1)} %g0.1), channel_id=1, source_target_pairs={{0,1},{1,0},{2,3},{3,2},{4,5},{5,4},{6,7},{7,6},{8,9},{9,8},{10,11... | collective-permute-start | bytes 5505032 | tf_op jit(solution)/shard_map/ppermute | solution.py:177
  4.0 0.1 collective-permute-start.2
  4.1 0.4 collective-permute-start.3
  4.5 0.1 collective-permute-start
  4.6 4.8 %shard_map.167 = bf16[8,2,4096]{2,1,0:T(2,128)(2,1)} custom-call(s32[1]{0:T(128)} %bitcast.place, s32[2]{0:T(128)} %lengths.1, s32[64]{0:T(128)} %counts.1, bf16[2,2,16384]{2,1,0:T(2,128)(2,1)} %ql_hbm.1, bf16[2,2,2048]{2,1,0:T(2,128)(2,1)} %qr_hbm.1, bf16[2,384,512]{2,1,0:T(8,128)(2,1)} %cl_hbm.1, bf16[2,64,384]{2,1,0:T(8,128)(2,1)} %cr_hbm.1, ...), custom_call_target="tpu_custom_call" | custom-call | flops 160000000 | bytes 6000000 | tf_op jit(solution)/shard_map/pallas_call | solution.py:100
  9.4 7.1 %all-to-all-start = ((bf16[8,2,4096]{2,1,0:T(2,128)(2,1)}), bf16[8,2,4096]{2,1,0:T(2,128)(2,1)S(1)}, u32[]{:S(2)}, u32[]{:S(2)}) async-start(bf16[8,2,4096]{2,1,0:T(2,128)(2,1)} %shard_map.167), calls=%async_computation | async-start | bytes 262144 | tf_op jit(solution)/shard_map/all_to_all | solution.py:193
  16.5 0.0 copy-done.5
  16.5 0.1 iota_compare_fusion
  16.6 0.0 copy-done.3
  16.6 0.0 copy-done.4
  16.6 0.1 lt.37
  16.8 0.8 dynamic_slice.10
  17.6 7.0 %all-to-all-done = bf16[8,2,4096]{2,1,0:T(2,128)(2,1)S(1)} async-done(((bf16[8,2,4096]{2,1,0:T(2,128)(2,1)}), bf16[8,2,4096]{2,1,0:T(2,128)(2,1)S(1)}, u32[]{:S(2)}, u32[]{:S(2)}) %all-to-all-start) | async-done | bytes 131104 | tf_op jit(solution)/shard_map/all_to_all | solution.py:193
  24.5 0.0 collective-permute-done
  24.5 0.0 collective-permute-done.1.g1
  24.5 0.0 collective-permute-done.2.u1
  24.6 0.0 collective-permute-done.3.d1
  24.6 0.1 broadcast_in_dim.19
  24.7 0.1 copy.21
  24.9 0.1 copy.23
  24.9 0.2 broadcast_in_dim.42
  25.1 0.0 copy-start.6
  25.2 32.8 %all_to_all.30 = bf16[16,8,8192]{2,1,0:T(8,128)(2,1)S(1)} all-to-all(bf16[16,8,8192]{2,1,0:T(8,128)(2,1)S(1)} %broadcast_in_dim.42), channel_id=1, replica_groups=mesh['x'=4,'y'=4,'h'=4,'l'=2,'c'=2] {'x','y'}, dimensions={0} | all-to-all | bytes 4194304 | tf_op jit(solution)/shard_map/all_to_all | solution.py:32
  57.9 0.0 copy-done.6
  57.9 0.4 convolution_bitcast_fusion
  58.4 0.5 fusion
  58.9 0.7 broadcast_in_dim.43
  59.6 3.4 %all-to-all-start.2 = ((bf16[8,112,128]{2,1,0:T(8,128)(2,1)}), bf16[8,112,128]{2,1,0:T(8,128)(2,1)S(1)}, u32[]{:S(2)}, u32[]{:S(2)}) async-start(bf16[8,112,128]{2,1,0:T(8,128)(2,1)} %broadcast_in_dim.43), calls=%async_computation.2 | async-start | bytes 458752 | tf_op jit(solution)/shard_map/all_to_all | solution.py:32
  63.0 0.1 pad.9.clone
  63.1 8.8 %all-to-all-done.2 = bf16[8,112,128]{2,1,0:T(8,128)(2,1)S(1)} async-done(((bf16[8,112,128]{2,1,0:T(8,128)(2,1)}), bf16[8,112,128]{2,1,0:T(8,128)(2,1)S(1)}, u32[]{:S(2)}, u32[]{:S(2)}) %all-to-all-start.2) | async-done | bytes 229408 | tf_op jit(solution)/shard_map/all_to_all | solution.py:32
  72.0 0.1 multiply_reduce_fusion
  72.1 0.1 maximum_maximum_fusion
  72.2 0.0 copy-start.2
  72.3 0.2 broadcast_in_dim.45
  72.5 0.0 copy-start
  72.5 0.0 copy-start.1
  72.5 24.8 %all_to_all.31.rows = bf16[16,464,128]{2,1,0:T(8,128)(2,1)S(1)} all-to-all(bf16[16,464,128]{2,1,0:T(8,128)(2,1)S(1)} %broadcast_in_dim.45), channel_id=1, replica_groups=mesh['x'=4,'y'=4,'h'=4,'l'=2,'c'=2] {'x','y'}, dimensions={0} | all-to-all | bytes 3801088 | tf_op jit(solution)/shard_map/all_to_all | solution.py:32
  97.3 3.9 %shard_map.168 = bf16[128,7168]{1,0:T(8,128)(2,1)S(1)} custom-call(bf16[16,464,128]{2,1,0:T(8,128)(2,1)S(1)} %all_to_all.31.rows, f32[1,128]{1,0:T(1,128)S(1)} %dynamic-slice_select_fusion.weight, bf16[7168,128]{1,0:T(8,128)(2,1)S(1)} %copy-done, bf16[7168,128]{1,0:T(8,128)(2,1)S(1)} %collective-permute-done.1.g1, bf16[7168,128]{1,0:T(8,128)(2,1)S(1)} %copy-done.1, ...), custom_call_target="tpu_custom_call" | custom-call | flops 705000000 | bytes 15000000 | tf_op jit(solution)/shard_map/pallas_call | solution.py:145
  101.2 23.4 %all_to_all.32 = bf16[16,8,7168]{2,1,0:T(8,128)(2,1)S(1)} all-to-all(bf16[16,8,7168]{2,1,0:T(8,128)(2,1)S(1)} %bitcast.34), channel_id=1, replica_groups=mesh['x'=4,'y'=4,'h'=4,'l'=2,'c'=2] {'x','y'}, dimensions={0} | all-to-all | bytes 3670016 | tf_op jit(solution)/shard_map/all_to_all | solution.py:226
  124.6 0.3 reduce_sum.57
  124.8 0.1 reshape.88
  124.9 0.7 copy.22
  125.6 10.2 %all-to-all-start.5 = ((bf16[16,2,1792]{2,1,0:T(2,128)(2,1)}), bf16[16,2,1792]{2,1,0:T(2,128)(2,1)S(1)}, u32[]{:S(2)}, u32[]{:S(2)}) async-start(bf16[16,2,1792]{2,1,0:T(2,128)(2,1)} %bitcast.14), calls=%async_computation.5 | async-start | bytes 229376 | tf_op jit(solution)/shard_map/all_to_all | solution.py:235
  135.8 0.3 collective-permute-start.4
  136.1 0.9 collective-permute-done.4
  137.0 0.6 fusion.4
  137.6 7.0 %all-to-all-done.5 = bf16[16,2,1792]{2,1,0:T(2,128)(2,1)S(1)} async-done(((bf16[16,2,1792]{2,1,0:T(2,128)(2,1)}), bf16[16,2,1792]{2,1,0:T(2,128)(2,1)S(1)}, u32[]{:S(2)}, u32[]{:S(2)}) %all-to-all-start.5) | async-done | bytes 114720 | tf_op jit(solution)/shard_map/all_to_all | solution.py:235
  144.7 0.7 reduce.3
  (15 shorter events, 0.1 us)
Async XLA Ops:
  0.6 23.9 %collective-permute-start.1 = (bf16[7168,128]{1,0:T(8,128)(2,1)}, bf16[7168,128]{1,0:T(8,128)(2,1)S(1)}, u32[]{:S(2)}, u32[]{:S(2)}) collective-permute-start(bf16[7168,128]{1,0:T(8,128)(2,1)} %g0.1), channel_id=1, source_target_pairs={{0,1},{1,0},{2,3},{3,2},{4,5},{5,4},{6,7},{7,6},{8,9},{9,8},{10,11... | collective-permute-start | bytes 5505032 | tf_op jit(solution)/shard_map/ppermute | solution.py:177
  4.0 20.6 %collective-permute-start.2 = (bf16[7168,128]{1,0:T(8,128)(2,1)}, bf16[7168,128]{1,0:T(8,128)(2,1)}, u32[]{:S(2)}, u32[]{:S(2)}) collective-permute-start(bf16[7168,128]{1,0:T(8,128)(2,1)} %u0.1), channel_id=1, source_target_pairs={{0,1},{1,0},{2,3},{3,2},{4,5},{5,4},{6,7},{7,6},{8,9},{9,8},{10,11... | collective-permute-start | bytes 5505032 | tf_op jit(solution)/shard_map/ppermute | solution.py:178
  4.1 20.5 %collective-permute-start.3 = (bf16[128,7168]{1,0:T(8,128)(2,1)}, bf16[128,7168]{1,0:T(8,128)(2,1)}, u32[]{:S(2)}, u32[]{:S(2)}) collective-permute-start(bf16[128,7168]{1,0:T(8,128)(2,1)} %d0.1), channel_id=1, source_target_pairs={{0,1},{1,0},{2,3},{3,2},{4,5},{5,4},{6,7},{7,6},{8,9},{9,8},{10,11... | collective-permute-start | bytes 5505032 | tf_op jit(solution)/shard_map/ppermute | solution.py:179
  4.5 20.1 %collective-permute-start = (bf16[4096,112]{0,1:T(8,128)(2,1)}, bf16[4096,112]{0,1:T(8,128)(2,1)S(1)}, u32[]{:S(2)}, u32[]{:S(2)}) collective-permute-start(bf16[4096,112]{0,1:T(8,128)(2,1)} %param.27), channel_id=1, source_target_pairs={{0,1},{1,0},{2,3},{3,2},{4,5},{5,4},{6,7},{7,6},{8,9},{9,8},{10,11... | collective-permute-start | bytes 2752520 | tf_op jit(solution)/shard_map/ppermute | solution.py:176
  4.6 11.9 %copy-start.5 = (s32[64]{0:T(128)S(1)}, s32[64]{0:T(128)}, u32[]{:S(2)}) copy-start(s32[64]{0:T(128)} %counts.1) | copy-start | bytes 772
  4.6 12.0 %copy-start.3 = (f32[2,128,4]{1,2,0:T(4,128)S(1)}, f32[2,128,4]{1,2,0:T(4,128)}, u32[]{:S(2)}) copy-start(f32[2,128,4]{1,2,0:T(4,128)} %param.30) | copy-start | bytes 12292
  4.6 12.0 %copy-start.4 = (s32[2,128,4]{1,2,0:T(4,128)S(1)}, s32[2,128,4]{1,2,0:T(4,128)}, u32[]{:S(2)}) copy-start(s32[2,128,4]{1,2,0:T(4,128)} %param.29) | copy-start | bytes 12292
  9.4 15.2 %all-to-all-start = ((bf16[8,2,4096]{2,1,0:T(2,128)(2,1)}), bf16[8,2,4096]{2,1,0:T(2,128)(2,1)S(1)}, u32[]{:S(2)}, u32[]{:S(2)}) async-start(bf16[8,2,4096]{2,1,0:T(2,128)(2,1)} %shard_map.167), calls=%async_computation | async-start | bytes 262144 | tf_op jit(solution)/shard_map/all_to_all | solution.py:193
  25.1 32.8 %copy-start.6 = (bf16[4096,112]{0,1:T(8,128)(2,1)S(1)}, bf16[4096,112]{0,1:T(8,128)(2,1)}, u32[]{:S(2)}) copy-start(bf16[4096,112]{0,1:T(8,128)(2,1)} %param.27) | copy-start | bytes 2752516
  59.6 12.3 %all-to-all-start.2 = ((bf16[8,112,128]{2,1,0:T(8,128)(2,1)}), bf16[8,112,128]{2,1,0:T(8,128)(2,1)S(1)}, u32[]{:S(2)}, u32[]{:S(2)}) async-start(bf16[8,112,128]{2,1,0:T(8,128)(2,1)} %broadcast_in_dim.43), calls=%async_computation.2 | async-start | bytes 458752 | tf_op jit(solution)/shard_map/all_to_all | solution.py:32
  72.2 25.1 %copy-start.2 = (bf16[128,7168]{1,0:T(8,128)(2,1)S(1)}, bf16[128,7168]{1,0:T(8,128)(2,1)}, u32[]{:S(2)}) copy-start(bf16[128,7168]{1,0:T(8,128)(2,1)} %d0.1) | copy-start | bytes 5505028
  72.5 24.8 %copy-start = (bf16[7168,128]{1,0:T(8,128)(2,1)S(1)}, bf16[7168,128]{1,0:T(8,128)(2,1)}, u32[]{:S(2)}) copy-start(bf16[7168,128]{1,0:T(8,128)(2,1)} %g0.1) | copy-start | bytes 5505028
  72.5 24.8 %copy-start.1 = (bf16[7168,128]{1,0:T(8,128)(2,1)S(1)}, bf16[7168,128]{1,0:T(8,128)(2,1)}, u32[]{:S(2)}) copy-start(bf16[7168,128]{1,0:T(8,128)(2,1)} %u0.1) | copy-start | bytes 5505028
  125.6 19.0 %all-to-all-start.5 = ((bf16[16,2,1792]{2,1,0:T(2,128)(2,1)}), bf16[16,2,1792]{2,1,0:T(2,128)(2,1)S(1)}, u32[]{:S(2)}, u32[]{:S(2)}) async-start(bf16[16,2,1792]{2,1,0:T(2,128)(2,1)} %bitcast.14), calls=%async_computation.5 | async-start | bytes 229376 | tf_op jit(solution)/shard_map/all_to_all | solution.py:235
  135.8 1.2 collective-permute-start.4

commit v7 on v6

--- a/solution.py
+++ b/solution.py
@@ -152,6 +152,32 @@
     )(rows, weight, *weights)
 
 
+def stage_kernel(a, b, to_a, to_b, sems):
+    copies = [pltpu.make_async_copy(a, to_a, sems.at[0]), pltpu.make_async_copy(b, to_b, sems.at[1])]
+    for copy in copies:
+        copy.start()
+    for copy in copies:
+        copy.wait()
+
+
+def stage(*arrays):
+    return pl.pallas_call(
+        stage_kernel,
+        in_specs=[pl.BlockSpec(memory_space=pl.ANY)] * 2,
+        out_specs=[pl.BlockSpec(memory_space=pltpu.VMEM)] * 2,
+        out_shape=[jax.ShapeDtypeStruct(a.shape, a.dtype) for a in arrays],
+        scratch_shapes=[pltpu.SemaphoreType.DMA((2,))],
+    )(*arrays)
+
+
+def unwritten(*arrays):
+    return pl.pallas_call(
+        lambda *outs: None,
+        out_specs=[pl.BlockSpec(memory_space=pltpu.VMEM)] * 2,
+        out_shape=[jax.ShapeDtypeStruct(a.shape, a.dtype) for a in arrays],
+    )()
+
+
 def body(
     query_latent,
     query_rope,
@@ -191,17 +217,29 @@
         value_up,
     )
     ctx = lax.all_to_all(ctx, ("h", "c"), 0, 0).reshape(NH, 2, SLOTS, -1)
-    gain = lax.dynamic_slice_in_dim(norm_gain, column * (D // 16), D // 16, 0)
-    gain = jnp.broadcast_to(gain[:, None], (D // 16, 128))
-    fours = jnp.sum(jnp.where(expert_ids == column, route_gates, 0.0), axis=2)
-    live = (jnp.arange(SLOTS)[None, :] < row_counts[:, None]).astype(f32).reshape(1, 128)
-    weight = lax.dynamic_slice_in_dim(fours, core, 1, 0) * live
-    ctx, gain, weight, out_other, gate_other, up_other, down_other = lax.optimization_barrier(
-        (ctx, gain, weight, out_other, gate_other, up_other, down_other)
+    sources = (norm_gain, expert_ids, route_gates, row_counts, gate_proj, up_proj)
+    blank = jnp.zeros((D // 16, 128), f32), jnp.zeros((1, 128), f32), *unwritten(gate_proj, up_proj)
+    ctx, blank, sources, out_other, gate_other, up_other, down_other = lax.optimization_barrier(
+        (ctx, blank, sources, out_other, gate_other, up_other, down_other)
     )
+
+    def prepare(norm_gain, expert_ids, route_gates, row_counts, *weights):
+        gain = lax.dynamic_slice_in_dim(norm_gain, column * (D // 16), D // 16, 0)
+        fours = jnp.sum(jnp.where(expert_ids == column, route_gates, 0.0), axis=2)
+        live = (jnp.arange(SLOTS)[None, :] < row_counts[:, None]).astype(f32).reshape(1, 128)
+        return (
+            jnp.broadcast_to(gain[:, None], (D // 16, 128)),
+            lax.dynamic_slice_in_dim(fours, core, 1, 0) * live,
+            *stage(*weights),
+        )
+
+    early = lax.cond(core == 0, lambda _, sources: prepare(*sources), lambda blank, _: blank, blank, sources)
+    ctx, early = lax.optimization_barrier((ctx, early))
     ctx = lax.cond(core == 0, lambda v: jnp.stack([v[:, 1], v[:, 0]], axis=1), lambda v: v, ctx)
     ctx = jnp.transpose(ctx, (0, 2, 1, 3)).reshape(8, -1)
     ctx = spread(ctx, XY, NXY).reshape(128, -1)
+    ctx, early, sources = lax.optimization_barrier((ctx, early, sources))
+    gain, weight, gate_own, up_own = lax.cond(core == 0, lambda early, _: early, lambda _, sources: prepare(*sources), early, sources)
 
     half = ctx.shape[1] // 2
     part = jnp.dot(ctx[:, :half], out_other, preferred_element_type=f32)
@@ -221,7 +259,7 @@
     rows = spread(packed, XY, NXY)
     rows, own_hid = lax.optimization_barrier((rows, own_hid))
 
-    out = experts(rows, weight, gate_proj, gate_other, up_proj, up_other, down_proj, down_other)
+    out = experts(rows, weight, gate_own, gate_other, up_own, up_other, down_proj, down_other)
     out, own_hid = lax.optimization_barrier((out, own_hid))
     got = lax.all_to_all(out.reshape(NXY, 8, D), XY, 0, 0)
     got, own_hid = lax.optimization_barrier((got, own_hid))

time: 146 us -> 137 us (0.938)
  blocking collectives: 80.9 us -> 66.1 us
  waiting for transfers between devices: 23.7 us -> 18 us
  Pallas kernels: 8.65 us -> 14.3 us
  starting transfers between devices: 25 us -> 30.5 us
    all_to_all x2, blocking collectives: 57.5 us -> 46.7 us  [spread(): return lax.all_to_all(copies, axes, 0, 0)]
    pallas_call x0 -> x2, Pallas kernels: none -> 5.7 us  [the longest x1 3.89 us: stage(): pl.pallas_call(stage_kernel, in_specs=[pl.BlockSpec(memory_space=pl.ANY)]...]
    all_to_all x1, waiting for transfers between devices: 8.84 us -> 3.83 us  [spread(): return lax.all_to_all(copies, axes, 0, 0)]
    all_to_all x1, starting transfers between devices: 10.2 us -> 15.1 us  [body(): own = lax.all_to_all(sums, ('h', 'l', 'c'), 0, 0)]
    all_to_all x1, blocking collectives: 23.4 us -> 19.4 us  [body(): got = lax.all_to_all(out.reshape(NXY, 8, D), XY, 0, 0)]
  transfers between devices with their start and end apart: 8 -> 8, of which waited for: 4 -> 4; matrix products, arithmetic and copies ran while one was open for 1% -> 1% of each run, Pallas kernels for 3% -> 8%
where the time goes in v7:
time: 137 us; the launch traced here: 136 us
  blocking collectives  66.1 us (48%)
  starting transfers between devices  30.5 us (22%)
  waiting for transfers between devices  18 us (13%)
  Pallas kernels  14.3 us (10%)
  local copies, waits for them, and re-layouts  3.35 us (2%)
  other arithmetic  1.97 us (1%)
    all_to_all x2, blocking collectives, spread(): return lax.all_to_all(copies, axes, 0, 0)  46.7 us
    all_to_all x1, blocking collectives, body(): got = lax.all_to_all(out.reshape(NXY, 8, D), XY, 0, 0)  19.4 us
    all_to_all x1, starting transfers between devices, body(): own = lax.all_to_all(sums, ('h', 'l', 'c'), 0, 0)  15.1 us
    all_to_all x1, starting transfers between devices, body(): ctx = lax.all_to_all(ctx, ('h', 'c'), 0, 0).reshape(NH, 2, SLOTS, -1)  7.15 us
    all_to_all x1, waiting for transfers between devices, body(): own = lax.all_to_all(sums, ('h', 'l', 'c'), 0, 0)  7.02 us
    all_to_all x1, waiting for transfers between devices, body(): ctx = lax.all_to_all(ctx, ('h', 'c'), 0, 0).reshape(NH, 2, SLOTS, -1)  6.21 us
    pallas_call x1, Pallas kernels, attend(): pl.pallas_call(attend_kernel, in_specs=[scalars] * 3 + [far] * 7, out_spe...  4.78 us
    all_to_all x1, starting transfers between devices, spread(): return lax.all_to_all(copies, axes, 0, 0)  4.06 us
  transfers between devices with their start and end apart: 8, of which 4 were waited for; matrix products, arithmetic and copies ran while one was open for 1% of the time, Pallas kernels for 8%

profile of v7, /device:TPU:1, one launch (start us, length us, event | category | flops | bytes accessed | tf_op | source)
XLA Modules:
  0.0 136.1 jit_solution(8759986721360512691)
XLA Ops:
  0.6 3.3 %collective-permute-start.1 = (bf16[7168,128]{1,0:T(8,128)(2,1)}, bf16[7168,128]{1,0:T(8,128)(2,1)S(1)}, u32[]{:S(2)}, u32[]{:S(2)}) collective-permute-start(bf16[7168,128]{1,0:T(8,128)(2,1)} %param.35), channel_id=1, source_target_pairs={{0,1},{1,0},{2,3},{3,2},{4,5},{5,4},{6,7},{7,6},{8,9},{9,8},{10,11... | collective-permute-start | bytes 5505032 | tf_op jit(solution)/shard_map/ppermute | solution.py:203
  4.0 0.1 collective-permute-start.2
  4.1 0.4 collective-permute-start.3
  4.5 0.1 collective-permute-start
  4.6 4.8 %shard_map.167 = bf16[8,2,4096]{2,1,0:T(2,128)(2,1)} custom-call(s32[1]{0:T(128)} %bitcast.place, s32[2]{0:T(128)} %lengths.1, s32[64]{0:T(128)} %counts.1, bf16[2,2,16384]{2,1,0:T(2,128)(2,1)} %ql_hbm.1, bf16[2,2,2048]{2,1,0:T(2,128)(2,1)} %qr_hbm.1, bf16[2,384,512]{2,1,0:T(8,128)(2,1)} %cl_hbm.1, bf16[2,64,384]{2,1,0:T(8,128)(2,1)} %cr_hbm.1, ...), custom_call_target="tpu_custom_call" | custom-call | flops 160000000 | bytes 6000000 | tf_op jit(solution)/shard_map/pallas_call | solution.py:100
  9.4 7.1 %all-to-all-start = ((bf16[8,2,4096]{2,1,0:T(2,128)(2,1)}), bf16[8,2,4096]{2,1,0:T(2,128)(2,1)S(1)}, u32[]{:S(2)}, u32[]{:S(2)}) async-start(bf16[8,2,4096]{2,1,0:T(2,128)(2,1)} %shard_map.167), calls=%async_computation | async-start | bytes 262144 | tf_op jit(solution)/shard_map/all_to_all | solution.py:219
  16.5 1.8 %shard_map.168 = (bf16[7168,128]{1,0:T(8,128)(2,1)}, bf16[7168,128]{1,0:T(8,128)(2,1)}) custom-call(), custom_call_target="tpu_custom_call" | custom-call | tf_op jit(solution)/shard_map/pallas_call | solution.py:174
  18.3 6.2 %all-to-all-done = bf16[8,2,4096]{2,1,0:T(2,128)(2,1)S(1)} async-done(((bf16[8,2,4096]{2,1,0:T(2,128)(2,1)}), bf16[8,2,4096]{2,1,0:T(2,128)(2,1)S(1)}, u32[]{:S(2)}, u32[]{:S(2)}) %all-to-all-start) | async-done | bytes 131104 | tf_op jit(solution)/shard_map/all_to_all | solution.py:219
  24.5 0.0 collective-permute-done
  24.5 0.0 collective-permute-done.1.g1
  24.6 0.0 collective-permute-done.2.u1
  24.6 0.0 collective-permute-done.3.d1
  24.7 0.1 copy.21
  24.8 0.1 copy.23
  24.9 0.2 broadcast_in_dim.59
  25.1 0.0 copy-start.6
  25.1 26.9 %all_to_all.30 = bf16[16,8,8192]{2,1,0:T(8,128)(2,1)S(1)} all-to-all(bf16[16,8,8192]{2,1,0:T(8,128)(2,1)S(1)} %broadcast_in_dim.59), channel_id=1, replica_groups=mesh['x'=4,'y'=4,'h'=4,'l'=2,'c'=2] {'x','y'}, dimensions={0} | all-to-all | bytes 4194304 | tf_op jit(solution)/shard_map/all_to_all | solution.py:32
  52.0 0.4 convolution_bitcast_fusion
  52.4 0.5 fusion
  52.9 0.7 broadcast_in_dim.60
  53.6 4.1 %all-to-all-start.2 = ((bf16[8,112,128]{2,1,0:T(8,128)(2,1)}), bf16[8,112,128]{2,1,0:T(8,128)(2,1)S(1)}, u32[]{:S(2)}, u32[]{:S(2)}) async-start(bf16[8,112,128]{2,1,0:T(8,128)(2,1)} %broadcast_in_dim.60), calls=%async_computation.2 | async-start | bytes 458752 | tf_op jit(solution)/shard_map/all_to_all | solution.py:32
  57.7 0.1 pad.9.clone
  57.7 5.1 %conditional.5 = ((f32[448,128]{1,0:T(8,128)S(1)}, f32[1,128]{1,0:T(1,128)S(1)}, bf16[7168,128]{1,0:T(8,128)(2,1)}, bf16[7168,128]{1,0:T(8,128)(2,1)})) conditional(s32[]{:T(128)} %convert_element_type.70, (s32[]{:T(128)}, f32[7168]{0:T(1024)}, s32[64]{0:T(128)S(1)}, s32[2,128,4]{1,2,0:T(4,128)S(1)}, f32[2,128,4]{1,2,0:T(4,128)S(1)}, ...), branch_computations={%region_6.8_spmd, %region_8.9_spmd} | conditional | flops 3079 | bytes 245892 | solution.py:242
  57.7 0.8 dynamic_slice.13
  58.5 0.1 broadcast_in_dim.11
  58.6 0.1 iota_compare_fusion.1
  58.7 0.2 lt.59
  58.9 3.9 %branch_0_fun.1 = (bf16[7168,128]{1,0:T(8,128)(2,1)}, bf16[7168,128]{1,0:T(8,128)(2,1)}) custom-call(bf16[7168,128]{1,0:T(8,128)(2,1)} %get-tuple-element.69.a, bf16[7168,128]{1,0:T(8,128)(2,1)} %get-tuple-element.70.b), custom_call_target="tpu_custom_call" | custom-call | tf_op jit(solution)/shard_map/cond/branch_0_fun/pallas_call | solution.py:164
  62.8 3.8 %all-to-all-done.2 = bf16[8,112,128]{2,1,0:T(8,128)(2,1)S(1)} async-done(((bf16[8,112,128]{2,1,0:T(8,128)(2,1)}), bf16[8,112,128]{2,1,0:T(8,128)(2,1)S(1)}, u32[]{:S(2)}, u32[]{:S(2)}) %all-to-all-start.2) | async-done | bytes 229408 | tf_op jit(solution)/shard_map/all_to_all | solution.py:32
  66.7 0.1 multiply_reduce_fusion
  66.8 0.1 maximum_maximum_fusion
  67.0 0.0 copy-start.2
  67.0 0.2 broadcast_in_dim.62
  67.2 0.0 copy-start
  67.2 0.0 copy-start.1
  67.2 19.8 %all_to_all.31.rows = bf16[16,464,128]{2,1,0:T(8,128)(2,1)S(1)} all-to-all(bf16[16,464,128]{2,1,0:T(8,128)(2,1)S(1)} %broadcast_in_dim.62), channel_id=1, replica_groups=mesh['x'=4,'y'=4,'h'=4,'l'=2,'c'=2] {'x','y'}, dimensions={0} | all-to-all | bytes 3801088 | tf_op jit(solution)/shard_map/all_to_all | solution.py:32
  87.1 0.0 copy-done.1
  87.1 3.9 %shard_map.169 = bf16[128,7168]{1,0:T(8,128)(2,1)S(1)} custom-call(bf16[16,464,128]{2,1,0:T(8,128)(2,1)S(1)} %all_to_all.31.rows, f32[1,128]{1,0:T(1,128)S(1)} %get-tuple-element.162.weight, bf16[7168,128]{1,0:T(8,128)(2,1)S(1)} %copy-done.1, bf16[7168,128]{1,0:T(8,128)(2,1)S(1)} %collective-permute-done.1.g1, bf16[7168,128]{1,0:T(8,128)(2,1)S(1)} %copy-done.2, ...), custom_call_target="tpu_custom_call" | custom-call | flops 705000000 | bytes 15000000 | tf_op jit(solution)/shard_map/pallas_call | solution.py:145
  90.9 19.4 %all_to_all.32 = bf16[16,8,7168]{2,1,0:T(8,128)(2,1)S(1)} all-to-all(bf16[16,8,7168]{2,1,0:T(8,128)(2,1)S(1)} %bitcast.34), channel_id=1, replica_groups=mesh['x'=4,'y'=4,'h'=4,'l'=2,'c'=2] {'x','y'}, dimensions={0} | all-to-all | bytes 3670016 | tf_op jit(solution)/shard_map/all_to_all | solution.py:264
  110.4 0.3 reduce_sum.65
  110.6 0.1 reshape.113
  110.7 0.7 copy.22
  111.4 15.1 %all-to-all-start.5 = ((bf16[16,2,1792]{2,1,0:T(2,128)(2,1)}), bf16[16,2,1792]{2,1,0:T(2,128)(2,1)S(1)}, u32[]{:S(2)}, u32[]{:S(2)}) async-start(bf16[16,2,1792]{2,1,0:T(2,128)(2,1)} %bitcast.14), calls=%async_computation.5 | async-start | bytes 229376 | tf_op jit(solution)/shard_map/all_to_all | solution.py:273
  126.5 0.3 collective-permute-start.4
  126.8 0.9 collective-permute-done.4
  127.7 0.6 fusion.4
  128.3 7.0 %all-to-all-done.5 = bf16[16,2,1792]{2,1,0:T(2,128)(2,1)S(1)} async-done(((bf16[16,2,1792]{2,1,0:T(2,128)(2,1)}), bf16[16,2,1792]{2,1,0:T(2,128)(2,1)S(1)}, u32[]{:S(2)}, u32[]{:S(2)}) %all-to-all-start.5) | async-done | bytes 114720 | tf_op jit(solution)/shard_map/all_to_all | solution.py:273
  135.4 0.7 reduce.3
  (21 shorter events, 0.2 us)
Async XLA Ops:
  0.6 23.9 %collective-permute-start.1 = (bf16[7168,128]{1,0:T(8,128)(2,1)}, bf16[7168,128]{1,0:T(8,128)(2,1)S(1)}, u32[]{:S(2)}, u32[]{:S(2)}) collective-permute-start(bf16[7168,128]{1,0:T(8,128)(2,1)} %param.35), channel_id=1, source_target_pairs={{0,1},{1,0},{2,3},{3,2},{4,5},{5,4},{6,7},{7,6},{8,9},{9,8},{10,11... | collective-permute-start | bytes 5505032 | tf_op jit(solution)/shard_map/ppermute | solution.py:203
  4.0 20.6 %collective-permute-start.2 = (bf16[7168,128]{1,0:T(8,128)(2,1)}, bf16[7168,128]{1,0:T(8,128)(2,1)}, u32[]{:S(2)}, u32[]{:S(2)}) collective-permute-start(bf16[7168,128]{1,0:T(8,128)(2,1)} %param.36), channel_id=1, source_target_pairs={{0,1},{1,0},{2,3},{3,2},{4,5},{5,4},{6,7},{7,6},{8,9},{9,8},{10,11... | collective-permute-start | bytes 5505032 | tf_op jit(solution)/shard_map/ppermute | solution.py:204
  4.1 20.5 %collective-permute-start.3 = (bf16[128,7168]{1,0:T(8,128)(2,1)}, bf16[128,7168]{1,0:T(8,128)(2,1)}, u32[]{:S(2)}, u32[]{:S(2)}) collective-permute-start(bf16[128,7168]{1,0:T(8,128)(2,1)} %d0.1), channel_id=1, source_target_pairs={{0,1},{1,0},{2,3},{3,2},{4,5},{5,4},{6,7},{7,6},{8,9},{9,8},{10,11... | collective-permute-start | bytes 5505032 | tf_op jit(solution)/shard_map/ppermute | solution.py:205
  4.5 20.1 %collective-permute-start = (bf16[4096,112]{0,1:T(8,128)(2,1)}, bf16[4096,112]{0,1:T(8,128)(2,1)S(1)}, u32[]{:S(2)}, u32[]{:S(2)}) collective-permute-start(bf16[4096,112]{0,1:T(8,128)(2,1)} %param.31), channel_id=1, source_target_pairs={{0,1},{1,0},{2,3},{3,2},{4,5},{5,4},{6,7},{7,6},{8,9},{9,8},{10,11... | collective-permute-start | bytes 2752520 | tf_op jit(solution)/shard_map/ppermute | solution.py:202
  4.6 20.0 %copy-start.3 = (s32[2,128,4]{1,2,0:T(4,128)S(1)}, s32[2,128,4]{1,2,0:T(4,128)}, u32[]{:S(2)}) copy-start(s32[2,128,4]{1,2,0:T(4,128)} %param.33) | copy-start | bytes 12292
  4.6 20.0 %copy-start.4 = (f32[2,128,4]{1,2,0:T(4,128)S(1)}, f32[2,128,4]{1,2,0:T(4,128)}, u32[]{:S(2)}) copy-start(f32[2,128,4]{1,2,0:T(4,128)} %param.34) | copy-start | bytes 12292
  4.6 20.0 %copy-start.5 = (s32[64]{0:T(128)S(1)}, s32[64]{0:T(128)}, u32[]{:S(2)}) copy-start(s32[64]{0:T(128)} %counts.1) | copy-start | bytes 772
  9.4 15.2 %all-to-all-start = ((bf16[8,2,4096]{2,1,0:T(2,128)(2,1)}), bf16[8,2,4096]{2,1,0:T(2,128)(2,1)S(1)}, u32[]{:S(2)}, u32[]{:S(2)}) async-start(bf16[8,2,4096]{2,1,0:T(2,128)(2,1)} %shard_map.167), calls=%async_computation | async-start | bytes 262144 | tf_op jit(solution)/shard_map/all_to_all | solution.py:219
  25.1 26.9 %copy-start.6 = (bf16[4096,112]{0,1:T(8,128)(2,1)S(1)}, bf16[4096,112]{0,1:T(8,128)(2,1)}, u32[]{:S(2)}) copy-start(bf16[4096,112]{0,1:T(8,128)(2,1)} %param.31) | copy-start | bytes 2752516
  53.6 13.0 %all-to-all-start.2 = ((bf16[8,112,128]{2,1,0:T(8,128)(2,1)}), bf16[8,112,128]{2,1,0:T(8,128)(2,1)S(1)}, u32[]{:S(2)}, u32[]{:S(2)}) async-start(bf16[8,112,128]{2,1,0:T(8,128)(2,1)} %broadcast_in_dim.60), calls=%async_computation.2 | async-start | bytes 458752 | tf_op jit(solution)/shard_map/all_to_all | solution.py:32
  67.0 20.1 %copy-start.2 = (bf16[7168,128]{1,0:T(8,128)(2,1)S(1)}, bf16[7168,128]{1,0:T(8,128)(2,1)}, u32[]{:S(2)}) copy-start(bf16[7168,128]{1,0:T(8,128)(2,1)} %get-tuple-element.165.u0) | copy-start | bytes 5505028
  67.2 19.8 %copy-start = (bf16[128,7168]{1,0:T(8,128)(2,1)S(1)}, bf16[128,7168]{1,0:T(8,128)(2,1)}, u32[]{:S(2)}) copy-start(bf16[128,7168]{1,0:T(8,128)(2,1)} %d0.1) | copy-start | bytes 5505028
  67.2 19.8 %copy-start.1 = (bf16[7168,128]{1,0:T(8,128)(2,1)S(1)}, bf16[7168,128]{1,0:T(8,128)(2,1)}, u32[]{:S(2)}) copy-start(bf16[7168,128]{1,0:T(8,128)(2,1)} %get-tuple-element.163.g0) | copy-start | bytes 5505028
  111.4 23.9 %all-to-all-start.5 = ((bf16[16,2,1792]{2,1,0:T(2,128)(2,1)}), bf16[16,2,1792]{2,1,0:T(2,128)(2,1)S(1)}, u32[]{:S(2)}, u32[]{:S(2)}) async-start(bf16[16,2,1792]{2,1,0:T(2,128)(2,1)} %bitcast.14), calls=%async_computation.5 | async-start | bytes 229376 | tf_op jit(solution)/shard_map/all_to_all | solution.py:273
  126.5 1.2 collective-permute-start.4

commit v8 on v7

--- a/solution.py
+++ b/solution.py
@@ -178,6 +178,45 @@
     )()
 
 
+def sum_kernel(got, out):
+    total = jnp.sum(got[...].astype(f32), axis=0).astype(bf16)
+    for h in range(NH):
+        for q in range(4):
+            out[h * 4 + q] = total[h * SLOTS : (h + 1) * SLOTS, q * (D // 4) : (q + 1) * (D // 4)]
+
+
+def sum_sources(got):
+    near = pl.BlockSpec(memory_space=pltpu.VMEM)
+    return pl.pallas_call(
+        sum_kernel,
+        in_specs=[near],
+        out_specs=near,
+        out_shape=jax.ShapeDtypeStruct((16, SLOTS, D // 4), bf16),
+        compiler_params=pltpu.CompilerParams(vmem_limit_bytes=16 * 1024 * 1024),
+    )(got)
+
+
+def project_kernel(ctx, own, other, out):
+    dims = (((1,), (1,)), ((), ()))
+    half = own.shape[1]
+    part = lax.dot_general(other[...], ctx[:, :half], dims, preferred_element_type=f32)
+    part += lax.dot_general(own[...], ctx[:, half:], dims, preferred_element_type=f32)
+    part = part.astype(bf16)
+    for i in range(NZ):
+        out[i] = part
+
+
+def project(ctx, own, other):
+    near = pl.BlockSpec(memory_space=pltpu.VMEM)
+    return pl.pallas_call(
+        project_kernel,
+        in_specs=[near] * 3,
+        out_specs=near,
+        out_shape=jax.ShapeDtypeStruct((NZ, own.shape[0], 128), bf16),
+        compiler_params=pltpu.CompilerParams(vmem_limit_bytes=16 * 1024 * 1024),
+    )(ctx, own, other)
+
+
 def body(
     query_latent,
     query_rope,
@@ -199,7 +238,7 @@
     core = lax.axis_index("c")
     column = lax.axis_index(XY)
 
-    out_other = lax.ppermute(out_proj, "c", SWAP)
+    out_other = lax.ppermute(out_proj.T, "c", SWAP)
     gate_other = lax.ppermute(gate_proj, "c", SWAP)
     up_other = lax.ppermute(up_proj, "c", SWAP)
     down_other = lax.ppermute(down_proj, "c", SWAP)
@@ -217,10 +256,10 @@
         value_up,
     )
     ctx = lax.all_to_all(ctx, ("h", "c"), 0, 0).reshape(NH, 2, SLOTS, -1)
-    sources = (norm_gain, expert_ids, route_gates, row_counts, gate_proj, up_proj)
-    blank = jnp.zeros((D // 16, 128), f32), jnp.zeros((1, 128), f32), *unwritten(gate_proj, up_proj)
-    ctx, blank, sources, out_other, gate_other, up_other, down_other = lax.optimization_barrier(
-        (ctx, blank, sources, out_other, gate_other, up_other, down_other)
+    sources = (norm_gain, expert_ids, route_gates, row_counts, up_other, down_other)
+    blank = jnp.zeros((D // 16, 128), f32), jnp.zeros((1, 128), f32), *unwritten(up_other, down_other)
+    ctx, blank, sources, out_other, gate_other = lax.optimization_barrier(
+        (ctx, blank, sources, out_other, gate_other)
     )
 
     def prepare(norm_gain, expert_ids, route_gates, row_counts, *weights):
@@ -239,13 +278,9 @@
     ctx = jnp.transpose(ctx, (0, 2, 1, 3)).reshape(8, -1)
     ctx = spread(ctx, XY, NXY).reshape(128, -1)
     ctx, early, sources = lax.optimization_barrier((ctx, early, sources))
-    gain, weight, gate_own, up_own = lax.cond(core == 0, lambda early, _: early, lambda _, sources: prepare(*sources), early, sources)
-
-    half = ctx.shape[1] // 2
-    part = jnp.dot(ctx[:, :half], out_other, preferred_element_type=f32)
-    part = part + jnp.dot(ctx[:, half:], out_proj, preferred_element_type=f32)
-    chip = part.T.astype(bf16)
-    pieces = spread(chip, Z, NZ).reshape(NH, 2, D // 64, 128).astype(f32)
+    gain, weight, up_other, down_other = lax.cond(core == 0, lambda early, _: early, lambda _, sources: prepare(*sources), early, sources)
+
+    pieces = lax.all_to_all(project(ctx, out_proj.T, out_other), Z, 0, 0).reshape(NH, 2, D // 64, 128).astype(f32)
     hid = jnp.sum(pieces, axis=1).astype(bf16)
     own_hid = lax.dynamic_index_in_dim(hid, lax.axis_index("h"), 0, keepdims=False)
 
@@ -259,12 +294,11 @@
     rows = spread(packed, XY, NXY)
     rows, own_hid = lax.optimization_barrier((rows, own_hid))
 
-    out = experts(rows, weight, gate_own, gate_other, up_own, up_other, down_proj, down_other)
+    out = experts(rows, weight, gate_proj, gate_other, up_proj, up_other, down_proj, down_other)
     out, own_hid = lax.optimization_barrier((out, own_hid))
     got = lax.all_to_all(out.reshape(NXY, 8, D), XY, 0, 0)
     got, own_hid = lax.optimization_barrier((got, own_hid))
-    sums = jnp.sum(got.astype(f32), axis=0).astype(bf16)
-    sums = jnp.transpose(sums.reshape(NH, SLOTS, 4, D // 4), (0, 2, 1, 3)).reshape(16, SLOTS, D // 4)
+    sums = sum_sources(got)
 
     other_hid = lax.ppermute(own_hid, "c", SWAP)
     steps = jnp.where(core == 0, jnp.stack([own_hid, other_hid]), jnp.stack([other_hid, own_hid]))

time: 137 us -> 136 us (level)
  Pallas kernels: 14.3 us -> 16.7 us
  local copies, waits for them, and re-layouts: 3.35 us -> 1.84 us
    ppermute x1, starting transfers between devices: 0.1 us -> 3.33 us  [body(): up_other = lax.ppermute(up_proj, 'c', SWAP)]
    ppermute x1, starting transfers between devices: 3.33 us -> 0.41 us  [body(): gate_other = lax.ppermute(gate_proj, 'c', SWAP)]
    pallas_call x0 -> x2, Pallas kernels: none -> 2.31 us  [the longest x1 1.4 us: project(): pl.pallas_call(project_kernel, in_specs=[near] * 3, out_specs=near, out_s...]
where the time goes in v8:
time: 136 us
  blocking collectives  66.1 us (49%)
  starting transfers between devices  30.5 us (22%)
  waiting for transfers between devices  17.9 us (13%)
  Pallas kernels  16.7 us (12%)
  local copies, waits for them, and re-layouts  1.84 us (1%)
  other arithmetic  1.72 us (1%)
    all_to_all x2, blocking collectives, spread(): return lax.all_to_all(copies, axes, 0, 0)  46.7 us
    all_to_all x1, blocking collectives, body(): got = lax.all_to_all(out.reshape(NXY, 8, D), XY, 0, 0)  19.4 us
    all_to_all x1, starting transfers between devices, body(): own = lax.all_to_all(sums, ('h', 'l', 'c'), 0, 0)  15.1 us
    all_to_all x1, starting transfers between devices, body(): ctx = lax.all_to_all(ctx, ('h', 'c'), 0, 0).reshape(NH, 2, SLOTS, -1)  7.14 us
    all_to_all x1, waiting for transfers between devices, body(): own = lax.all_to_all(sums, ('h', 'l', 'c'), 0, 0)  7.02 us
    all_to_all x1, waiting for transfers between devices, body(): ctx = lax.all_to_all(ctx, ('h', 'c'), 0, 0).reshape(NH, 2, SLOTS, -1)  6.19 us
    pallas_call x1, Pallas kernels, attend(): pl.pallas_call(attend_kernel, in_specs=[scalars] * 3 + [far] * 7, out_spe...  4.78 us
    all_to_all x1, starting transfers between devices, body(): lax.all_to_all(project(ctx, out_proj.T, out_other), Z, 0, 0)  4.03 us
  transfers between devices with their start and end apart: 8, of which 4 were waited for; matrix products, arithmetic and copies ran while one was open for 1% of the time, Pallas kernels for 8%

profile of v8, /device:TPU:1, one launch (start us, length us, event | category | flops | bytes accessed | tf_op | source)
XLA Modules:
  0.0 135.7 jit_solution(4216128201196951253)
XLA Ops:
  0.6 3.3 %collective-permute-start = (bf16[7168,128]{1,0:T(8,128)(2,1)}, bf16[7168,128]{1,0:T(8,128)(2,1)}, u32[]{:S(2)}, u32[]{:S(2)}) collective-permute-start(bf16[7168,128]{1,0:T(8,128)(2,1)} %u0.1), channel_id=1, source_target_pairs={{0,1},{1,0},{2,3},{3,2},{4,5},{5,4},{6,7},{7,6},{8,9},{9,8},{10,11... | collective-permute-start | bytes 5505032 | tf_op jit(solution)/shard_map/ppermute | solution.py:243
  4.0 0.1 collective-permute-start.1
  4.1 0.4 collective-permute-start.3
  4.5 0.1 collective-permute-start.2
  4.6 4.8 %shard_map.167 = bf16[8,2,4096]{2,1,0:T(2,128)(2,1)} custom-call(s32[1]{0:T(128)} %bitcast.place, s32[2]{0:T(128)} %lengths.1, s32[64]{0:T(128)} %counts.1, bf16[2,2,16384]{2,1,0:T(2,128)(2,1)} %ql_hbm.1, bf16[2,2,2048]{2,1,0:T(2,128)(2,1)} %qr_hbm.1, bf16[2,384,512]{2,1,0:T(8,128)(2,1)} %cl_hbm.1, bf16[2,64,384]{2,1,0:T(8,128)(2,1)} %cr_hbm.1, ...), custom_call_target="tpu_custom_call" | custom-call | flops 160000000 | bytes 6000000 | tf_op jit(solution)/shard_map/pallas_call | solution.py:100
  9.4 7.1 %all-to-all-start = ((bf16[8,2,4096]{2,1,0:T(2,128)(2,1)}), bf16[8,2,4096]{2,1,0:T(2,128)(2,1)S(1)}, u32[]{:S(2)}, u32[]{:S(2)}) async-start(bf16[8,2,4096]{2,1,0:T(2,128)(2,1)} %shard_map.167), calls=%async_computation | async-start | bytes 262144 | tf_op jit(solution)/shard_map/all_to_all | solution.py:258
  16.5 1.8 %shard_map.168 = (bf16[7168,128]{1,0:T(8,128)(2,1)}, bf16[128,7168]{1,0:T(8,128)(2,1)}) custom-call(), custom_call_target="tpu_custom_call" | custom-call | tf_op jit(solution)/shard_map/pallas_call | solution.py:174
  18.4 6.2 %all-to-all-done = bf16[8,2,4096]{2,1,0:T(2,128)(2,1)S(1)} async-done(((bf16[8,2,4096]{2,1,0:T(2,128)(2,1)}), bf16[8,2,4096]{2,1,0:T(2,128)(2,1)S(1)}, u32[]{:S(2)}, u32[]{:S(2)}) %all-to-all-start) | async-done | bytes 131104 | tf_op jit(solution)/shard_map/all_to_all | solution.py:258
  24.5 0.0 collective-permute-done.2.other
  24.5 0.0 collective-permute-done
  24.6 0.0 collective-permute-done.1
  24.6 0.0 collective-permute-done.3.g1
  24.6 0.0 copy-done.4
  24.6 0.0 copy-done.5
  24.6 0.0 copy-done.6
  24.7 0.1 copy.18
  24.8 0.1 copy.19
  24.9 0.2 broadcast_in_dim.53
  25.1 0.0 copy-start.3
  25.1 26.9 %all_to_all.30 = bf16[16,8,8192]{2,1,0:T(8,128)(2,1)S(1)} all-to-all(bf16[16,8,8192]{2,1,0:T(8,128)(2,1)S(1)} %broadcast_in_dim.53), channel_id=1, replica_groups=mesh['x'=4,'y'=4,'h'=4,'l'=2,'c'=2] {'x','y'}, dimensions={0} | all-to-all | bytes 4194304 | tf_op jit(solution)/shard_map/all_to_all | solution.py:32
  52.0 0.0 copy-done.3
  52.0 1.4 %shard_map.169 = bf16[8,112,128]{2,1,0:T(8,128)(2,1)} custom-call(bf16[128,8192]{1,0:T(8,128)(2,1)S(1)} %bitcast.29, bf16[112,4096]{1,0:T(8,128)(2,1)S(1)} %bitcast.32, bf16[112,4096]{1,0:T(8,128)(2,1)S(1)} %collective-permute-done.2.other), custom_call_target="tpu_custom_call" | custom-call | tf_op jit(solution)/shard_map/pallas_call | solution.py:211
  53.4 4.0 %all-to-all-start.2 = ((bf16[8,112,128]{2,1,0:T(8,128)(2,1)}), bf16[8,112,128]{2,1,0:T(8,128)(2,1)S(1)}, u32[]{:S(2)}, u32[]{:S(2)}) async-start(bf16[8,112,128]{2,1,0:T(8,128)(2,1)} %shard_map.169), calls=%async_computation.2 | async-start | bytes 458752 | tf_op jit(solution)/shard_map/all_to_all | solution.py:283
  57.4 0.1 pad.9.clone
  57.5 5.1 %conditional.5 = ((f32[448,128]{1,0:T(8,128)S(1)}, f32[1,128]{1,0:T(1,128)S(1)}, bf16[7168,128]{1,0:T(8,128)(2,1)}, bf16[128,7168]{1,0:T(8,128)(2,1)})) conditional(s32[]{:T(128)} %convert_element_type.65, (s32[]{:T(128)}, f32[7168]{0:T(1024)}, s32[64]{0:T(128)S(1)}, s32[2,128,4]{1,2,0:T(4,128)S(1)}, f32[2,128,4]{1,2,0:T(4,128)S(1)}, ...), branch_computations={%region_6.8_spmd, %region_8.9_spmd} | conditional | flops 3079 | bytes 245892 | solution.py:281
  57.5 0.8 dynamic_slice.13
  58.3 0.1 broadcast_in_dim.22
  58.4 0.1 iota_compare_fusion.1
  58.5 0.2 lt.59
  58.7 3.9 %branch_0_fun.1 = (bf16[7168,128]{1,0:T(8,128)(2,1)}, bf16[128,7168]{1,0:T(8,128)(2,1)}) custom-call(bf16[7168,128]{1,0:T(8,128)(2,1)} %get-tuple-element.69.a, bf16[128,7168]{1,0:T(8,128)(2,1)} %get-tuple-element.70.b), custom_call_target="tpu_custom_call" | custom-call | tf_op jit(solution)/shard_map/cond/branch_0_fun/pallas_call | solution.py:164
  62.6 3.8 %all-to-all-done.2 = bf16[8,112,128]{2,1,0:T(8,128)(2,1)S(1)} async-done(((bf16[8,112,128]{2,1,0:T(8,128)(2,1)}), bf16[8,112,128]{2,1,0:T(8,128)(2,1)S(1)}, u32[]{:S(2)}, u32[]{:S(2)}) %all-to-all-start.2) | async-done | bytes 229408 | tf_op jit(solution)/shard_map/all_to_all | solution.py:283
  66.4 0.1 multiply_reduce_fusion
  66.6 0.1 maximum_maximum_fusion
  66.7 0.0 copy-start.2
  66.7 0.2 broadcast_in_dim.55
  67.0 0.0 copy-start
  67.0 0.0 copy-start.1
  67.0 19.8 %all_to_all.31.rows = bf16[16,464,128]{2,1,0:T(8,128)(2,1)S(1)} all-to-all(bf16[16,464,128]{2,1,0:T(8,128)(2,1)S(1)} %broadcast_in_dim.55), channel_id=1, replica_groups=mesh['x'=4,'y'=4,'h'=4,'l'=2,'c'=2] {'x','y'}, dimensions={0} | all-to-all | bytes 3801088 | tf_op jit(solution)/shard_map/all_to_all | solution.py:32
  86.8 0.0 copy-done
  86.8 3.9 %shard_map.170 = bf16[128,7168]{1,0:T(8,128)(2,1)S(1)} custom-call(bf16[16,464,128]{2,1,0:T(8,128)(2,1)S(1)} %all_to_all.31.rows, f32[1,128]{1,0:T(1,128)S(1)} %get-tuple-element.160.weight, bf16[7168,128]{1,0:T(8,128)(2,1)S(1)} %copy-done.2, bf16[7168,128]{1,0:T(8,128)(2,1)S(1)} %collective-permute-done.3.g1, bf16[7168,128]{1,0:T(8,128)(2,1)S(1)} %copy-done, ...), custom_call_target="tpu_custom_call" | custom-call | flops 705000000 | bytes 15000000 | tf_op jit(solution)/shard_map/pallas_call | solution.py:145
  90.7 19.4 %all_to_all.32.got = bf16[16,8,7168]{2,1,0:T(8,128)(2,1)S(1)} all-to-all(bf16[16,8,7168]{2,1,0:T(8,128)(2,1)S(1)} %bitcast.30), channel_id=1, replica_groups=mesh['x'=4,'y'=4,'h'=4,'l'=2,'c'=2] {'x','y'}, dimensions={0} | all-to-all | bytes 3670016 | tf_op jit(solution)/shard_map/all_to_all | solution.py:299
  110.1 0.9 shard_map.171
  111.0 15.1 %all-to-all-start.5 = ((bf16[16,2,1792]{2,1,0:T(2,128)(2,1)}), bf16[16,2,1792]{2,1,0:T(2,128)(2,1)S(1)}, u32[]{:S(2)}, u32[]{:S(2)}) async-start(bf16[16,2,1792]{2,1,0:T(2,128)(2,1)} %shard_map.171), calls=%async_computation.5 | async-start | bytes 229376 | tf_op jit(solution)/shard_map/all_to_all | solution.py:307
  126.1 0.3 collective-permute-start.4
  126.4 0.9 collective-permute-done.4
  127.3 0.6 fusion.1
  127.9 7.0 %all-to-all-done.5 = bf16[16,2,1792]{2,1,0:T(2,128)(2,1)S(1)} async-done(((bf16[16,2,1792]{2,1,0:T(2,128)(2,1)}), bf16[16,2,1792]{2,1,0:T(2,128)(2,1)S(1)}, u32[]{:S(2)}, u32[]{:S(2)}) %all-to-all-start.5) | async-done | bytes 114720 | tf_op jit(solution)/shard_map/all_to_all | solution.py:307
  135.0 0.7 reduce.2
  (17 shorter events, 0.2 us)
Async XLA Ops:
  0.6 23.9 %collective-permute-start = (bf16[7168,128]{1,0:T(8,128)(2,1)}, bf16[7168,128]{1,0:T(8,128)(2,1)}, u32[]{:S(2)}, u32[]{:S(2)}) collective-permute-start(bf16[7168,128]{1,0:T(8,128)(2,1)} %u0.1), channel_id=1, source_target_pairs={{0,1},{1,0},{2,3},{3,2},{4,5},{5,4},{6,7},{7,6},{8,9},{9,8},{10,11... | collective-permute-start | bytes 5505032 | tf_op jit(solution)/shard_map/ppermute | solution.py:243
  4.0 20.6 %collective-permute-start.1 = (bf16[128,7168]{1,0:T(8,128)(2,1)}, bf16[128,7168]{1,0:T(8,128)(2,1)}, u32[]{:S(2)}, u32[]{:S(2)}) collective-permute-start(bf16[128,7168]{1,0:T(8,128)(2,1)} %d0.1), channel_id=1, source_target_pairs={{0,1},{1,0},{2,3},{3,2},{4,5},{5,4},{6,7},{7,6},{8,9},{9,8},{10,11... | collective-permute-start | bytes 5505032 | tf_op jit(solution)/shard_map/ppermute | solution.py:244
  4.1 20.5 %collective-permute-start.3 = (bf16[7168,128]{1,0:T(8,128)(2,1)}, bf16[7168,128]{1,0:T(8,128)(2,1)S(1)}, u32[]{:S(2)}, u32[]{:S(2)}) collective-permute-start(bf16[7168,128]{1,0:T(8,128)(2,1)} %g0.1), channel_id=1, source_target_pairs={{0,1},{1,0},{2,3},{3,2},{4,5},{5,4},{6,7},{7,6},{8,9},{9,8},{10,11... | collective-permute-start | bytes 5505032 | tf_op jit(solution)/shard_map/ppermute | solution.py:242
  4.5 20.1 %collective-permute-start.2 = (bf16[112,4096]{1,0:T(8,128)(2,1)}, bf16[112,4096]{1,0:T(8,128)(2,1)S(1)}, u32[]{:S(2)}, u32[]{:S(2)}) collective-permute-start(bf16[112,4096]{1,0:T(8,128)(2,1)} %bitcast.31), channel_id=1, source_target_pairs={{0,1},{1,0},{2,3},{3,2},{4,5},{5,4},{6,7},{7,6},{8,9},{9,8},{10,11... | collective-permute-start | bytes 2752520 | tf_op jit(solution)/shard_map/ppermute | solution.py:241
  4.6 20.0 %copy-start.4 = (s32[2,128,4]{1,2,0:T(4,128)S(1)}, s32[2,128,4]{1,2,0:T(4,128)}, u32[]{:S(2)}) copy-start(s32[2,128,4]{1,2,0:T(4,128)} %param.33) | copy-start | bytes 12292
  4.6 20.0 %copy-start.5 = (f32[2,128,4]{1,2,0:T(4,128)S(1)}, f32[2,128,4]{1,2,0:T(4,128)}, u32[]{:S(2)}) copy-start(f32[2,128,4]{1,2,0:T(4,128)} %param.34) | copy-start | bytes 12292
  4.6 20.0 %copy-start.6 = (s32[64]{0:T(128)S(1)}, s32[64]{0:T(128)}, u32[]{:S(2)}) copy-start(s32[64]{0:T(128)} %counts.1) | copy-start | bytes 772
  9.4 15.2 %all-to-all-start = ((bf16[8,2,4096]{2,1,0:T(2,128)(2,1)}), bf16[8,2,4096]{2,1,0:T(2,128)(2,1)S(1)}, u32[]{:S(2)}, u32[]{:S(2)}) async-start(bf16[8,2,4096]{2,1,0:T(2,128)(2,1)} %shard_map.167), calls=%async_computation | async-start | bytes 262144 | tf_op jit(solution)/shard_map/all_to_all | solution.py:258
  25.1 26.9 %copy-start.3 = (bf16[4096,112]{0,1:T(8,128)(2,1)S(1)}, bf16[4096,112]{0,1:T(8,128)(2,1)}, u32[]{:S(2)}) copy-start(bf16[4096,112]{0,1:T(8,128)(2,1)} %param.31) | copy-start | bytes 2752516
  53.4 13.0 %all-to-all-start.2 = ((bf16[8,112,128]{2,1,0:T(8,128)(2,1)}), bf16[8,112,128]{2,1,0:T(8,128)(2,1)S(1)}, u32[]{:S(2)}, u32[]{:S(2)}) async-start(bf16[8,112,128]{2,1,0:T(8,128)(2,1)} %shard_map.169), calls=%async_computation.2 | async-start | bytes 458752 | tf_op jit(solution)/shard_map/all_to_all | solution.py:283
  66.7 20.1 %copy-start.2 = (bf16[7168,128]{1,0:T(8,128)(2,1)S(1)}, bf16[7168,128]{1,0:T(8,128)(2,1)}, u32[]{:S(2)}) copy-start(bf16[7168,128]{1,0:T(8,128)(2,1)} %g0.1) | copy-start | bytes 5505028
  67.0 19.8 %copy-start = (bf16[7168,128]{1,0:T(8,128)(2,1)S(1)}, bf16[7168,128]{1,0:T(8,128)(2,1)}, u32[]{:S(2)}) copy-start(bf16[7168,128]{1,0:T(8,128)(2,1)} %u0.1) | copy-start | bytes 5505028
  67.0 19.8 %copy-start.1 = (bf16[128,7168]{1,0:T(8,128)(2,1)S(1)}, bf16[128,7168]{1,0:T(8,128)(2,1)}, u32[]{:S(2)}) copy-start(bf16[128,7168]{1,0:T(8,128)(2,1)} %d0.1) | copy-start | bytes 5505028
  111.0 23.9 %all-to-all-start.5 = ((bf16[16,2,1792]{2,1,0:T(2,128)(2,1)}), bf16[16,2,1792]{2,1,0:T(2,128)(2,1)S(1)}, u32[]{:S(2)}, u32[]{:S(2)}) async-start(bf16[16,2,1792]{2,1,0:T(2,128)(2,1)} %shard_map.171), calls=%async_computation.5 | async-start | bytes 229376 | tf_op jit(solution)/shard_map/all_to_all | solution.py:307
  126.1 1.2 collective-permute-start.4

commit v9 on v8

--- a/solution.py
+++ b/solution.py
@@ -196,6 +196,25 @@
     )(got)
 
 
+def finish_kernel(own, out):
+    for s in range(STEPS):
+        total = own[s].astype(f32)
+        for z in range(1, NZ):
+            total += own[z * STEPS + s].astype(f32)
+        out[s] = total.astype(bf16)
+
+
+def finish(own):
+    near = pl.BlockSpec(memory_space=pltpu.VMEM)
+    return pl.pallas_call(
+        finish_kernel,
+        in_specs=[near],
+        out_specs=near,
+        out_shape=jax.ShapeDtypeStruct((STEPS, SLOTS, D // 4), bf16),
+        compiler_params=pltpu.CompilerParams(vmem_limit_bytes=16 * 1024 * 1024),
+    )(own)
+
+
 def project_kernel(ctx, own, other, out):
     dims = (((1,), (1,)), ((), ()))
     half = own.shape[1]
@@ -305,7 +324,7 @@
     hidden = jnp.transpose(steps, (0, 2, 1))
 
     own = lax.all_to_all(sums, ("h", "l", "c"), 0, 0)
-    mixed = jnp.sum(own.astype(f32).reshape(NZ, STEPS, SLOTS, D // 4), axis=0).astype(bf16)
+    mixed = finish(own)
     return hidden, mixed
 
 

time: 136 us -> 136 us (level)
  no operation moved by 1% of the time
where the time goes in v9:
time: 136 us
  blocking collectives  66.1 us (49%)
  starting transfers between devices  30.5 us (22%)
  waiting for transfers between devices  17.9 us (13%)
  Pallas kernels  17.4 us (13%)
  local copies, waits for them, and re-layouts  1.84 us (1%)
    all_to_all x2, blocking collectives, spread(): return lax.all_to_all(copies, axes, 0, 0)  46.7 us
    all_to_all x1, blocking collectives, body(): got = lax.all_to_all(out.reshape(NXY, 8, D), XY, 0, 0)  19.4 us
    all_to_all x1, starting transfers between devices, body(): own = lax.all_to_all(sums, ('h', 'l', 'c'), 0, 0)  15.1 us
    all_to_all x1, starting transfers between devices, body(): ctx = lax.all_to_all(ctx, ('h', 'c'), 0, 0).reshape(NH, 2, SLOTS, -1)  7.14 us
    all_to_all x1, waiting for transfers between devices, body(): own = lax.all_to_all(sums, ('h', 'l', 'c'), 0, 0)  7.02 us
    all_to_all x1, waiting for transfers between devices, body(): ctx = lax.all_to_all(ctx, ('h', 'c'), 0, 0).reshape(NH, 2, SLOTS, -1)  6.19 us
    pallas_call x1, Pallas kernels, attend(): pl.pallas_call(attend_kernel, in_specs=[scalars] * 3 + [far] * 7, out_spe...  4.79 us
    all_to_all x1, starting transfers between devices, body(): lax.all_to_all(project(ctx, out_proj.T, out_other), Z, 0, 0)  4.02 us
  transfers between devices with their start and end apart: 8, of which 4 were waited for; matrix products, arithmetic and copies ran while one was open for 1% of the time, Pallas kernels for 8%

profile of v9, /device:TPU:1, one launch (start us, length us, event | category | flops | bytes accessed | tf_op | source)
XLA Modules:
  0.0 135.6 jit_solution(9731714044417317702)
XLA Ops:
  0.6 3.3 %collective-permute-start = (bf16[7168,128]{1,0:T(8,128)(2,1)}, bf16[7168,128]{1,0:T(8,128)(2,1)}, u32[]{:S(2)}, u32[]{:S(2)}) collective-permute-start(bf16[7168,128]{1,0:T(8,128)(2,1)} %u0.1), channel_id=1, source_target_pairs={{0,1},{1,0},{2,3},{3,2},{4,5},{5,4},{6,7},{7,6},{8,9},{9,8},{10,11... | collective-permute-start | bytes 5505032 | tf_op jit(solution)/shard_map/ppermute | solution.py:262
  4.0 0.1 collective-permute-start.1
  4.1 0.4 collective-permute-start.3
  4.5 0.1 collective-permute-start.2
  4.6 4.8 %shard_map.167 = bf16[8,2,4096]{2,1,0:T(2,128)(2,1)} custom-call(s32[1]{0:T(128)} %bitcast.place, s32[2]{0:T(128)} %lengths.1, s32[64]{0:T(128)} %counts.1, bf16[2,2,16384]{2,1,0:T(2,128)(2,1)} %ql_hbm.1, bf16[2,2,2048]{2,1,0:T(2,128)(2,1)} %qr_hbm.1, bf16[2,384,512]{2,1,0:T(8,128)(2,1)} %cl_hbm.1, bf16[2,64,384]{2,1,0:T(8,128)(2,1)} %cr_hbm.1, ...), custom_call_target="tpu_custom_call" | custom-call | flops 160000000 | bytes 6000000 | tf_op jit(solution)/shard_map/pallas_call | solution.py:100
  9.4 7.1 %all-to-all-start = ((bf16[8,2,4096]{2,1,0:T(2,128)(2,1)}), bf16[8,2,4096]{2,1,0:T(2,128)(2,1)S(1)}, u32[]{:S(2)}, u32[]{:S(2)}) async-start(bf16[8,2,4096]{2,1,0:T(2,128)(2,1)} %shard_map.167), calls=%async_computation | async-start | bytes 262144 | tf_op jit(solution)/shard_map/all_to_all | solution.py:277
  16.5 1.8 %shard_map.168 = (bf16[7168,128]{1,0:T(8,128)(2,1)}, bf16[128,7168]{1,0:T(8,128)(2,1)}) custom-call(), custom_call_target="tpu_custom_call" | custom-call | tf_op jit(solution)/shard_map/pallas_call | solution.py:174
  18.4 6.2 %all-to-all-done = bf16[8,2,4096]{2,1,0:T(2,128)(2,1)S(1)} async-done(((bf16[8,2,4096]{2,1,0:T(2,128)(2,1)}), bf16[8,2,4096]{2,1,0:T(2,128)(2,1)S(1)}, u32[]{:S(2)}, u32[]{:S(2)}) %all-to-all-start) | async-done | bytes 131104 | tf_op jit(solution)/shard_map/all_to_all | solution.py:277
  24.6 0.0 collective-permute-done.2.other
  24.6 0.0 collective-permute-done
  24.6 0.0 collective-permute-done.1
  24.6 0.0 collective-permute-done.3.g1
  24.6 0.0 copy-done.4
  24.6 0.0 copy-done.5
  24.6 0.0 copy-done.6
  24.7 0.1 copy.18
  24.8 0.1 copy.19
  24.9 0.2 broadcast_in_dim.53
  25.1 0.0 copy-start.3
  25.1 26.9 %all_to_all.30 = bf16[16,8,8192]{2,1,0:T(8,128)(2,1)S(1)} all-to-all(bf16[16,8,8192]{2,1,0:T(8,128)(2,1)S(1)} %broadcast_in_dim.53), channel_id=1, replica_groups=mesh['x'=4,'y'=4,'h'=4,'l'=2,'c'=2] {'x','y'}, dimensions={0} | all-to-all | bytes 4194304 | tf_op jit(solution)/shard_map/all_to_all | solution.py:32
  52.0 0.0 copy-done.3
  52.0 1.4 %shard_map.169 = bf16[8,112,128]{2,1,0:T(8,128)(2,1)} custom-call(bf16[128,8192]{1,0:T(8,128)(2,1)S(1)} %bitcast.28, bf16[112,4096]{1,0:T(8,128)(2,1)S(1)} %bitcast.31, bf16[112,4096]{1,0:T(8,128)(2,1)S(1)} %collective-permute-done.2.other), custom_call_target="tpu_custom_call" | custom-call | tf_op jit(solution)/shard_map/pallas_call | solution.py:230
  53.4 4.0 %all-to-all-start.2 = ((bf16[8,112,128]{2,1,0:T(8,128)(2,1)}), bf16[8,112,128]{2,1,0:T(8,128)(2,1)S(1)}, u32[]{:S(2)}, u32[]{:S(2)}) async-start(bf16[8,112,128]{2,1,0:T(8,128)(2,1)} %shard_map.169), calls=%async_computation.2 | async-start | bytes 458752 | tf_op jit(solution)/shard_map/all_to_all | solution.py:302
  57.4 0.1 pad.9.clone
  57.5 5.1 %conditional.5 = ((f32[448,128]{1,0:T(8,128)S(1)}, f32[1,128]{1,0:T(1,128)S(1)}, bf16[7168,128]{1,0:T(8,128)(2,1)}, bf16[128,7168]{1,0:T(8,128)(2,1)})) conditional(s32[]{:T(128)} %convert_element_type.61, (s32[]{:T(128)}, f32[7168]{0:T(1024)}, s32[64]{0:T(128)S(1)}, s32[2,128,4]{1,2,0:T(4,128)S(1)}, f32[2,128,4]{1,2,0:T(4,128)S(1)}, ...), branch_computations={%region_6.8_spmd, %region_8.9_spmd} | conditional | flops 3079 | bytes 245892 | solution.py:300
  57.5 0.8 dynamic_slice.13
  58.3 0.1 broadcast_in_dim.22
  58.4 0.1 iota_compare_fusion.1
  58.5 0.2 lt.59
  58.7 3.9 %branch_0_fun.1 = (bf16[7168,128]{1,0:T(8,128)(2,1)}, bf16[128,7168]{1,0:T(8,128)(2,1)}) custom-call(bf16[7168,128]{1,0:T(8,128)(2,1)} %get-tuple-element.69.a, bf16[128,7168]{1,0:T(8,128)(2,1)} %get-tuple-element.70.b), custom_call_target="tpu_custom_call" | custom-call | tf_op jit(solution)/shard_map/cond/branch_0_fun/pallas_call | solution.py:164
  62.6 3.8 %all-to-all-done.2 = bf16[8,112,128]{2,1,0:T(8,128)(2,1)S(1)} async-done(((bf16[8,112,128]{2,1,0:T(8,128)(2,1)}), bf16[8,112,128]{2,1,0:T(8,128)(2,1)S(1)}, u32[]{:S(2)}, u32[]{:S(2)}) %all-to-all-start.2) | async-done | bytes 229408 | tf_op jit(solution)/shard_map/all_to_all | solution.py:302
  66.4 0.1 multiply_reduce_fusion
  66.6 0.1 maximum_maximum_fusion
  66.7 0.0 copy-start.2
  66.7 0.2 broadcast_in_dim.55
  67.0 0.0 copy-start
  67.0 0.0 copy-start.1
  67.0 19.8 %all_to_all.31.rows = bf16[16,464,128]{2,1,0:T(8,128)(2,1)S(1)} all-to-all(bf16[16,464,128]{2,1,0:T(8,128)(2,1)S(1)} %broadcast_in_dim.55), channel_id=1, replica_groups=mesh['x'=4,'y'=4,'h'=4,'l'=2,'c'=2] {'x','y'}, dimensions={0} | all-to-all | bytes 3801088 | tf_op jit(solution)/shard_map/all_to_all | solution.py:32
  86.8 0.0 copy-done.2
  86.8 3.9 %shard_map.170 = bf16[128,7168]{1,0:T(8,128)(2,1)S(1)} custom-call(bf16[16,464,128]{2,1,0:T(8,128)(2,1)S(1)} %all_to_all.31.rows, f32[1,128]{1,0:T(1,128)S(1)} %get-tuple-element.160.weight, bf16[7168,128]{1,0:T(8,128)(2,1)S(1)} %copy-done.2, bf16[7168,128]{1,0:T(8,128)(2,1)S(1)} %collective-permute-done.3.g1, bf16[7168,128]{1,0:T(8,128)(2,1)S(1)} %copy-done, ...), custom_call_target="tpu_custom_call" | custom-call | flops 705000000 | bytes 15000000 | tf_op jit(solution)/shard_map/pallas_call | solution.py:145
  90.7 19.4 %all_to_all.32.got = bf16[16,8,7168]{2,1,0:T(8,128)(2,1)S(1)} all-to-all(bf16[16,8,7168]{2,1,0:T(8,128)(2,1)S(1)} %bitcast.29), channel_id=1, replica_groups=mesh['x'=4,'y'=4,'h'=4,'l'=2,'c'=2] {'x','y'}, dimensions={0} | all-to-all | bytes 3670016 | tf_op jit(solution)/shard_map/all_to_all | solution.py:318
  110.1 0.9 shard_map.171
  111.1 15.1 %all-to-all-start.5 = ((bf16[16,2,1792]{2,1,0:T(2,128)(2,1)}), bf16[16,2,1792]{2,1,0:T(2,128)(2,1)S(1)}, u32[]{:S(2)}, u32[]{:S(2)}) async-start(bf16[16,2,1792]{2,1,0:T(2,128)(2,1)} %shard_map.171), calls=%async_computation.5 | async-start | bytes 229376 | tf_op jit(solution)/shard_map/all_to_all | solution.py:326
  126.1 0.3 collective-permute-start.4
  126.4 0.9 collective-permute-done.4
  127.3 0.6 fusion.1
  128.0 7.0 %all-to-all-done.5.own = bf16[16,2,1792]{2,1,0:T(2,128)(2,1)S(1)} async-done(((bf16[16,2,1792]{2,1,0:T(2,128)(2,1)}), bf16[16,2,1792]{2,1,0:T(2,128)(2,1)S(1)}, u32[]{:S(2)}, u32[]{:S(2)}) %all-to-all-start.5) | async-done | bytes 114720 | tf_op jit(solution)/shard_map/all_to_all | solution.py:326
  135.0 0.6 shard_map.172
  (17 shorter events, 0.2 us)
Async XLA Ops:
  0.6 23.9 %collective-permute-start = (bf16[7168,128]{1,0:T(8,128)(2,1)}, bf16[7168,128]{1,0:T(8,128)(2,1)}, u32[]{:S(2)}, u32[]{:S(2)}) collective-permute-start(bf16[7168,128]{1,0:T(8,128)(2,1)} %u0.1), channel_id=1, source_target_pairs={{0,1},{1,0},{2,3},{3,2},{4,5},{5,4},{6,7},{7,6},{8,9},{9,8},{10,11... | collective-permute-start | bytes 5505032 | tf_op jit(solution)/shard_map/ppermute | solution.py:262
  4.0 20.6 %collective-permute-start.1 = (bf16[128,7168]{1,0:T(8,128)(2,1)}, bf16[128,7168]{1,0:T(8,128)(2,1)}, u32[]{:S(2)}, u32[]{:S(2)}) collective-permute-start(bf16[128,7168]{1,0:T(8,128)(2,1)} %d0.1), channel_id=1, source_target_pairs={{0,1},{1,0},{2,3},{3,2},{4,5},{5,4},{6,7},{7,6},{8,9},{9,8},{10,11... | collective-permute-start | bytes 5505032 | tf_op jit(solution)/shard_map/ppermute | solution.py:263
  4.1 20.5 %collective-permute-start.3 = (bf16[7168,128]{1,0:T(8,128)(2,1)}, bf16[7168,128]{1,0:T(8,128)(2,1)S(1)}, u32[]{:S(2)}, u32[]{:S(2)}) collective-permute-start(bf16[7168,128]{1,0:T(8,128)(2,1)} %g0.1), channel_id=1, source_target_pairs={{0,1},{1,0},{2,3},{3,2},{4,5},{5,4},{6,7},{7,6},{8,9},{9,8},{10,11... | collective-permute-start | bytes 5505032 | tf_op jit(solution)/shard_map/ppermute | solution.py:261
  4.5 20.1 %collective-permute-start.2 = (bf16[112,4096]{1,0:T(8,128)(2,1)}, bf16[112,4096]{1,0:T(8,128)(2,1)S(1)}, u32[]{:S(2)}, u32[]{:S(2)}) collective-permute-start(bf16[112,4096]{1,0:T(8,128)(2,1)} %bitcast.30), channel_id=1, source_target_pairs={{0,1},{1,0},{2,3},{3,2},{4,5},{5,4},{6,7},{7,6},{8,9},{9,8},{10,11... | collective-permute-start | bytes 2752520 | tf_op jit(solution)/shard_map/ppermute | solution.py:260
  4.6 20.0 %copy-start.4 = (s32[2,128,4]{1,2,0:T(4,128)S(1)}, s32[2,128,4]{1,2,0:T(4,128)}, u32[]{:S(2)}) copy-start(s32[2,128,4]{1,2,0:T(4,128)} %param.33) | copy-start | bytes 12292
  4.6 20.0 %copy-start.5 = (f32[2,128,4]{1,2,0:T(4,128)S(1)}, f32[2,128,4]{1,2,0:T(4,128)}, u32[]{:S(2)}) copy-start(f32[2,128,4]{1,2,0:T(4,128)} %param.34) | copy-start | bytes 12292
  4.6 20.1 %copy-start.6 = (s32[64]{0:T(128)S(1)}, s32[64]{0:T(128)}, u32[]{:S(2)}) copy-start(s32[64]{0:T(128)} %counts.1) | copy-start | bytes 772
  9.4 15.2 %all-to-all-start = ((bf16[8,2,4096]{2,1,0:T(2,128)(2,1)}), bf16[8,2,4096]{2,1,0:T(2,128)(2,1)S(1)}, u32[]{:S(2)}, u32[]{:S(2)}) async-start(bf16[8,2,4096]{2,1,0:T(2,128)(2,1)} %shard_map.167), calls=%async_computation | async-start | bytes 262144 | tf_op jit(solution)/shard_map/all_to_all | solution.py:277
  25.1 26.9 %copy-start.3 = (bf16[4096,112]{0,1:T(8,128)(2,1)S(1)}, bf16[4096,112]{0,1:T(8,128)(2,1)}, u32[]{:S(2)}) copy-start(bf16[4096,112]{0,1:T(8,128)(2,1)} %param.31) | copy-start | bytes 2752516
  53.4 13.0 %all-to-all-start.2 = ((bf16[8,112,128]{2,1,0:T(8,128)(2,1)}), bf16[8,112,128]{2,1,0:T(8,128)(2,1)S(1)}, u32[]{:S(2)}, u32[]{:S(2)}) async-start(bf16[8,112,128]{2,1,0:T(8,128)(2,1)} %shard_map.169), calls=%async_computation.2 | async-start | bytes 458752 | tf_op jit(solution)/shard_map/all_to_all | solution.py:302
  66.7 20.1 %copy-start.2 = (bf16[7168,128]{1,0:T(8,128)(2,1)S(1)}, bf16[7168,128]{1,0:T(8,128)(2,1)}, u32[]{:S(2)}) copy-start(bf16[7168,128]{1,0:T(8,128)(2,1)} %g0.1) | copy-start | bytes 5505028
  67.0 19.9 %copy-start = (bf16[7168,128]{1,0:T(8,128)(2,1)S(1)}, bf16[7168,128]{1,0:T(8,128)(2,1)}, u32[]{:S(2)}) copy-start(bf16[7168,128]{1,0:T(8,128)(2,1)} %u0.1) | copy-start | bytes 5505028
  67.0 19.8 %copy-start.1 = (bf16[128,7168]{1,0:T(8,128)(2,1)S(1)}, bf16[128,7168]{1,0:T(8,128)(2,1)}, u32[]{:S(2)}) copy-start(bf16[128,7168]{1,0:T(8,128)(2,1)} %d0.1) | copy-start | bytes 5505028
  111.1 23.9 %all-to-all-start.5 = ((bf16[16,2,1792]{2,1,0:T(2,128)(2,1)}), bf16[16,2,1792]{2,1,0:T(2,128)(2,1)S(1)}, u32[]{:S(2)}, u32[]{:S(2)}) async-start(bf16[16,2,1792]{2,1,0:T(2,128)(2,1)} %shard_map.171), calls=%async_computation.5 | async-start | bytes 229376 | tf_op jit(solution)/shard_map/all_to_all | solution.py:326
  126.1 1.2 collective-permute-start.4

commit v10 on v8

--- a/solution.py
+++ b/solution.py
@@ -85,12 +85,15 @@
     copies[6].wait()
     slot = lax.broadcasted_iota(jnp.int32, (STEPS * SLOTS, HD), 0) % SLOTS
     live = slot < counts[place[0]]
-    for h in range(heads):
-        ctx = jnp.dot(lat[h].astype(bf16), v[h], preferred_element_type=f32)
-        ctx = jnp.where(live, ctx[: STEPS * SLOTS], 0.0).astype(bf16)
-        for to in range(NH):
-            for s in range(STEPS):
-                out[to * 2 + s, :, h * HD : (h + 1) * HD] = ctx[s * SLOTS : (s + 1) * SLOTS]
+    for h in range(0, heads, 2):
+        rows2 = jnp.concatenate([lat[h], lat[h + 1]], axis=0).astype(bf16)
+        both = jnp.dot(rows2, jnp.concatenate([v[h], v[h + 1]], axis=1), preferred_element_type=f32)
+        for i in range(2):
+            ctx = both[8 * i : 8 * i + STEPS * SLOTS, HD * i : HD * (i + 1)]
+            ctx = jnp.where(live, ctx, 0.0).astype(bf16)
+            for to in range(NH):
+                for s in range(STEPS):
+                    out[to * 2 + s, :, (h + i) * HD : (h + i + 1) * HD] = ctx[s * SLOTS : (s + 1) * SLOTS]
 
 
 def attend(place, lengths, counts, *arrays):

time: 136 us -> 136 us (level)
  no operation moved by 1% of the time
where the time goes in v10:
time: 136 us
  blocking collectives  66.1 us (49%)
  starting transfers between devices  30.5 us (22%)
  waiting for transfers between devices  17.9 us (13%)
  Pallas kernels  16.7 us (12%)
  local copies, waits for them, and re-layouts  1.84 us (1%)
  other arithmetic  1.72 us (1%)
    all_to_all x2, blocking collectives, spread(): return lax.all_to_all(copies, axes, 0, 0)  46.7 us
    all_to_all x1, blocking collectives, body(): got = lax.all_to_all(out.reshape(NXY, 8, D), XY, 0, 0)  19.4 us
    all_to_all x1, starting transfers between devices, body(): own = lax.all_to_all(sums, ('h', 'l', 'c'), 0, 0)  15.1 us
    all_to_all x1, starting transfers between devices, body(): ctx = lax.all_to_all(ctx, ('h', 'c'), 0, 0).reshape(NH, 2, SLOTS, -1)  7.14 us
    all_to_all x1, waiting for transfers between devices, body(): own = lax.all_to_all(sums, ('h', 'l', 'c'), 0, 0)  7.02 us
    all_to_all x1, waiting for transfers between devices, body(): ctx = lax.all_to_all(ctx, ('h', 'c'), 0, 0).reshape(NH, 2, SLOTS, -1)  6.19 us
    pallas_call x1, Pallas kernels, attend(): pl.pallas_call(attend_kernel, in_specs=[scalars] * 3 + [far] * 7, out_spe...  4.77 us
    all_to_all x1, starting transfers between devices, body(): lax.all_to_all(project(ctx, out_proj.T, out_other), Z, 0, 0)  4.03 us
  transfers between devices with their start and end apart: 8, of which 4 were waited for; matrix products, arithmetic and copies ran while one was open for 1% of the time, Pallas kernels for 8%

profile of v10, /device:TPU:1, one launch (start us, length us, event | category | flops | bytes accessed | tf_op | source)
XLA Modules:
  0.0 135.7 jit_solution(12782765390031326284)
XLA Ops:
  0.6 3.3 %collective-permute-start = (bf16[7168,128]{1,0:T(8,128)(2,1)}, bf16[7168,128]{1,0:T(8,128)(2,1)}, u32[]{:S(2)}, u32[]{:S(2)}) collective-permute-start(bf16[7168,128]{1,0:T(8,128)(2,1)} %u0.1), channel_id=1, source_target_pairs={{0,1},{1,0},{2,3},{3,2},{4,5},{5,4},{6,7},{7,6},{8,9},{9,8},{10,11... | collective-permute-start | bytes 5505032 | tf_op jit(solution)/shard_map/ppermute | solution.py:246
  4.0 0.1 collective-permute-start.1
  4.1 0.4 collective-permute-start.3
  4.5 0.1 collective-permute-start.2
  4.6 4.8 %shard_map.167 = bf16[8,2,4096]{2,1,0:T(2,128)(2,1)} custom-call(s32[1]{0:T(128)} %bitcast.place, s32[2]{0:T(128)} %lengths.1, s32[64]{0:T(128)} %counts.1, bf16[2,2,16384]{2,1,0:T(2,128)(2,1)} %ql_hbm.1, bf16[2,2,2048]{2,1,0:T(2,128)(2,1)} %qr_hbm.1, bf16[2,384,512]{2,1,0:T(8,128)(2,1)} %cl_hbm.1, bf16[2,64,384]{2,1,0:T(8,128)(2,1)} %cr_hbm.1, ...), custom_call_target="tpu_custom_call" | custom-call | flops 160000000 | bytes 6000000 | tf_op jit(solution)/shard_map/pallas_call | solution.py:103
  9.4 7.1 %all-to-all-start = ((bf16[8,2,4096]{2,1,0:T(2,128)(2,1)}), bf16[8,2,4096]{2,1,0:T(2,128)(2,1)S(1)}, u32[]{:S(2)}, u32[]{:S(2)}) async-start(bf16[8,2,4096]{2,1,0:T(2,128)(2,1)} %shard_map.167), calls=%async_computation | async-start | bytes 262144 | tf_op jit(solution)/shard_map/all_to_all | solution.py:261
  16.5 1.8 %shard_map.168 = (bf16[7168,128]{1,0:T(8,128)(2,1)}, bf16[128,7168]{1,0:T(8,128)(2,1)}) custom-call(), custom_call_target="tpu_custom_call" | custom-call | tf_op jit(solution)/shard_map/pallas_call | solution.py:177
  18.3 6.2 %all-to-all-done = bf16[8,2,4096]{2,1,0:T(2,128)(2,1)S(1)} async-done(((bf16[8,2,4096]{2,1,0:T(2,128)(2,1)}), bf16[8,2,4096]{2,1,0:T(2,128)(2,1)S(1)}, u32[]{:S(2)}, u32[]{:S(2)}) %all-to-all-start) | async-done | bytes 131104 | tf_op jit(solution)/shard_map/all_to_all | solution.py:261
  24.5 0.0 collective-permute-done.2.other
  24.5 0.0 collective-permute-done
  24.5 0.0 collective-permute-done.1
  24.5 0.0 collective-permute-done.3.g1
  24.6 0.0 copy-done.4
  24.6 0.0 copy-done.5
  24.6 0.0 copy-done.6
  24.7 0.1 copy.18
  24.8 0.1 copy.19
  24.9 0.2 broadcast_in_dim.53
  25.1 0.0 copy-start.3
  25.1 26.9 %all_to_all.30 = bf16[16,8,8192]{2,1,0:T(8,128)(2,1)S(1)} all-to-all(bf16[16,8,8192]{2,1,0:T(8,128)(2,1)S(1)} %broadcast_in_dim.53), channel_id=1, replica_groups=mesh['x'=4,'y'=4,'h'=4,'l'=2,'c'=2] {'x','y'}, dimensions={0} | all-to-all | bytes 4194304 | tf_op jit(solution)/shard_map/all_to_all | solution.py:32
  52.0 0.0 copy-done.3
  52.0 1.4 %shard_map.169 = bf16[8,112,128]{2,1,0:T(8,128)(2,1)} custom-call(bf16[128,8192]{1,0:T(8,128)(2,1)S(1)} %bitcast.29, bf16[112,4096]{1,0:T(8,128)(2,1)S(1)} %bitcast.32, bf16[112,4096]{1,0:T(8,128)(2,1)S(1)} %collective-permute-done.2.other), custom_call_target="tpu_custom_call" | custom-call | tf_op jit(solution)/shard_map/pallas_call | solution.py:214
  53.4 4.0 %all-to-all-start.2 = ((bf16[8,112,128]{2,1,0:T(8,128)(2,1)}), bf16[8,112,128]{2,1,0:T(8,128)(2,1)S(1)}, u32[]{:S(2)}, u32[]{:S(2)}) async-start(bf16[8,112,128]{2,1,0:T(8,128)(2,1)} %shard_map.169), calls=%async_computation.2 | async-start | bytes 458752 | tf_op jit(solution)/shard_map/all_to_all | solution.py:286
  57.4 0.1 pad.9.clone
  57.5 5.1 %conditional.5 = ((f32[448,128]{1,0:T(8,128)S(1)}, f32[1,128]{1,0:T(1,128)S(1)}, bf16[7168,128]{1,0:T(8,128)(2,1)}, bf16[128,7168]{1,0:T(8,128)(2,1)})) conditional(s32[]{:T(128)} %convert_element_type.65, (s32[]{:T(128)}, f32[7168]{0:T(1024)}, s32[64]{0:T(128)S(1)}, s32[2,128,4]{1,2,0:T(4,128)S(1)}, f32[2,128,4]{1,2,0:T(4,128)S(1)}, ...), branch_computations={%region_6.8_spmd, %region_8.9_spmd} | conditional | flops 3079 | bytes 245892 | solution.py:284
  57.5 0.8 dynamic_slice.13
  58.3 0.1 broadcast_in_dim.22
  58.4 0.1 iota_compare_fusion.1
  58.5 0.2 lt.59
  58.6 3.9 %branch_0_fun.1 = (bf16[7168,128]{1,0:T(8,128)(2,1)}, bf16[128,7168]{1,0:T(8,128)(2,1)}) custom-call(bf16[7168,128]{1,0:T(8,128)(2,1)} %get-tuple-element.69.a, bf16[128,7168]{1,0:T(8,128)(2,1)} %get-tuple-element.70.b), custom_call_target="tpu_custom_call" | custom-call | tf_op jit(solution)/shard_map/cond/branch_0_fun/pallas_call | solution.py:167
  62.6 3.8 %all-to-all-done.2 = bf16[8,112,128]{2,1,0:T(8,128)(2,1)S(1)} async-done(((bf16[8,112,128]{2,1,0:T(8,128)(2,1)}), bf16[8,112,128]{2,1,0:T(8,128)(2,1)S(1)}, u32[]{:S(2)}, u32[]{:S(2)}) %all-to-all-start.2) | async-done | bytes 229408 | tf_op jit(solution)/shard_map/all_to_all | solution.py:286
  66.4 0.1 multiply_reduce_fusion
  66.6 0.1 maximum_maximum_fusion
  66.7 0.0 copy-start.2
  66.7 0.2 broadcast_in_dim.55
  67.0 0.0 copy-start
  67.0 0.0 copy-start.1
  67.0 19.8 %all_to_all.31.rows = bf16[16,464,128]{2,1,0:T(8,128)(2,1)S(1)} all-to-all(bf16[16,464,128]{2,1,0:T(8,128)(2,1)S(1)} %broadcast_in_dim.55), channel_id=1, replica_groups=mesh['x'=4,'y'=4,'h'=4,'l'=2,'c'=2] {'x','y'}, dimensions={0} | all-to-all | bytes 3801088 | tf_op jit(solution)/shard_map/all_to_all | solution.py:32
  86.8 0.0 copy-done
  86.8 3.9 %shard_map.170 = bf16[128,7168]{1,0:T(8,128)(2,1)S(1)} custom-call(bf16[16,464,128]{2,1,0:T(8,128)(2,1)S(1)} %all_to_all.31.rows, f32[1,128]{1,0:T(1,128)S(1)} %get-tuple-element.160.weight, bf16[7168,128]{1,0:T(8,128)(2,1)S(1)} %copy-done.2, bf16[7168,128]{1,0:T(8,128)(2,1)S(1)} %collective-permute-done.3.g1, bf16[7168,128]{1,0:T(8,128)(2,1)S(1)} %copy-done, ...), custom_call_target="tpu_custom_call" | custom-call | flops 705000000 | bytes 15000000 | tf_op jit(solution)/shard_map/pallas_call | solution.py:148
  90.7 19.4 %all_to_all.32.got = bf16[16,8,7168]{2,1,0:T(8,128)(2,1)S(1)} all-to-all(bf16[16,8,7168]{2,1,0:T(8,128)(2,1)S(1)} %bitcast.30), channel_id=1, replica_groups=mesh['x'=4,'y'=4,'h'=4,'l'=2,'c'=2] {'x','y'}, dimensions={0} | all-to-all | bytes 3670016 | tf_op jit(solution)/shard_map/all_to_all | solution.py:302
  110.1 0.9 shard_map.171
  111.0 15.1 %all-to-all-start.5 = ((bf16[16,2,1792]{2,1,0:T(2,128)(2,1)}), bf16[16,2,1792]{2,1,0:T(2,128)(2,1)S(1)}, u32[]{:S(2)}, u32[]{:S(2)}) async-start(bf16[16,2,1792]{2,1,0:T(2,128)(2,1)} %shard_map.171), calls=%async_computation.5 | async-start | bytes 229376 | tf_op jit(solution)/shard_map/all_to_all | solution.py:310
  126.1 0.3 collective-permute-start.4
  126.4 0.9 collective-permute-done.4
  127.3 0.6 fusion.1
  127.9 7.0 %all-to-all-done.5 = bf16[16,2,1792]{2,1,0:T(2,128)(2,1)S(1)} async-done(((bf16[16,2,1792]{2,1,0:T(2,128)(2,1)}), bf16[16,2,1792]{2,1,0:T(2,128)(2,1)S(1)}, u32[]{:S(2)}, u32[]{:S(2)}) %all-to-all-start.5) | async-done | bytes 114720 | tf_op jit(solution)/shard_map/all_to_all | solution.py:310
  135.0 0.7 reduce.2
  (17 shorter events, 0.2 us)
Async XLA Ops:
  0.6 23.9 %collective-permute-start = (bf16[7168,128]{1,0:T(8,128)(2,1)}, bf16[7168,128]{1,0:T(8,128)(2,1)}, u32[]{:S(2)}, u32[]{:S(2)}) collective-permute-start(bf16[7168,128]{1,0:T(8,128)(2,1)} %u0.1), channel_id=1, source_target_pairs={{0,1},{1,0},{2,3},{3,2},{4,5},{5,4},{6,7},{7,6},{8,9},{9,8},{10,11... | collective-permute-start | bytes 5505032 | tf_op jit(solution)/shard_map/ppermute | solution.py:246
  4.0 20.6 %collective-permute-start.1 = (bf16[128,7168]{1,0:T(8,128)(2,1)}, bf16[128,7168]{1,0:T(8,128)(2,1)}, u32[]{:S(2)}, u32[]{:S(2)}) collective-permute-start(bf16[128,7168]{1,0:T(8,128)(2,1)} %d0.1), channel_id=1, source_target_pairs={{0,1},{1,0},{2,3},{3,2},{4,5},{5,4},{6,7},{7,6},{8,9},{9,8},{10,11... | collective-permute-start | bytes 5505032 | tf_op jit(solution)/shard_map/ppermute | solution.py:247
  4.1 20.5 %collective-permute-start.3 = (bf16[7168,128]{1,0:T(8,128)(2,1)}, bf16[7168,128]{1,0:T(8,128)(2,1)S(1)}, u32[]{:S(2)}, u32[]{:S(2)}) collective-permute-start(bf16[7168,128]{1,0:T(8,128)(2,1)} %g0.1), channel_id=1, source_target_pairs={{0,1},{1,0},{2,3},{3,2},{4,5},{5,4},{6,7},{7,6},{8,9},{9,8},{10,11... | collective-permute-start | bytes 5505032 | tf_op jit(solution)/shard_map/ppermute | solution.py:245
  4.5 20.1 %collective-permute-start.2 = (bf16[112,4096]{1,0:T(8,128)(2,1)}, bf16[112,4096]{1,0:T(8,128)(2,1)S(1)}, u32[]{:S(2)}, u32[]{:S(2)}) collective-permute-start(bf16[112,4096]{1,0:T(8,128)(2,1)} %bitcast.31), channel_id=1, source_target_pairs={{0,1},{1,0},{2,3},{3,2},{4,5},{5,4},{6,7},{7,6},{8,9},{9,8},{10,11... | collective-permute-start | bytes 2752520 | tf_op jit(solution)/shard_map/ppermute | solution.py:244
  4.6 20.0 %copy-start.4 = (s32[2,128,4]{1,2,0:T(4,128)S(1)}, s32[2,128,4]{1,2,0:T(4,128)}, u32[]{:S(2)}) copy-start(s32[2,128,4]{1,2,0:T(4,128)} %param.33) | copy-start | bytes 12292
  4.6 20.0 %copy-start.5 = (f32[2,128,4]{1,2,0:T(4,128)S(1)}, f32[2,128,4]{1,2,0:T(4,128)}, u32[]{:S(2)}) copy-start(f32[2,128,4]{1,2,0:T(4,128)} %param.34) | copy-start | bytes 12292
  4.6 20.0 %copy-start.6 = (s32[64]{0:T(128)S(1)}, s32[64]{0:T(128)}, u32[]{:S(2)}) copy-start(s32[64]{0:T(128)} %counts.1) | copy-start | bytes 772
  9.4 15.2 %all-to-all-start = ((bf16[8,2,4096]{2,1,0:T(2,128)(2,1)}), bf16[8,2,4096]{2,1,0:T(2,128)(2,1)S(1)}, u32[]{:S(2)}, u32[]{:S(2)}) async-start(bf16[8,2,4096]{2,1,0:T(2,128)(2,1)} %shard_map.167), calls=%async_computation | async-start | bytes 262144 | tf_op jit(solution)/shard_map/all_to_all | solution.py:261
  25.1 26.9 %copy-start.3 = (bf16[4096,112]{0,1:T(8,128)(2,1)S(1)}, bf16[4096,112]{0,1:T(8,128)(2,1)}, u32[]{:S(2)}) copy-start(bf16[4096,112]{0,1:T(8,128)(2,1)} %param.31) | copy-start | bytes 2752516
  53.4 13.0 %all-to-all-start.2 = ((bf16[8,112,128]{2,1,0:T(8,128)(2,1)}), bf16[8,112,128]{2,1,0:T(8,128)(2,1)S(1)}, u32[]{:S(2)}, u32[]{:S(2)}) async-start(bf16[8,112,128]{2,1,0:T(8,128)(2,1)} %shard_map.169), calls=%async_computation.2 | async-start | bytes 458752 | tf_op jit(solution)/shard_map/all_to_all | solution.py:286
  66.7 20.1 %copy-start.2 = (bf16[7168,128]{1,0:T(8,128)(2,1)S(1)}, bf16[7168,128]{1,0:T(8,128)(2,1)}, u32[]{:S(2)}) copy-start(bf16[7168,128]{1,0:T(8,128)(2,1)} %g0.1) | copy-start | bytes 5505028
  67.0 19.8 %copy-start = (bf16[7168,128]{1,0:T(8,128)(2,1)S(1)}, bf16[7168,128]{1,0:T(8,128)(2,1)}, u32[]{:S(2)}) copy-start(bf16[7168,128]{1,0:T(8,128)(2,1)} %u0.1) | copy-start | bytes 5505028
  67.0 19.8 %copy-start.1 = (bf16[128,7168]{1,0:T(8,128)(2,1)S(1)}, bf16[128,7168]{1,0:T(8,128)(2,1)}, u32[]{:S(2)}) copy-start(bf16[128,7168]{1,0:T(8,128)(2,1)} %d0.1) | copy-start | bytes 5505028
  111.0 23.9 %all-to-all-start.5 = ((bf16[16,2,1792]{2,1,0:T(2,128)(2,1)}), bf16[16,2,1792]{2,1,0:T(2,128)(2,1)S(1)}, u32[]{:S(2)}, u32[]{:S(2)}) async-start(bf16[16,2,1792]{2,1,0:T(2,128)(2,1)} %shard_map.171), calls=%async_computation.5 | async-start | bytes 229376 | tf_op jit(solution)/shard_map/all_to_all | solution.py:310
  126.1 1.2 collective-permute-start.4
